TPU v7x, 32 devices: a whole 2x2x4 slice. The times are simulated.
32 devices in a mesh: parts: 2 (over y), expert: 4 (over z), tensor: 4 (over x, core).
Axes of the slice: x: 2, y: 2, z: 4, core: 2. Of those that a mesh axis runs over, the one named last changes fastest.
Arguments:
- tokens_in: bfloat16 [512, 3072], P(('parts', 'expert', 'tensor')), parts along dimension 0, may hold values from -6 to 6
- out_grad: bfloat16 [512, 3072], P(('parts', 'expert', 'tensor')), parts along dimension 0, may hold values from -6 to 6
- expert_ids: int32 [512, 2], P(('parts', 'expert', 'tensor')), parts along dimension 0, may hold values from 0 to 3, all different within a row; in each aligned block of 64 rows (0 to 63, 64 to 127, ...) at most 48 rows name the same one
- gate_probs: bfloat16 [512, 2], P(('parts', 'expert', 'tensor')), parts along dimension 0, may hold values from 0.099609375 to 1
- w_in: bfloat16 [4, 3072, 8192], P('expert', None, 'tensor'), may hold values from -0.109375 to 0.109375
- w_out: bfloat16 [4, 8192, 3072], P('expert', 'tensor'), may hold values from -0.0625 to 0.0625
Outputs:
- token_grad: bfloat16 [512, 3072], P(('parts', 'expert', 'tensor')), parts along dimension 0
There are 2 independent parts, one for each index of `parts`. A program takes and returns all parts, laid end to end along the dimension named above; an argument that names none is the same for every part. Nothing has to cross between parts.
Inputs may be any that keep to these rules, and one draw needn't show every extreme that they name: `expert_ids`: each token names two different experts. In each aligned block of 64 tokens no expert is named by more than 48 tokens, a bound that some block reaches.
All inputs are finite; a program needn't handle non-finite values.
Results may differ from a plain program's by a relative error of at most 0.02.
Values may be sent and summed in bfloat16 or wider, within the bound.
No kernel may reach another device: no remote copies, remote signals or barrier semaphores. Data moves between devices by JAX's collectives and lax.ppermute only.
A program may use at most 64 MiB of HBM per device.

v0:
```python
import math

import jax
import jax.numpy as jnp
from jax import lax
from jax.sharding import PartitionSpec as P


def gelu_slope(value):
    coeff = math.sqrt(2.0 / math.pi)
    inner = jnp.tanh(coeff * (value + 0.044715 * value * value * value))
    return 0.5 * (1.0 + inner) + 0.5 * value * (1.0 - inner * inner) * coeff * (
        1.0 + 3.0 * 0.044715 * value * value
    )


def slot_table(route_all, experts, capacity):
    flat_ids = route_all.reshape(-1)
    pair_count = flat_ids.shape[0]
    onehot = (flat_ids[:, None] == jnp.arange(experts, dtype=jnp.int32)[None, :]).astype(jnp.int32)
    before = jnp.cumsum(onehot, axis=0) - onehot
    slot_index = jnp.sum(before * onehot, axis=1)
    target = flat_ids * capacity + slot_index
    cell_index = jnp.arange(experts * capacity, dtype=jnp.int32)
    matches = target[None, :] == cell_index[:, None]
    source = jnp.sum(
        jnp.where(matches, jnp.arange(pair_count, dtype=jnp.int32)[None, :], 0), axis=1
    )
    filled = jnp.any(matches, axis=1)
    return (target, source, filled)


def local(tokens_in, out_grad, expert_ids, gate_probs, w_in, w_out):
    experts = lax.axis_size("expert")
    shards = lax.axis_size("tensor")
    local_rows = tokens_in.shape[0]
    features = tokens_in.shape[1]
    capacity = 3 * local_rows * shards // experts
    route_all = lax.all_gather(expert_ids, "tensor", axis=0, tiled=True)
    target, source, filled = slot_table(route_all, experts, capacity)
    inputs_all, grads_all, gates_all = (
        lax.all_gather(tokens_in, "tensor", axis=0, tiled=True),
        lax.all_gather(out_grad, "tensor", axis=0, tiled=True),
        lax.all_gather(gate_probs, "tensor", axis=0, tiled=True),
    )
    token_of = source // 2
    occupied = filled[:, None]
    send_in = jnp.where(occupied, jnp.take(inputs_all, token_of, axis=0), 0)
    send_in = send_in.reshape(experts, capacity, -1)
    send_grad = jnp.where(occupied, jnp.take(grads_all, token_of, axis=0), 0)
    send_grad = send_grad.reshape(experts, capacity, -1)
    send_gate = jnp.where(filled, jnp.take(gates_all.reshape(-1), source), 0)
    send_gate = send_gate.reshape(experts, capacity)
    rows_in = lax.all_to_all(send_in, "expert", split_axis=0, concat_axis=0, tiled=True)
    rows_grad = lax.all_to_all(send_grad, "expert", split_axis=0, concat_axis=0, tiled=True)
    rows_gate = lax.all_to_all(send_gate, "expert", split_axis=0, concat_axis=0, tiled=True)
    slot_count = rows_in.shape[1]
    flat_in = rows_in.reshape(-1, features)
    flat_grad = rows_grad.reshape(-1, features)
    preact = jnp.dot(flat_in, w_in[0], preferred_element_type=jnp.float32)
    hidden_grad = jnp.einsum("rd,hd->rh", flat_grad, w_out[0], preferred_element_type=jnp.float32)
    scaled = (
        rows_gate.reshape(-1, 1).astype(jnp.float32) * hidden_grad * gelu_slope(preact)
    ).astype(jnp.bfloat16)
    partial_rows = jnp.einsum(
        "rh,dh->rd", scaled, w_in[0], preferred_element_type=jnp.float32
    ).astype(jnp.bfloat16)
    summed = lax.psum(partial_rows, "tensor").astype(jnp.float32)
    outgoing = summed.astype(jnp.bfloat16).reshape(experts, slot_count, -1)
    returned = lax.all_to_all(outgoing, "expert", split_axis=0, concat_axis=0, tiled=True)
    row_table = returned.reshape(experts * capacity, -1)
    offset_row = lax.axis_index("tensor") * (2 * local_rows)
    own_rows = lax.dynamic_slice_in_dim(target, offset_row, 2 * local_rows)
    picked = (
        jnp.take(row_table, own_rows, axis=0).astype(jnp.float32).reshape(local_rows, 2, features)
    )
    return jnp.sum(picked, axis=1).astype(jnp.bfloat16)


def solution(mesh):
    return jax.shard_map(
        local,
        mesh=mesh,
        in_specs=(
            P(("parts", "expert", "tensor"), None),
            P(("parts", "expert", "tensor"), None),
            P(("parts", "expert", "tensor"), None),
            P(("parts", "expert", "tensor"), None),
            P("expert", None, "tensor"),
            P("expert", "tensor", None),
        ),
        out_specs=P(("parts", "expert", "tensor"), None),
        check_vma=False,
    )
```

profile of v0, /device:TPU:0, one launch (start us, length us, event | category | flops | bytes accessed | tf_op | source)
XLA Modules:
  0.0 203.1 jit_solution(13865159401821321779)
XLA Ops:
  6.5 6.2 %all-gather = s32[4,16,2]{1,2,0:T(2,128)S(1)} all-gather(s32[1,16,2]{1,2,0:T(2,128)} %bitcast.37), channel_id=1, replica_groups=mesh['parts'=2,'expert'=4,'tensor'=4] {'tensor'}, dimensions={0}, use_global_device_ids=true | all-gather | bytes 640 | tf_op jit(solution)/shard_map/all_gather | solution.py:39
  12.8 0.1 copy.14
  12.9 0.1 reshape.143
  13.0 0.1 fusion.36
  13.1 0.2 reduce_window_sum.11
  13.3 0.2 select_reduce_fusion.1
  13.5 0.1 select_reduce_fusion
  13.6 0.1 fusion.35
  13.7 0.1 reduce_or.12
  13.8 5.4 %all-gather.1 = bf16[4,16,2]{1,2,0:T(2,128)(2,1)S(1)} all-gather(bf16[1,16,2]{1,2,0:T(2,128)(2,1)} %bitcast.38), channel_id=1, replica_groups=mesh['parts'=2,'expert'=4,'tensor'=4] {'tensor'}, dimensions={0}, use_global_device_ids=true | all-gather | bytes 320 | tf_op jit(solution)/shard_map/all_gather | solution.py:44
  19.2 0.1 copy.15
  19.3 0.1 reshape.144
  19.5 0.1 reduce_sum.36
  19.6 1.6 gather_fusion
  21.1 0.1 gather.16
  21.2 0.6 copy.16
  21.8 5.1 %all-to-all-start = ((bf16[4,1,48]{2,1,0:T(2,128)(2,1)}), bf16[4,1,48]{2,1,0:T(2,128)(2,1)S(1)}, u32[]{:S(2)}, u32[]{:S(2)}) async-start(bf16[4,1,48]{2,1,0:T(2,128)(2,1)} %copy.16), calls=%async_computation | async-start | bytes 4096 | tf_op jit(solution)/shard_map/all_to_all | solution.py:56
  26.9 6.7 %all_gather.15 = bf16[64,3072]{1,0:T(8,128)(2,1)S(1)} all-gather(bf16[16,3072]{1,0:T(8,128)(2,1)} %param.8), channel_id=1, replica_groups=mesh['parts'=2,'expert'=4,'tensor'=4] {'tensor'}, dimensions={0}, use_global_device_ids=true | all-gather | bytes 491520 | tf_op jit(solution)/shard_map/all_gather | solution.py:42
  33.6 6.8 %all_gather.14 = bf16[64,3072]{1,0:T(8,128)(2,1)S(1)} all-gather(bf16[16,3072]{1,0:T(8,128)(2,1)} %param.9), channel_id=1, replica_groups=mesh['parts'=2,'expert'=4,'tensor'=4] {'tensor'}, dimensions={0}, use_global_device_ids=true | all-gather | bytes 491520 | tf_op jit(solution)/shard_map/all_gather | solution.py:43
  40.4 1.3 gather_fusion.3
  41.7 1.3 gather_fusion.2
  43.0 1.3 select_select_fusion
  44.4 0.0 all-to-all-done
  44.4 33.9 %all_to_all.21 = bf16[4,48,3072]{2,1,0:T(8,128)(2,1)S(1)} all-to-all(bf16[4,48,3072]{2,1,0:T(8,128)(2,1)S(1)} %bitcast.31), channel_id=1, replica_groups=mesh['parts'=2,'expert'=4,'tensor'=4] {'expert'}, dimensions={0} | all-to-all | bytes 2359296 | tf_op jit(solution)/shard_map/all_to_all | solution.py:54
  78.3 3.5 %all-to-all-start.1 = ((bf16[4,48,3072]{2,1,0:T(8,128)(2,1)}), bf16[4,48,3072]{2,1,0:T(8,128)(2,1)S(1)}, u32[]{:S(2)}, u32[]{:S(2)}) async-start(bf16[4,48,3072]{2,1,0:T(8,128)(2,1)} %bitcast.4), calls=%async_computation.1 | async-start | bytes 2359296 | tf_op jit(solution)/shard_map/all_to_all | solution.py:55
  81.8 0.0 all-reduce.2.cloned.1.call-start
  81.9 0.1 reshape.151
  82.0 8.3 %fusion.2 = f32[192,2048]{1,0:T(8,128)} fusion(bf16[192,3072]{1,0:T(8,128)(2,1)S(1)} %bitcast.33, bf16[1,3072,2048]{2,1,0:T(8,128)(2,1)} %param.12), kind=kOutput, calls=%fused_computation.6 | convolution fusion | flops 2415919104 | bytes 15335424 | tf_op jit(solution)/shard_map/dot_general | solution.py:60
  90.3 19.7 %all-to-all-done.1 = bf16[4,48,3072]{2,1,0:T(8,128)(2,1)S(1)} async-done(((bf16[4,48,3072]{2,1,0:T(8,128)(2,1)}), bf16[4,48,3072]{2,1,0:T(8,128)(2,1)S(1)}, u32[]{:S(2)}, u32[]{:S(2)}) %all-to-all-start.1) | async-done | bytes 1179680 | tf_op jit(solution)/shard_map/all_to_all | solution.py:55
  110.0 15.2 %fusion.6 = bf16[192,3072]{1,0:T(8,128)(2,1)} fusion(bf16[1,3072,2048]{2,1,0:T(8,128)(2,1)} %param.12, bf16[192,3072]{1,0:T(8,128)(2,1)S(1)} %bitcast.32, bf16[1,2048,3072]{2,1,0:T(8,128)(2,1)} %param.13, f32[192,2048]{1,0:T(8,128)} %fusion.2, f32[192]{0:T(256)S(1)} %reshape.151), kind=kOutput, calls=%fused_computation.10 | convolution fusion | flops 4840292352 | bytes 29098752 | tf_op jit(solution)/shard_map/rh,dh->rd/dot_general | solution.py:65
  125.2 0.0 all-reduce.2.cloned.1.call-update
  125.3 36.2 %all-reduce.2.cloned.1.call-done = bf16[4,48,3072]{2,1,0:T(8,128)(2,1)} async-done(((bf16[4,48,3072]{2,1,0:T(8,128)(2,1)}), bf16[4,48,3072]{2,1,0:T(8,128)(2,1)}) %all-reduce.2.cloned.1.call-update) | async-done | bytes 1179664 | tf_op jit(solution)/shard_map/psum | solution.py:68
  161.5 4.6 %all-to-all-start.3 = ((bf16[4,48,3072]{2,1,0:T(8,128)(2,1)}), bf16[4,48,3072]{2,1,0:T(8,128)(2,1)S(1)}, u32[]{:S(2)}, u32[]{:S(2)}) async-start(bf16[4,48,3072]{2,1,0:T(8,128)(2,1)} %all-reduce.2.cloned.1.call-done), calls=%async_computation.3 | async-start | bytes 2359296 | tf_op jit(solution)/shard_map/all_to_all | solution.py:70
  166.1 0.1 compare_and_fusion.1
  166.2 0.1 broadcast_in_dim.66
  166.3 28.1 %all-to-all-done.3 = bf16[4,48,3072]{2,1,0:T(8,128)(2,1)S(1)} async-done(((bf16[4,48,3072]{2,1,0:T(8,128)(2,1)}), bf16[4,48,3072]{2,1,0:T(8,128)(2,1)S(1)}, u32[]{:S(2)}, u32[]{:S(2)}) %all-to-all-start.3) | async-done | bytes 1179680 | tf_op jit(solution)/shard_map/all_to_all | solution.py:70
  194.4 0.7 gather_fusion.1
  195.1 0.1 gather.18
  195.2 1.1 fusion.34
  (8 shorter events, 0.1 us)
Async XLA Ops:
  21.8 22.6 %all-to-all-start = ((bf16[4,1,48]{2,1,0:T(2,128)(2,1)}), bf16[4,1,48]{2,1,0:T(2,128)(2,1)S(1)}, u32[]{:S(2)}, u32[]{:S(2)}) async-start(bf16[4,1,48]{2,1,0:T(2,128)(2,1)} %copy.16), calls=%async_computation | async-start | bytes 4096 | tf_op jit(solution)/shard_map/all_to_all | solution.py:56
  78.3 31.7 %all-to-all-start.1 = ((bf16[4,48,3072]{2,1,0:T(8,128)(2,1)}), bf16[4,48,3072]{2,1,0:T(8,128)(2,1)S(1)}, u32[]{:S(2)}, u32[]{:S(2)}) async-start(bf16[4,48,3072]{2,1,0:T(8,128)(2,1)} %bitcast.4), calls=%async_computation.1 | async-start | bytes 2359296 | tf_op jit(solution)/shard_map/all_to_all | solution.py:55
  81.8 79.7 %all-reduce.2.cloned.1.call-start = ((), (), s32[]{:S(2)}) async-start(), calls=%async_computation.4 | async-start | bytes 2359296 | tf_op jit(solution)/shard_map/psum | solution.py:68
  161.5 32.9 %all-to-all-start.3 = ((bf16[4,48,3072]{2,1,0:T(8,128)(2,1)}), bf16[4,48,3072]{2,1,0:T(8,128)(2,1)S(1)}, u32[]{:S(2)}, u32[]{:S(2)}) async-start(bf16[4,48,3072]{2,1,0:T(8,128)(2,1)} %all-reduce.2.cloned.1.call-done), calls=%async_computation.3 | async-start | bytes 2359296 | tf_op jit(solution)/shard_map/all_to_all | solution.py:70
Sparse Core Ops, SparseCore 0:
  125.4 36.0 all-reduce.1
where the time goes:
time: 204 us; the launch traced here: 203 us
  waiting for transfers between devices  84.1 us (41%)
  blocking collectives  59 us (29%)
  matrix products  23.6 us (12%)
  between operations  13.5 us (7%)
  starting transfers between devices  13.3 us (7%)
  local copies, waits for them, and re-layouts  6.41 us (3%)
  other arithmetic  3.28 us (2%)
    psum x1, waiting for transfers between devices, local(): summed = lax.psum(partial_rows, 'tensor').astype(jnp.float32)  36.2 us
    all_to_all x1, blocking collectives, local(): lax.all_to_all(send_in, 'expert', split_axis=0, concat_axis=0, tiled=True)  33.9 us
    all_to_all x1, waiting for transfers between devices, local(): lax.all_to_all(outgoing, 'expert', split_axis=0, concat_axis=0, tiled=True)  28.1 us
    all_to_all x1, waiting for transfers between devices, local(): lax.all_to_all(send_grad, 'expert', split_axis=0, concat_axis=0, tiled=True)  19.7 us
    dot_general x1, matrix products, local(): jnp.einsum('rh,dh->rd', scaled, w_in[0], preferred_element_type=jnp.float32)  15.2 us
    dot_general x1, matrix products, local(): preact = jnp.dot(flat_in, w_in[0], preferred_element_type=jnp.float32)  8.34 us
    all_gather x1, blocking collectives, local(): lax.all_gather(out_grad, 'tensor', axis=0, tiled=True)  6.78 us
    all_gather x1, blocking collectives, local(): lax.all_gather(tokens_in, 'tensor', axis=0, tiled=True)  6.67 us
  transfers between devices with their start and end apart: 4, of which 3 were waited for; matrix products, arithmetic and copies ran while one was open for 6% of the time, Pallas kernels for 0%

commit v1 on v0

--- a/solution.py
+++ b/solution.py
@@ -3,6 +3,8 @@
 import jax
 import jax.numpy as jnp
 from jax import lax
+from jax.experimental import pallas as pl
+from jax.experimental.pallas import tpu as pltpu
 from jax.sharding import PartitionSpec as P
 
 
@@ -30,7 +32,7 @@
     return (target, source, filled)
 
 
-def local(tokens_in, out_grad, expert_ids, gate_probs, w_in, w_out):
+def routed(tokens_in, out_grad, expert_ids, gate_probs, w_in, w_out):
     experts = lax.axis_size("expert")
     shards = lax.axis_size("tensor")
     local_rows = tokens_in.shape[0]
@@ -77,6 +79,219 @@
     return jnp.sum(picked, axis=1).astype(jnp.bfloat16)
 
 
+CORES = 2
+LANES = 128
+CHUNKS = 2
+NT = (((1,), (1,)), ((), ()))
+
+
+def in_vmem(array):
+    return pltpu.with_memory_space_constraint(array, pltpu.VMEM)
+
+
+def whole_block():
+    return pl.BlockSpec(memory_space=pltpu.VMEM)
+
+
+def assemble(pieces, rows_ref):
+    start = 0
+    width = rows_ref.shape[1]
+    for piece in pieces:
+        rows_ref[pl.ds(start, piece.shape[0]), :] = piece[:, :width]
+        start += piece.shape[0]
+
+
+def slope_rows(pieces, weight, tile):
+    rows = sum(piece.shape[0] for piece in pieces)
+    features, width = weight.shape
+
+    def kernel(*refs):
+        *piece_refs, weight_ref, out_ref, rows_ref = refs
+        assemble(piece_refs, rows_ref)
+
+        @pl.loop(0, width // tile)
+        def _(step):
+            cols = pl.ds(pl.multiple_of(step * tile, tile), tile)
+            preact = jnp.dot(
+                rows_ref[...], weight_ref[:, cols], preferred_element_type=jnp.float32
+            )
+            out_ref[:, cols] = gelu_slope(preact)
+
+    return pl.pallas_call(
+        kernel,
+        out_shape=jax.ShapeDtypeStruct((rows, width), jnp.float32),
+        in_specs=[whole_block()] * (len(pieces) + 1),
+        out_specs=whole_block(),
+        scratch_shapes=[pltpu.VMEM((rows, features), jnp.bfloat16)],
+        compiler_params=pltpu.CompilerParams(vmem_limit_bytes=16 * 2**20),
+        cost_estimate=pl.CostEstimate(
+            flops=2 * rows * features * width,
+            bytes_accessed=4 * rows * width + 2 * rows * features,
+            transcendentals=rows * width,
+        ),
+    )(*pieces, in_vmem(weight))
+
+
+def scaled_rows(pieces, weight, slope, tile):
+    rows, width = slope.shape
+    features = weight.shape[1]
+
+    def kernel(expert_ref, *refs):
+        *piece_refs, weight_ref, slope_ref, out_ref, rows_ref, gate_ref = refs
+        assemble(piece_refs, rows_ref)
+        start = 0
+        for piece in piece_refs:
+            gates = piece[:, features:].astype(jnp.float32)
+            lane = lax.broadcasted_iota(jnp.int32, gates.shape, 1)
+            gate_ref[pl.ds(start, piece.shape[0]), :] = jnp.sum(
+                jnp.where(lane == expert_ref[0], gates, 0.0), axis=1, keepdims=True
+            )
+            start += piece.shape[0]
+
+        @pl.loop(0, width // tile)
+        def _(step):
+            cols = pl.ds(pl.multiple_of(step * tile, tile), tile)
+            hidden_grad = lax.dot_general(
+                rows_ref[...], weight_ref[cols, :], NT, preferred_element_type=jnp.float32
+            )
+            out_ref[:, cols] = (gate_ref[...] * hidden_grad * slope_ref[:, cols]).astype(
+                jnp.bfloat16
+            )
+
+    expert = lax.axis_index("expert").astype(jnp.int32).reshape(1)
+    return pl.pallas_call(
+        kernel,
+        out_shape=jax.ShapeDtypeStruct((rows, width), jnp.bfloat16),
+        in_specs=[pl.BlockSpec(memory_space=pltpu.SMEM)] + [whole_block()] * (len(pieces) + 2),
+        out_specs=whole_block(),
+        scratch_shapes=[
+            pltpu.VMEM((rows, features), jnp.bfloat16),
+            pltpu.VMEM((rows, 1), jnp.float32),
+        ],
+        compiler_params=pltpu.CompilerParams(vmem_limit_bytes=16 * 2**20),
+        cost_estimate=pl.CostEstimate(
+            flops=2 * rows * features * width,
+            bytes_accessed=6 * rows * width + 2 * rows * features,
+            transcendentals=0,
+        ),
+    )(expert, *pieces, in_vmem(weight), slope)
+
+
+def partial_rows(scaled, weight, first, count, tile):
+    rows, width = scaled.shape
+    half = rows // CORES
+
+    def kernel(scaled_ref, weight_ref, *out_refs):
+        @pl.loop(0, count // tile)
+        def _(step):
+            offset = pl.multiple_of(step * tile, tile)
+            cols = pl.ds(offset, tile)
+            product = lax.dot_general(
+                scaled_ref[...],
+                weight_ref[pl.ds(first + offset, tile), :],
+                NT,
+                preferred_element_type=jnp.float32,
+            ).astype(jnp.bfloat16)
+            for place, out_ref in enumerate(out_refs):
+                out_ref[:, cols] = product[place * half : (place + 1) * half]
+
+    return pl.pallas_call(
+        kernel,
+        out_shape=[jax.ShapeDtypeStruct((half, count), jnp.bfloat16)] * CORES,
+        in_specs=[whole_block()] * 2,
+        out_specs=[whole_block()] * CORES,
+        compiler_params=pltpu.CompilerParams(vmem_limit_bytes=16 * 2**20),
+        cost_estimate=pl.CostEstimate(
+            flops=2 * rows * count * width,
+            bytes_accessed=2 * rows * (count + width),
+            transcendentals=0,
+        ),
+    )(scaled, in_vmem(weight))
+
+
+def along_expert(array, shift):
+    size = lax.axis_size("expert")
+    return lax.ppermute(array, "expert", [(i, (i + shift) % size) for i in range(size)])
+
+
+def along_chips(array, shift):
+    size = lax.axis_size("tensor")
+    return lax.ppermute(
+        array, "tensor", [(i, (i + CORES * shift) % size) for i in range(size)]
+    )
+
+
+def other_core(array):
+    size = lax.axis_size("tensor")
+    return lax.ppermute(array, "tensor", [(i, i ^ 1) for i in range(size)])
+
+
+def gather_rows(block):
+    experts, chips = lax.axis_size("expert"), lax.axis_size("tensor") // CORES
+    rows = block.shape[0]
+    column = jnp.concatenate(
+        [block] + [along_expert(block, shift) for shift in range(1, experts)], axis=0
+    )
+    pieces = [column]
+    for shift in range(1, chips):
+        pieces.append(along_chips(block, shift))
+        pieces.append(along_chips(column[rows:], shift))
+    beside = jnp.concatenate(pieces[1:], axis=0)
+    return [column, beside, other_core(column), other_core(beside)]
+
+
+def add_rows(*terms):
+    total = terms[0].astype(jnp.float32)
+    for term in terms[1:]:
+        total = total + term.astype(jnp.float32)
+    return total.astype(jnp.bfloat16)
+
+
+def scatter_rows(kept, sent, rows):
+    experts, chips = lax.axis_size("expert"), lax.axis_size("tensor") // CORES
+    total = add_rows(kept, other_core(sent))
+    column = rows * experts
+    total = add_rows(
+        total[:column],
+        *[
+            along_chips(total[shift * column : (shift + 1) * column], -shift)
+            for shift in range(1, chips)
+        ],
+    )
+    return add_rows(
+        total[:rows],
+        *[
+            along_expert(total[shift * rows : (shift + 1) * rows], -shift)
+            for shift in range(1, experts)
+        ],
+    )
+
+
+def dense(tokens_in, out_grad, expert_ids, gate_probs, w_in, w_out):
+    local_rows, features = tokens_in.shape
+    lane = jnp.arange(LANES, dtype=jnp.int32)
+    named = expert_ids[:, :, None] == lane
+    gates = jnp.sum(jnp.where(named, gate_probs[:, :, None].astype(jnp.float32), 0.0), axis=1)
+    grads = jnp.concatenate([out_grad, gates.astype(jnp.bfloat16)], axis=1)
+    input_pieces = gather_rows(tokens_in)
+    grad_pieces = gather_rows(grads)
+    slope = slope_rows(input_pieces, w_in[0], 1024)
+    scaled = scaled_rows(grad_pieces, w_out[0], slope, 1024)
+    count = features // CHUNKS
+    chunks = [
+        scatter_rows(*partial_rows(scaled, w_in[0], place * count, count, 768), local_rows)
+        for place in range(CHUNKS)
+    ]
+    return jnp.concatenate(chunks, axis=1)
+
+
+def local(*args):
+    experts = lax.axis_size("expert")
+    if experts <= 6 and lax.axis_size("tensor") % CORES == 0:
+        return dense(*args)
+    return routed(*args)
+
+
 def solution(mesh):
     return jax.shard_map(
         local,

time: 204 us -> 94.8 us (0.46)
  blocking collectives: 59 us -> 0 us
  waiting for transfers between devices: 84.1 us -> 41.7 us
  matrix products: 23.6 us -> 0 us
  between operations: 13.5 us -> 0.27 us
  Pallas kernels: 0 us -> 12.6 us
  starting transfers between devices: 13.3 us -> 25.4 us
  local copies, waits for them, and re-layouts: 6.41 us -> 10.2 us
    all_to_all x3 -> x0, waiting for transfers between devices: 47.8 us -> none  [the longest x1 28.1 us: local(): lax.all_to_all(outgoing, 'expert', split_axis=0, concat_axis=0, tiled=True)]
    ppermute x0 -> x24, waiting for transfers between devices: none -> 41.7 us  [the longest x6 21.5 us: along_chips(): lax.ppermute(array, 'tensor', [(i, (i + CORES * shift) % size) for i in r...]
    psum x1 -> x0, waiting for transfers between devices: 36.2 us -> none  [local(): summed = lax.psum(partial_rows, 'tensor').astype(jnp.float32)]
    all_to_all x1 -> x0, blocking collectives: 33.9 us -> none  [local(): lax.all_to_all(send_in, 'expert', split_axis=0, concat_axis=0, tiled=True)]
    ppermute x0 -> x24, starting transfers between devices: none -> 25.4 us  [the longest x12 17.6 us: along_expert(): lax.ppermute(array, 'expert', [(i, (i + shift) % size) for i in range(siz...]
    all_gather x4 -> x0, blocking collectives: 25.1 us -> none  [the longest x1 6.78 us: local(): lax.all_gather(out_grad, 'tensor', axis=0, tiled=True)]
    dot_general x2 -> x0, matrix products: 23.6 us -> none  [the longest x1 15.2 us: local(): jnp.einsum('rh,dh->rd', scaled, w_in[0], preferred_element_type=jnp.float32)]
    all_to_all x3 -> x0, starting transfers between devices: 13.2 us -> none  [the longest x1 5.11 us: local(): lax.all_to_all(send_gate, 'expert', split_axis=0, concat_axis=0, tiled=True)]
  transfers between devices with their start and end apart: 4 -> 24, of which waited for: 3 -> 13; matrix products, arithmetic and copies ran while one was open for 6% -> 2% of each run, Pallas kernels for 0% -> 7%
where the time goes in v1:
time: 94.8 us; the launch traced here: 94.5 us
  waiting for transfers between devices  41.7 us (44%)
  starting transfers between devices  25.4 us (27%)
  Pallas kernels  12.6 us (13%)
  local copies, waits for them, and re-layouts  10.2 us (11%)
  other arithmetic  4.27 us (5%)
    ppermute x6, waiting for transfers between devices, along_chips(): lax.ppermute(array, 'tensor', [(i, (i + CORES * shift) % size) for i in r...  21.5 us
    ppermute x12, waiting for transfers between devices, along_expert(): lax.ppermute(array, 'expert', [(i, (i + shift) % size) for i in range(siz...  19.7 us
    ppermute x12, starting transfers between devices, along_expert(): lax.ppermute(array, 'expert', [(i, (i + shift) % size) for i in range(siz...  17.6 us
    unnamed x15, local copies, waits for them, and re-layouts  10.1 us
    ppermute x6, starting transfers between devices, along_chips(): lax.ppermute(array, 'tensor', [(i, (i + CORES * shift) % size) for i in r...  6.92 us
    pallas_call x1, Pallas kernels, slope_rows(): pl.pallas_call(kernel, out_shape=jax.ShapeDtypeStruct((rows, width), jnp....  4.71 us
    pallas_call x2, Pallas kernels, partial_rows(): pl.pallas_call(kernel, out_shape=[jax.ShapeDtypeStruct((half, count), jnp...  4.07 us
    pallas_call x1, Pallas kernels, scaled_rows(): pl.pallas_call(kernel, out_shape=jax.ShapeDtypeStruct((rows, width), jnp....  3.85 us
  transfers between devices with their start and end apart: 24, of which 13 were waited for; matrix products, arithmetic and copies ran while one was open for 2% of the time, Pallas kernels for 7%

profile of v1, /device:TPU:0, one launch (start us, length us, event | category | flops | bytes accessed | tf_op | source)
XLA Modules:
  0.0 94.5 jit_solution(12159338577535834108)
XLA Ops:
  0.0 0.7 convert_element_type.73
  0.7 0.8 select_reduce_fusion
  1.4 0.9 pad_maximum_fusion.3
  2.3 3.0 %collective-permute-start = (bf16[16,3200]{1,0:T(8,128)(2,1)S(1)}, bf16[16,3200]{1,0:T(8,128)(2,1)S(1)}, u32[]{:S(2)}, u32[]{:S(2)}) collective-permute-start(bf16[16,3200]{1,0:T(8,128)(2,1)S(1)} %pad_maximum_fusion.3), channel_id=1, source_target_pairs={{0,4},{4,8},{8,12},{12,0},{1,5},{5,9},{9,13},{13,1},{2,6},{6,10},{... | collective-permute-start | bytes 307208 | tf_op jit(solution)/shard_map/ppermute | solution.py:214
  5.3 2.6 %collective-permute-start.1 = (bf16[16,3200]{1,0:T(8,128)(2,1)S(1)}, bf16[16,3200]{1,0:T(8,128)(2,1)S(1)}, u32[]{:S(2)}, u32[]{:S(2)}) collective-permute-start(bf16[16,3200]{1,0:T(8,128)(2,1)S(1)} %pad_maximum_fusion.3), channel_id=1, source_target_pairs={{0,8},{4,12},{8,0},{12,4},{1,9},{5,13},{9,1},{13,5},{2,10},{6,14},... | collective-permute-start | bytes 307208 | tf_op jit(solution)/shard_map/ppermute | solution.py:214
  7.9 1.3 %collective-permute-start.2 = (bf16[16,3200]{1,0:T(8,128)(2,1)S(1)}, bf16[16,3200]{1,0:T(8,128)(2,1)S(1)}, u32[]{:S(2)}, u32[]{:S(2)}) collective-permute-start(bf16[16,3200]{1,0:T(8,128)(2,1)S(1)} %pad_maximum_fusion.3), channel_id=1, source_target_pairs={{0,12},{4,0},{8,4},{12,8},{1,13},{5,1},{9,5},{13,9},{2,14},{6,2},{... | collective-permute-start | bytes 307208 | tf_op jit(solution)/shard_map/ppermute | solution.py:214
  9.3 1.5 %collective-permute-start.3 = (bf16[16,3200]{1,0:T(8,128)(2,1)S(1)}, bf16[16,3200]{1,0:T(8,128)(2,1)S(1)}, u32[]{:S(2)}, u32[]{:S(2)}) collective-permute-start(bf16[16,3200]{1,0:T(8,128)(2,1)S(1)} %pad_maximum_fusion.3), channel_id=1, source_target_pairs={{0,2},{1,3},{2,0},{3,1},{4,6},{5,7},{6,4},{7,5},{8,10},{9,11},{10,... | collective-permute-start | bytes 307208 | tf_op jit(solution)/shard_map/ppermute | solution.py:219
  10.8 0.7 collective-permute-start.7
  11.4 0.9 constant_dynamic-update-slice_fusion.5
  12.4 5.1 %collective-permute-done.7 = bf16[16,3072]{1,0:T(8,128)(2,1)S(1)} collective-permute-done((bf16[16,3072]{1,0:T(8,128)(2,1)}, bf16[16,3072]{1,0:T(8,128)(2,1)S(1)}, u32[]{:S(2)}, u32[]{:S(2)}) %collective-permute-start.7) | collective-permute-done | bytes 98336 | tf_op jit(solution)/shard_map/ppermute | solution.py:214
  17.5 2.4 %collective-permute-start.8 = (bf16[16,3072]{1,0:T(8,128)(2,1)}, bf16[16,3072]{1,0:T(8,128)(2,1)S(1)}, u32[]{:S(2)}, u32[]{:S(2)}) collective-permute-start(bf16[16,3072]{1,0:T(8,128)(2,1)} %param.6), channel_id=1, source_target_pairs={{0,8},{4,12},{8,0},{12,4},{1,9},{5,13},{9,1},{13,5},{2,10},{6,14},... | collective-permute-start | bytes 294920 | tf_op jit(solution)/shard_map/ppermute | solution.py:214
  19.9 4.5 %collective-permute-done.8 = bf16[16,3072]{1,0:T(8,128)(2,1)S(1)} collective-permute-done((bf16[16,3072]{1,0:T(8,128)(2,1)}, bf16[16,3072]{1,0:T(8,128)(2,1)S(1)}, u32[]{:S(2)}, u32[]{:S(2)}) %collective-permute-start.8) | collective-permute-done | bytes 98336 | tf_op jit(solution)/shard_map/ppermute | solution.py:214
  24.4 0.2 collective-permute-start.9
  24.6 4.7 %collective-permute-done.9 = bf16[16,3072]{1,0:T(8,128)(2,1)S(1)} collective-permute-done((bf16[16,3072]{1,0:T(8,128)(2,1)}, bf16[16,3072]{1,0:T(8,128)(2,1)S(1)}, u32[]{:S(2)}, u32[]{:S(2)}) %collective-permute-start.9) | collective-permute-done | bytes 98336 | tf_op jit(solution)/shard_map/ppermute | solution.py:214
  29.3 1.0 %collective-permute-start.10 = (bf16[16,3072]{1,0:T(8,128)(2,1)}, bf16[16,3072]{1,0:T(8,128)(2,1)S(1)}, u32[]{:S(2)}, u32[]{:S(2)}) collective-permute-start(bf16[16,3072]{1,0:T(8,128)(2,1)} %param.6), channel_id=1, source_target_pairs={{0,2},{1,3},{2,0},{3,1},{4,6},{5,7},{6,4},{7,5},{8,10},{9,11},{10,... | collective-permute-start | bytes 294920 | tf_op jit(solution)/shard_map/ppermute | solution.py:219
  30.3 3.8 %collective-permute-done.10 = bf16[16,3072]{1,0:T(8,128)(2,1)S(1)} collective-permute-done((bf16[16,3072]{1,0:T(8,128)(2,1)}, bf16[16,3072]{1,0:T(8,128)(2,1)S(1)}, u32[]{:S(2)}, u32[]{:S(2)}) %collective-permute-start.10) | collective-permute-done | bytes 98336 | tf_op jit(solution)/shard_map/ppermute | solution.py:219
  34.1 1.1 %collective-permute-start.11 = (bf16[48,3072]{1,0:T(8,128)(2,1)S(1)}, bf16[48,3072]{1,0:T(8,128)(2,1)S(1)}, u32[]{:S(2)}, u32[]{:S(2)}) collective-permute-start(bf16[48,3072]{1,0:T(8,128)(2,1)S(1)} %pad_maximum_fusion.2), channel_id=1, source_target_pairs={{0,2},{1,3},{2,0},{3,1},{4,6},{5,7},{6,4},{7,5},{8,10},{9,11},{10,... | collective-permute-start | bytes 884744 | tf_op jit(solution)/shard_map/ppermute | solution.py:219
  35.2 1.1 %collective-permute-start.4 = (bf16[48,3200]{1,0:T(8,128)(2,1)S(1)}, bf16[48,3200]{1,0:T(8,128)(2,1)S(1)}, u32[]{:S(2)}, u32[]{:S(2)}) collective-permute-start(bf16[48,3200]{1,0:T(8,128)(2,1)S(1)} %pad_maximum_fusion.1), channel_id=1, source_target_pairs={{0,2},{1,3},{2,0},{3,1},{4,6},{5,7},{6,4},{7,5},{8,10},{9,11},{10,... | collective-permute-start | bytes 921608 | tf_op jit(solution)/shard_map/ppermute | solution.py:219
  36.3 0.9 pad_maximum_fusion.refs_0_
  37.2 0.1 collective-permute-start.5
  37.3 6.6 %collective-permute-done.11 = bf16[48,3072]{1,0:T(8,128)(2,1)S(1)} collective-permute-done((bf16[48,3072]{1,0:T(8,128)(2,1)S(1)}, bf16[48,3072]{1,0:T(8,128)(2,1)S(1)}, u32[]{:S(2)}, u32[]{:S(2)}) %collective-permute-start.11) | collective-permute-done | bytes 294944 | tf_op jit(solution)/shard_map/ppermute | solution.py:219
  44.0 0.1 collective-permute-start.13
  44.1 6.1 %collective-permute-done.4 = bf16[48,3200]{1,0:T(8,128)(2,1)S(1)} collective-permute-done((bf16[48,3200]{1,0:T(8,128)(2,1)S(1)}, bf16[48,3200]{1,0:T(8,128)(2,1)S(1)}, u32[]{:S(2)}, u32[]{:S(2)}) %collective-permute-start.4) | collective-permute-done | bytes 307232 | tf_op jit(solution)/shard_map/ppermute | solution.py:219
  50.3 4.6 %copy-done = bf16[1,3072,2048]{2,1,0:T(8,128)(2,1)S(1)} copy-done((bf16[1,3072,2048]{2,1,0:T(8,128)(2,1)S(1)}, bf16[1,3072,2048]{2,1,0:T(8,128)(2,1)}, u32[]{:S(2)}) %copy-start) | copy-done | bytes 12582936
  54.9 4.7 %shard_map.64.refs_5_ = f32[256,2048]{1,0:T(8,128)S(1)} custom-call(bf16[64,3072]{1,0:T(8,128)(2,1)S(1)} %constant_dynamic-update-slice_fusion.2.refs_0_, bf16[64,3072]{1,0:T(8,128)(2,1)S(1)} %constant_dynamic-update-slice_fusion.6.refs_1_, bf16[64,3072]{1,0:T(8,128)(2,1)S(1)} %collective-permute-done.12.refs_2_, ...), custom_call_target="tpu_custom_call" | custom-call | flops 3221225472 | bytes 3670016 | tf_op jit(solution)/shard_map/pallas_call | solution.py:120
  59.6 4.6 %copy-done.1 = bf16[1,2048,3072]{2,1,0:T(8,128)(2,1)S(1)} copy-done((bf16[1,2048,3072]{2,1,0:T(8,128)(2,1)S(1)}, bf16[1,2048,3072]{2,1,0:T(8,128)(2,1)}, u32[]{:S(2)}) %copy-start.1) | copy-done | bytes 12582936
  64.2 3.9 %shard_map.65.scaled_ref = bf16[256,2048]{1,0:T(8,128)(2,1)S(1)} custom-call(s32[1]{0:T(128)} %bitcast.expert_ref, bf16[64,3200]{1,0:T(8,128)(2,1)S(1)} %pad_maximum_fusion.refs_0_, bf16[64,3200]{1,0:T(8,128)(2,1)S(1)} %constant_dynamic-update-slice_fusion.refs_1_, bf16[64,3200]{1,0:T(8,128)(2,1)S(1)} %collective-permute-done.5.refs_2_, ...), custom_call_target="tpu_custom_call" | custom-call | flops 3221225472 | bytes 4718592 | tf_op jit(solution)/shard_map/pallas_call | solution.py:162
  68.1 2.0 %shard_map.66 = (bf16[128,1536]{1,0:T(8,128)(2,1)S(1)}, bf16[128,1536]{1,0:T(8,128)(2,1)S(1)}) custom-call(bf16[256,2048]{1,0:T(8,128)(2,1)S(1)} %shard_map.65.scaled_ref, bf16[3072,2048]{1,0:T(8,128)(2,1)S(1)} %bitcast.6), custom_call_target="tpu_custom_call" | custom-call | flops 1610612736 | bytes 1835008 | tf_op jit(solution)/shard_map/pallas_call | solution.py:198
  70.1 0.5 collective-permute-start.14
  70.7 2.0 %shard_map.67 = (bf16[128,1536]{1,0:T(8,128)(2,1)S(1)}, bf16[128,1536]{1,0:T(8,128)(2,1)S(1)}) custom-call(bf16[256,2048]{1,0:T(8,128)(2,1)S(1)} %shard_map.65.scaled_ref, bf16[3072,2048]{1,0:T(8,128)(2,1)S(1)} %bitcast.7), custom_call_target="tpu_custom_call" | custom-call | flops 1610612736 | bytes 1835008 | tf_op jit(solution)/shard_map/pallas_call | solution.py:198
  72.7 0.1 collective-permute-start.19
  72.8 0.1 add_convert_fusion.1
  73.0 1.1 %collective-permute-start.15 = (bf16[64,1536]{1,0:T(8,128)(2,1)S(1)}, bf16[64,1536]{1,0:T(8,128)(2,1)S(1)}, u32[]{:S(2)}, u32[]{:S(2)}) collective-permute-start(bf16[64,1536]{1,0:T(8,128)(2,1)S(1)} %slice.53), channel_id=1, source_target_pairs={{0,2},{1,3},{2,0},{3,1},{4,6},{5,7},{6,4},{7,5},{8,10},{9,11},{10,... | collective-permute-start | bytes 589832 | tf_op jit(solution)/shard_map/ppermute | solution.py:219
  74.1 0.5 collective-permute-done.19
  74.5 0.1 add_convert_fusion
  74.6 1.1 %collective-permute-start.20 = (bf16[64,1536]{1,0:T(8,128)(2,1)S(1)}, bf16[64,1536]{1,0:T(8,128)(2,1)S(1)}, u32[]{:S(2)}, u32[]{:S(2)}) collective-permute-start(bf16[64,1536]{1,0:T(8,128)(2,1)S(1)} %slice.59), channel_id=1, source_target_pairs={{0,2},{1,3},{2,0},{3,1},{4,6},{5,7},{6,4},{7,5},{8,10},{9,11},{10,... | collective-permute-start | bytes 589832 | tf_op jit(solution)/shard_map/ppermute | solution.py:219
  75.8 5.0 %collective-permute-done.15 = bf16[64,1536]{1,0:T(8,128)(2,1)S(1)} collective-permute-done((bf16[64,1536]{1,0:T(8,128)(2,1)S(1)}, bf16[64,1536]{1,0:T(8,128)(2,1)S(1)}, u32[]{:S(2)}, u32[]{:S(2)}) %collective-permute-start.15) | collective-permute-done | bytes 196640 | tf_op jit(solution)/shard_map/ppermute | solution.py:219
  80.8 2.0 %collective-permute-start.16 = (bf16[16,1536]{1,0:T(8,128)(2,1)S(1)}, bf16[16,1536]{1,0:T(8,128)(2,1)S(1)}, u32[]{:S(2)}, u32[]{:S(2)}) collective-permute-start(bf16[16,1536]{1,0:T(8,128)(2,1)S(1)} %get-tuple-element.13), channel_id=1, source_target_pairs={{0,12},{4,0},{8,4},{12,8},{1,13},{5,1},{9,5},{13,9},{2,14},{6,2},{... | collective-permute-start | bytes 147464 | tf_op jit(solution)/shard_map/ppermute | solution.py:214
  82.8 1.7 %collective-permute-start.18 = (bf16[16,1536]{1,0:T(8,128)(2,1)S(1)}, bf16[16,1536]{1,0:T(8,128)(2,1)S(1)}, u32[]{:S(2)}, u32[]{:S(2)}) collective-permute-start(bf16[16,1536]{1,0:T(8,128)(2,1)S(1)} %get-tuple-element.14), channel_id=1, source_target_pairs={{0,4},{4,8},{8,12},{12,0},{1,5},{5,9},{9,13},{13,1},{2,6},{6,10},{... | collective-permute-start | bytes 147464 | tf_op jit(solution)/shard_map/ppermute | solution.py:214
  84.6 2.2 %collective-permute-start.21 = (bf16[16,1536]{1,0:T(8,128)(2,1)S(1)}, bf16[16,1536]{1,0:T(8,128)(2,1)S(1)}, u32[]{:S(2)}, u32[]{:S(2)}) collective-permute-start(bf16[16,1536]{1,0:T(8,128)(2,1)S(1)} %get-tuple-element.16), channel_id=1, source_target_pairs={{0,12},{4,0},{8,4},{12,8},{1,13},{5,1},{9,5},{13,9},{2,14},{6,2},{... | collective-permute-start | bytes 147464 | tf_op jit(solution)/shard_map/ppermute | solution.py:214
  86.8 1.1 %collective-permute-start.22 = (bf16[16,1536]{1,0:T(8,128)(2,1)S(1)}, bf16[16,1536]{1,0:T(8,128)(2,1)S(1)}, u32[]{:S(2)}, u32[]{:S(2)}) collective-permute-start(bf16[16,1536]{1,0:T(8,128)(2,1)S(1)} %get-tuple-element.18), channel_id=1, source_target_pairs={{0,8},{4,12},{8,0},{12,4},{1,9},{5,13},{9,1},{13,5},{2,10},{6,14},... | collective-permute-start | bytes 147464 | tf_op jit(solution)/shard_map/ppermute | solution.py:214
  87.9 0.4 collective-permute-start.23
  88.3 0.2 collective-permute-done.17
  88.5 0.6 collective-permute-done.18
  89.1 0.2 collective-permute-done.21
  89.3 2.9 %collective-permute-done.22 = bf16[16,1536]{1,0:T(8,128)(2,1)S(1)} collective-permute-done((bf16[16,1536]{1,0:T(8,128)(2,1)S(1)}, bf16[16,1536]{1,0:T(8,128)(2,1)S(1)}, u32[]{:S(2)}, u32[]{:S(2)}) %collective-permute-start.22) | collective-permute-done | bytes 49184 | tf_op jit(solution)/shard_map/ppermute | solution.py:214
  92.3 1.5 %collective-permute-done.23 = bf16[16,1536]{1,0:T(8,128)(2,1)S(1)} collective-permute-done((bf16[16,1536]{1,0:T(8,128)(2,1)S(1)}, bf16[16,1536]{1,0:T(8,128)(2,1)S(1)}, u32[]{:S(2)}, u32[]{:S(2)}) %collective-permute-start.23) | collective-permute-done | bytes 49184 | tf_op jit(solution)/shard_map/ppermute | solution.py:214
  93.8 0.6 pad_maximum_fusion.4
  (40 shorter events, 0.5 us)
Async XLA Ops:
  2.3 31.8 %collective-permute-start = (bf16[16,3200]{1,0:T(8,128)(2,1)S(1)}, bf16[16,3200]{1,0:T(8,128)(2,1)S(1)}, u32[]{:S(2)}, u32[]{:S(2)}) collective-permute-start(bf16[16,3200]{1,0:T(8,128)(2,1)S(1)} %pad_maximum_fusion.3), channel_id=1, source_target_pairs={{0,4},{4,8},{8,12},{12,0},{1,5},{5,9},{9,13},{13,1},{2,6},{6,10},{... | collective-permute-start | bytes 307208 | tf_op jit(solution)/shard_map/ppermute | solution.py:214
  5.3 29.9 %collective-permute-start.1 = (bf16[16,3200]{1,0:T(8,128)(2,1)S(1)}, bf16[16,3200]{1,0:T(8,128)(2,1)S(1)}, u32[]{:S(2)}, u32[]{:S(2)}) collective-permute-start(bf16[16,3200]{1,0:T(8,128)(2,1)S(1)} %pad_maximum_fusion.3), channel_id=1, source_target_pairs={{0,8},{4,12},{8,0},{12,4},{1,9},{5,13},{9,1},{13,5},{2,10},{6,14},... | collective-permute-start | bytes 307208 | tf_op jit(solution)/shard_map/ppermute | solution.py:214
  7.9 27.3 %collective-permute-start.2 = (bf16[16,3200]{1,0:T(8,128)(2,1)S(1)}, bf16[16,3200]{1,0:T(8,128)(2,1)S(1)}, u32[]{:S(2)}, u32[]{:S(2)}) collective-permute-start(bf16[16,3200]{1,0:T(8,128)(2,1)S(1)} %pad_maximum_fusion.3), channel_id=1, source_target_pairs={{0,12},{4,0},{8,4},{12,8},{1,13},{5,1},{9,5},{13,9},{2,14},{6,2},{... | collective-permute-start | bytes 307208 | tf_op jit(solution)/shard_map/ppermute | solution.py:214
  9.3 28.0 %collective-permute-start.3 = (bf16[16,3200]{1,0:T(8,128)(2,1)S(1)}, bf16[16,3200]{1,0:T(8,128)(2,1)S(1)}, u32[]{:S(2)}, u32[]{:S(2)}) collective-permute-start(bf16[16,3200]{1,0:T(8,128)(2,1)S(1)} %pad_maximum_fusion.3), channel_id=1, source_target_pairs={{0,2},{1,3},{2,0},{3,1},{4,6},{5,7},{6,4},{7,5},{8,10},{9,11},{10,... | collective-permute-start | bytes 307208 | tf_op jit(solution)/shard_map/ppermute | solution.py:219
  10.8 6.7 %collective-permute-start.7 = (bf16[16,3072]{1,0:T(8,128)(2,1)}, bf16[16,3072]{1,0:T(8,128)(2,1)S(1)}, u32[]{:S(2)}, u32[]{:S(2)}) collective-permute-start(bf16[16,3072]{1,0:T(8,128)(2,1)} %param.6), channel_id=1, source_target_pairs={{0,4},{4,8},{8,12},{12,0},{1,5},{5,9},{9,13},{13,1},{2,6},{6,10},{... | collective-permute-start | bytes 294920 | tf_op jit(solution)/shard_map/ppermute | solution.py:214
  17.5 6.9 %collective-permute-start.8 = (bf16[16,3072]{1,0:T(8,128)(2,1)}, bf16[16,3072]{1,0:T(8,128)(2,1)S(1)}, u32[]{:S(2)}, u32[]{:S(2)}) collective-permute-start(bf16[16,3072]{1,0:T(8,128)(2,1)} %param.6), channel_id=1, source_target_pairs={{0,8},{4,12},{8,0},{12,4},{1,9},{5,13},{9,1},{13,5},{2,10},{6,14},... | collective-permute-start | bytes 294920 | tf_op jit(solution)/shard_map/ppermute | solution.py:214
  24.4 4.8 %collective-permute-start.9 = (bf16[16,3072]{1,0:T(8,128)(2,1)}, bf16[16,3072]{1,0:T(8,128)(2,1)S(1)}, u32[]{:S(2)}, u32[]{:S(2)}) collective-permute-start(bf16[16,3072]{1,0:T(8,128)(2,1)} %param.6), channel_id=1, source_target_pairs={{0,12},{4,0},{8,4},{12,8},{1,13},{5,1},{9,5},{13,9},{2,14},{6,2},{... | collective-permute-start | bytes 294920 | tf_op jit(solution)/shard_map/ppermute | solution.py:214
  29.3 4.8 %collective-permute-start.10 = (bf16[16,3072]{1,0:T(8,128)(2,1)}, bf16[16,3072]{1,0:T(8,128)(2,1)S(1)}, u32[]{:S(2)}, u32[]{:S(2)}) collective-permute-start(bf16[16,3072]{1,0:T(8,128)(2,1)} %param.6), channel_id=1, source_target_pairs={{0,2},{1,3},{2,0},{3,1},{4,6},{5,7},{6,4},{7,5},{8,10},{9,11},{10,... | collective-permute-start | bytes 294920 | tf_op jit(solution)/shard_map/ppermute | solution.py:219
  34.1 16.2 %collective-permute-start.12 = (bf16[64,3072]{1,0:T(8,128)(2,1)S(1)}, bf16[64,3072]{1,0:T(8,128)(2,1)S(1)}, u32[]{:S(2)}, u32[]{:S(2)}) collective-permute-start(bf16[64,3072]{1,0:T(8,128)(2,1)S(1)} %constant_dynamic-update-slice_fusion.2.refs_0_), channel_id=1, source_target_pairs={{0,1},{1,0},{2,3},{3,2},{4,5},{5,4},{6,7},{7,6},{8,9},{9,8},{10,11... | collective-permute-start | bytes 1179656 | tf_op jit(solution)/shard_map/ppermute | solution.py:226
  34.1 9.9 %collective-permute-start.11 = (bf16[48,3072]{1,0:T(8,128)(2,1)S(1)}, bf16[48,3072]{1,0:T(8,128)(2,1)S(1)}, u32[]{:S(2)}, u32[]{:S(2)}) collective-permute-start(bf16[48,3072]{1,0:T(8,128)(2,1)S(1)} %pad_maximum_fusion.2), channel_id=1, source_target_pairs={{0,2},{1,3},{2,0},{3,1},{4,6},{5,7},{6,4},{7,5},{8,10},{9,11},{10,... | collective-permute-start | bytes 884744 | tf_op jit(solution)/shard_map/ppermute | solution.py:219
  35.2 14.9 %collective-permute-start.4 = (bf16[48,3200]{1,0:T(8,128)(2,1)S(1)}, bf16[48,3200]{1,0:T(8,128)(2,1)S(1)}, u32[]{:S(2)}, u32[]{:S(2)}) collective-permute-start(bf16[48,3200]{1,0:T(8,128)(2,1)S(1)} %pad_maximum_fusion.1), channel_id=1, source_target_pairs={{0,2},{1,3},{2,0},{3,1},{4,6},{5,7},{6,4},{7,5},{8,10},{9,11},{10,... | collective-permute-start | bytes 921608 | tf_op jit(solution)/shard_map/ppermute | solution.py:219
  37.2 22.4 %collective-permute-start.5 = (bf16[64,3200]{1,0:T(8,128)(2,1)S(1)}, bf16[64,3200]{1,0:T(8,128)(2,1)S(1)}, u32[]{:S(2)}, u32[]{:S(2)}) collective-permute-start(bf16[64,3200]{1,0:T(8,128)(2,1)S(1)} %pad_maximum_fusion.refs_0_), channel_id=1, source_target_pairs={{0,1},{1,0},{2,3},{3,2},{4,5},{5,4},{6,7},{7,6},{8,9},{9,8},{10,11... | collective-permute-start | bytes 1228808 | tf_op jit(solution)/shard_map/ppermute | solution.py:226
  44.0 6.3 %collective-permute-start.13 = (bf16[64,3072]{1,0:T(8,128)(2,1)S(1)}, bf16[64,3072]{1,0:T(8,128)(2,1)S(1)}, u32[]{:S(2)}, u32[]{:S(2)}) collective-permute-start(bf16[64,3072]{1,0:T(8,128)(2,1)S(1)} %constant_dynamic-update-slice_fusion.6.refs_1_), channel_id=1, source_target_pairs={{0,1},{1,0},{2,3},{3,2},{4,5},{5,4},{6,7},{7,6},{8,9},{9,8},{10,11... | collective-permute-start | bytes 1179656 | tf_op jit(solution)/shard_map/ppermute | solution.py:226
  50.2 9.4 %collective-permute-start.6 = (bf16[64,3200]{1,0:T(8,128)(2,1)S(1)}, bf16[64,3200]{1,0:T(8,128)(2,1)S(1)}, u32[]{:S(2)}, u32[]{:S(2)}) collective-permute-start(bf16[64,3200]{1,0:T(8,128)(2,1)S(1)} %constant_dynamic-update-slice_fusion.refs_1_), channel_id=1, source_target_pairs={{0,1},{1,0},{2,3},{3,2},{4,5},{5,4},{6,7},{7,6},{8,9},{9,8},{10,11... | collective-permute-start | bytes 1228808 | tf_op jit(solution)/shard_map/ppermute | solution.py:226
  50.3 4.6 %copy-start = (bf16[1,3072,2048]{2,1,0:T(8,128)(2,1)S(1)}, bf16[1,3072,2048]{2,1,0:T(8,128)(2,1)}, u32[]{:S(2)}) copy-start(bf16[1,3072,2048]{2,1,0:T(8,128)(2,1)} %param.10) | copy-start | bytes 37748740
  54.9 13.2 %slice-start = ((s8[12582912]{0:T(1024)(128)(4,1)}), s8[4194304]{0:T(1024)(128)(4,1)S(1)}, s32[]{:S(2)}) async-start(s8[12582912]{0:T(1024)(128)(4,1)} %bitcast.4), calls=%async_computation | async-start | bytes 8388608
  54.9 13.2 %slice-start.1 = ((s8[12582912]{0:T(1024)(128)(4,1)}), s8[4194304]{0:T(1024)(128)(4,1)S(1)}, s32[]{:S(2)}) async-start(s8[12582912]{0:T(1024)(128)(4,1)} %bitcast.4), calls=%async_computation.1 | async-start | bytes 8388608
  59.6 4.6 %copy-start.1 = (bf16[1,2048,3072]{2,1,0:T(8,128)(2,1)S(1)}, bf16[1,2048,3072]{2,1,0:T(8,128)(2,1)}, u32[]{:S(2)}) copy-start(bf16[1,2048,3072]{2,1,0:T(8,128)(2,1)} %param.11) | copy-start | bytes 37748740
  64.2 3.9 %slice-start.2 = ((s8[12582912]{0:T(1024)(128)(4,1)}), s8[4194304]{0:T(1024)(128)(4,1)S(1)}, s32[]{:S(2)}) async-start(s8[12582912]{0:T(1024)(128)(4,1)} %bitcast.4), calls=%async_computation.2 | async-start | bytes 8388608
  70.1 2.7 %collective-permute-start.14 = (bf16[128,1536]{1,0:T(8,128)(2,1)S(1)}, bf16[128,1536]{1,0:T(8,128)(2,1)S(1)}, u32[]{:S(2)}, u32[]{:S(2)}) collective-permute-start(bf16[128,1536]{1,0:T(8,128)(2,1)S(1)} %get-tuple-element.10), channel_id=1, source_target_pairs={{0,1},{1,0},{2,3},{3,2},{4,5},{5,4},{6,7},{7,6},{8,9},{9,8},{10,11... | collective-permute-start | bytes 1179656 | tf_op jit(solution)/shard_map/ppermute | solution.py:226
  72.7 1.8 %collective-permute-start.19 = (bf16[128,1536]{1,0:T(8,128)(2,1)S(1)}, bf16[128,1536]{1,0:T(8,128)(2,1)S(1)}, u32[]{:S(2)}, u32[]{:S(2)}) collective-permute-start(bf16[128,1536]{1,0:T(8,128)(2,1)S(1)} %get-tuple-element.12), channel_id=1, source_target_pairs={{0,1},{1,0},{2,3},{3,2},{4,5},{5,4},{6,7},{7,6},{8,9},{9,8},{10,11... | collective-permute-start | bytes 1179656 | tf_op jit(solution)/shard_map/ppermute | solution.py:226
  73.0 7.8 %collective-permute-start.15 = (bf16[64,1536]{1,0:T(8,128)(2,1)S(1)}, bf16[64,1536]{1,0:T(8,128)(2,1)S(1)}, u32[]{:S(2)}, u32[]{:S(2)}) collective-permute-start(bf16[64,1536]{1,0:T(8,128)(2,1)S(1)} %slice.53), channel_id=1, source_target_pairs={{0,2},{1,3},{2,0},{3,1},{4,6},{5,7},{6,4},{7,5},{8,10},{9,11},{10,... | collective-permute-start | bytes 589832 | tf_op jit(solution)/shard_map/ppermute | solution.py:219
  74.6 9.9 %collective-permute-start.20 = (bf16[64,1536]{1,0:T(8,128)(2,1)S(1)}, bf16[64,1536]{1,0:T(8,128)(2,1)S(1)}, u32[]{:S(2)}, u32[]{:S(2)}) collective-permute-start(bf16[64,1536]{1,0:T(8,128)(2,1)S(1)} %slice.59), channel_id=1, source_target_pairs={{0,2},{1,3},{2,0},{3,1},{4,6},{5,7},{6,4},{7,5},{8,10},{9,11},{10,... | collective-permute-start | bytes 589832 | tf_op jit(solution)/shard_map/ppermute | solution.py:219
  80.8 7.1 %collective-permute-start.16 = (bf16[16,1536]{1,0:T(8,128)(2,1)S(1)}, bf16[16,1536]{1,0:T(8,128)(2,1)S(1)}, u32[]{:S(2)}, u32[]{:S(2)}) collective-permute-start(bf16[16,1536]{1,0:T(8,128)(2,1)S(1)} %get-tuple-element.13), channel_id=1, source_target_pairs={{0,12},{4,0},{8,4},{12,8},{1,13},{5,1},{9,5},{13,9},{2,14},{6,2},{... | collective-permute-start | bytes 147464 | tf_op jit(solution)/shard_map/ppermute | solution.py:214
  82.8 5.7 %collective-permute-start.17 = (bf16[16,1536]{1,0:T(8,128)(2,1)S(1)}, bf16[16,1536]{1,0:T(8,128)(2,1)S(1)}, u32[]{:S(2)}, u32[]{:S(2)}) collective-permute-start(bf16[16,1536]{1,0:T(8,128)(2,1)S(1)} %get-tuple-element.15), channel_id=1, source_target_pairs={{0,8},{4,12},{8,0},{12,4},{1,9},{5,13},{9,1},{13,5},{2,10},{6,14},... | collective-permute-start | bytes 147464 | tf_op jit(solution)/shard_map/ppermute | solution.py:214
  82.8 6.3 %collective-permute-start.18 = (bf16[16,1536]{1,0:T(8,128)(2,1)S(1)}, bf16[16,1536]{1,0:T(8,128)(2,1)S(1)}, u32[]{:S(2)}, u32[]{:S(2)}) collective-permute-start(bf16[16,1536]{1,0:T(8,128)(2,1)S(1)} %get-tuple-element.14), channel_id=1, source_target_pairs={{0,4},{4,8},{8,12},{12,0},{1,5},{5,9},{9,13},{13,1},{2,6},{6,10},{... | collective-permute-start | bytes 147464 | tf_op jit(solution)/shard_map/ppermute | solution.py:214
  84.6 4.8 %collective-permute-start.21 = (bf16[16,1536]{1,0:T(8,128)(2,1)S(1)}, bf16[16,1536]{1,0:T(8,128)(2,1)S(1)}, u32[]{:S(2)}, u32[]{:S(2)}) collective-permute-start(bf16[16,1536]{1,0:T(8,128)(2,1)S(1)} %get-tuple-element.16), channel_id=1, source_target_pairs={{0,12},{4,0},{8,4},{12,8},{1,13},{5,1},{9,5},{13,9},{2,14},{6,2},{... | collective-permute-start | bytes 147464 | tf_op jit(solution)/shard_map/ppermute | solution.py:214
  86.8 5.5 %collective-permute-start.22 = (bf16[16,1536]{1,0:T(8,128)(2,1)S(1)}, bf16[16,1536]{1,0:T(8,128)(2,1)S(1)}, u32[]{:S(2)}, u32[]{:S(2)}) collective-permute-start(bf16[16,1536]{1,0:T(8,128)(2,1)S(1)} %get-tuple-element.18), channel_id=1, source_target_pairs={{0,8},{4,12},{8,0},{12,4},{1,9},{5,13},{9,1},{13,5},{2,10},{6,14},... | collective-permute-start | bytes 147464 | tf_op jit(solution)/shard_map/ppermute | solution.py:214
  87.9 5.9 %collective-permute-start.23 = (bf16[16,1536]{1,0:T(8,128)(2,1)S(1)}, bf16[16,1536]{1,0:T(8,128)(2,1)S(1)}, u32[]{:S(2)}, u32[]{:S(2)}) collective-permute-start(bf16[16,1536]{1,0:T(8,128)(2,1)S(1)} %get-tuple-element.17), channel_id=1, source_target_pairs={{0,4},{4,8},{8,12},{12,0},{1,5},{5,9},{9,13},{13,1},{2,6},{6,10},{... | collective-permute-start | bytes 147464 | tf_op jit(solution)/shard_map/ppermute | solution.py:214

commit v2 on v0

--- a/solution.py
+++ b/solution.py
@@ -3,6 +3,8 @@
 import jax
 import jax.numpy as jnp
 from jax import lax
+from jax.experimental import pallas as pl
+from jax.experimental.pallas import tpu as pltpu
 from jax.sharding import PartitionSpec as P
 
 
@@ -30,7 +32,7 @@
     return (target, source, filled)
 
 
-def local(tokens_in, out_grad, expert_ids, gate_probs, w_in, w_out):
+def routed(tokens_in, out_grad, expert_ids, gate_probs, w_in, w_out):
     experts = lax.axis_size("expert")
     shards = lax.axis_size("tensor")
     local_rows = tokens_in.shape[0]
@@ -77,6 +79,384 @@
     return jnp.sum(picked, axis=1).astype(jnp.bfloat16)
 
 
+CORES = 2
+EXPERTS = 4
+NEAR, FAR = 1, (2, 3)
+LANES = 128
+NT = (((1,), (1,)), ((), ()))
+VMEM_LIMIT = 24 * 2**20
+NO_COST = pl.CostEstimate(flops=0, bytes_accessed=0, transcendentals=0)
+
+
+def in_vmem(array):
+    return pltpu.with_memory_space_constraint(array, pltpu.VMEM)
+
+
+def whole_block():
+    return pl.BlockSpec(memory_space=pltpu.VMEM)
+
+
+def after(array, *earlier):
+    return lax.optimization_barrier((array, *earlier))[0]
+
+
+def assemble(pieces, rows_ref):
+    start = 0
+    for piece in pieces:
+        rows_ref[pl.ds(start, piece.shape[0]), :] = piece[:, : rows_ref.shape[1]]
+        start += piece.shape[0]
+
+
+def small_kernel(kernel, out_shape, operands):
+    return pl.pallas_call(
+        kernel,
+        out_shape=out_shape,
+        in_specs=[whole_block()] * len(operands),
+        out_specs=jax.tree.map(lambda _: whole_block(), out_shape),
+        compiler_params=pltpu.CompilerParams(vmem_limit_bytes=VMEM_LIMIT),
+        cost_estimate=NO_COST,
+    )(*operands)
+
+
+def stacked(*pieces, width=None, offsets=None):
+    width = width or pieces[0].shape[1]
+    offsets = offsets or [0] * len(pieces)
+    rows = sum(piece.shape[0] for piece in pieces)
+
+    def kernel(*refs):
+        out_ref = refs[-1]
+        start = 0
+        for piece, offset in zip(refs, offsets):
+            out_ref[pl.ds(start, piece.shape[0]), :] = piece[:, offset : offset + width]
+            start += piece.shape[0]
+
+    return small_kernel(kernel, jax.ShapeDtypeStruct((rows, width), jnp.bfloat16), pieces)
+
+
+def added(terms, sizes):
+    width = terms[0].shape[1]
+
+    def kernel(*refs):
+        term_refs, out_refs = refs[: len(terms)], refs[len(terms) :]
+        start = 0
+        for out_ref in out_refs:
+            rows = pl.ds(start, out_ref.shape[0])
+            total = term_refs[0][rows, :].astype(jnp.float32)
+            for term_ref in term_refs[1:]:
+                total += term_ref[rows, :].astype(jnp.float32)
+            out_ref[...] = total.astype(jnp.bfloat16)
+            start += out_ref.shape[0]
+
+    return small_kernel(
+        kernel, [jax.ShapeDtypeStruct((size, width), jnp.bfloat16) for size in sizes], terms
+    )
+
+
+def added_beside(chunks):
+    rows = chunks[0][0].shape[0]
+    widths = [chunk[0].shape[1] for chunk in chunks]
+    terms = [term for chunk in chunks for term in chunk]
+
+    def kernel(*refs):
+        *term_refs, out_ref = refs
+        start = 0
+        for chunk, width in zip(chunks, widths):
+            group, term_refs = term_refs[: len(chunk)], term_refs[len(chunk) :]
+            total = group[0][...].astype(jnp.float32)
+            for term_ref in group[1:]:
+                total += term_ref[...].astype(jnp.float32)
+            out_ref[:, start : start + width] = total.astype(jnp.bfloat16)
+            start += width
+
+    return small_kernel(kernel, jax.ShapeDtypeStruct((rows, sum(widths)), jnp.bfloat16), terms)
+
+
+def in_hbm(array):
+    return pltpu.with_memory_space_constraint(array, pltpu.HBM)
+
+
+def hbm_block():
+    return pl.BlockSpec(memory_space=pltpu.HBM)
+
+
+def with_gates(tokens, grads, expert_ids, gate_probs):
+    rows, features = grads.shape
+
+    def kernel(tokens_ref, grads_ref, ids_ref, probs_ref, out_ref, both_ref, ids, probs, sems):
+        copies = [
+            pltpu.make_async_copy(source, target, sems.at[place])
+            for place, (source, target) in enumerate(
+                (
+                    (ids_ref, ids),
+                    (probs_ref, probs),
+                    (tokens_ref, both_ref.at[:, pl.ds(0, features)]),
+                    (grads_ref, both_ref.at[:, pl.ds(features, features)]),
+                    (grads_ref, out_ref.at[:, pl.ds(0, features)]),
+                )
+            )
+        ]
+        for copy in copies:
+            copy.start()
+        copies[0].wait()
+        copies[1].wait()
+        lane = lax.broadcasted_iota(jnp.int32, (rows, LANES), 1)
+        here = lax.broadcasted_iota(jnp.int32, (rows, rows), 0) == lax.broadcasted_iota(
+            jnp.int32, (rows, rows), 1
+        )
+        upright = lambda row: jnp.sum(jnp.where(here, row, 0.0), axis=1, keepdims=True)
+        gates = jnp.zeros((rows, LANES), jnp.float32)
+        for k in range(ids.shape[0]):
+            named = upright(ids[k : k + 1, :].astype(jnp.float32)).astype(jnp.int32)
+            prob = upright(probs[k : k + 1, :].astype(jnp.float32))
+            gates += jnp.where(lane == named, prob, 0.0)
+        out_ref[:, features:] = gates.astype(jnp.bfloat16)
+        both_ref[:, 2 * features :] = gates.astype(jnp.bfloat16)
+        for copy in copies[2:]:
+            copy.wait()
+
+    return pl.pallas_call(
+        kernel,
+        out_shape=[
+            jax.ShapeDtypeStruct((rows, features + LANES), jnp.bfloat16),
+            jax.ShapeDtypeStruct((rows, 2 * features + LANES), jnp.bfloat16),
+        ],
+        in_specs=[hbm_block()] * 4,
+        out_specs=[whole_block()] * 2,
+        scratch_shapes=[
+            pltpu.VMEM(expert_ids.shape[::-1], expert_ids.dtype),
+            pltpu.VMEM(gate_probs.shape[::-1], gate_probs.dtype),
+            pltpu.SemaphoreType.DMA((5,)),
+        ],
+        compiler_params=pltpu.CompilerParams(vmem_limit_bytes=VMEM_LIMIT),
+        cost_estimate=NO_COST,
+    )(in_hbm(tokens), in_hbm(grads), in_hbm(expert_ids.T), in_hbm(gate_probs.T))
+
+
+def streamed(source_ref, target_ref, sems, first, parts, axis=0):
+    size = target_ref.shape[axis] // parts
+    copies = []
+    for part in range(parts):
+        here, there = pl.ds(first + part * size, size), pl.ds(part * size, size)
+        if axis == 0:
+            ends = source_ref.at[here], target_ref.at[there]
+        else:
+            ends = source_ref.at[:, here], target_ref.at[:, there]
+        copies.append(pltpu.make_async_copy(*ends, sems.at[part]))
+        copies[-1].start()
+    return copies
+
+
+def prefetched(weight, rows, parts=2):
+    def kernel(weight_ref, out_ref, sems):
+        for copy in streamed(weight_ref, out_ref, sems, 0, parts):
+            copy.wait()
+
+    return pl.pallas_call(
+        kernel,
+        out_shape=pltpu.VMEM((rows, weight.shape[1]), weight.dtype),
+        in_specs=[hbm_block()],
+        out_specs=whole_block(),
+        scratch_shapes=[pltpu.SemaphoreType.DMA((parts,))],
+        compiler_params=pltpu.CompilerParams(vmem_limit_bytes=VMEM_LIMIT),
+        cost_estimate=NO_COST,
+    )(in_hbm(weight))
+
+
+def slope_rows(pieces, weight, tile=1024):
+    rows = sum(piece.shape[0] for piece in pieces)
+    features, width = weight.shape
+
+    def kernel(*refs):
+        *piece_refs, weight_ref, out_ref, rows_ref = refs
+        assemble(piece_refs, rows_ref)
+        for start in range(0, width, tile):
+            cols = pl.ds(start, tile)
+            preact = jnp.dot(
+                rows_ref[...], weight_ref[:, cols], preferred_element_type=jnp.float32
+            )
+            out_ref[:, cols] = gelu_slope(preact)
+
+    return pl.pallas_call(
+        kernel,
+        out_shape=jax.ShapeDtypeStruct((rows, width), jnp.float32),
+        in_specs=[whole_block()] * (len(pieces) + 1),
+        out_specs=whole_block(),
+        scratch_shapes=[pltpu.VMEM((rows, features), jnp.bfloat16)],
+        compiler_params=pltpu.CompilerParams(vmem_limit_bytes=VMEM_LIMIT),
+        cost_estimate=NO_COST,
+    )(*pieces, in_vmem(weight))
+
+
+def scaled_rows(pieces, head, weight, slope, back, count, parts=2):
+    rows, width = slope.shape
+    features = weight.shape[1]
+    first = head.shape[0]
+
+    def kernel(expert_ref, *refs):
+        *piece_refs, head_ref, weight_ref, slope_ref, back_ref = refs[: len(pieces) + 4]
+        out_ref, kept_ref, sent_ref, rest_ref = refs[len(pieces) + 4 : len(pieces) + 8]
+        rows_ref, gate_ref, held_ref, held_back_ref, sems, back_sems, rest_sems = refs[
+            len(pieces) + 8 :
+        ]
+        copies = streamed(weight_ref, held_ref, sems, first, parts)
+        assemble(piece_refs, rows_ref)
+        start = 0
+        for piece in piece_refs:
+            gates = piece[:, features:].astype(jnp.float32)
+            lane = lax.broadcasted_iota(jnp.int32, gates.shape, 1)
+            gate_ref[pl.ds(start, piece.shape[0]), :] = jnp.sum(
+                jnp.where(lane == expert_ref[0], gates, 0.0), axis=1, keepdims=True
+            )
+            start += piece.shape[0]
+
+        def scale(block, cols):
+            hidden_grad = lax.dot_general(
+                rows_ref[...], block, NT, preferred_element_type=jnp.float32
+            )
+            out_ref[:, cols] = (gate_ref[...] * hidden_grad * slope_ref[:, cols]).astype(
+                jnp.bfloat16
+            )
+
+        size = (width - first) // parts
+        for start in range(0, first, size):
+            scale(head_ref[pl.ds(start, size), :], pl.ds(start, size))
+        back_copies = streamed(back_ref, held_back_ref, back_sems, 0, parts)
+        for part, copy in enumerate(copies):
+            copy.wait()
+            scale(held_ref[pl.ds(part * size, size), :], pl.ds(first + part * size, size))
+        rest_copies = streamed(back_ref, rest_ref, rest_sems, count, 1)
+        partial_product(out_ref, held_back_ref, back_copies, (kept_ref, sent_ref))
+        for copy in rest_copies:
+            copy.wait()
+
+    expert = lax.axis_index("expert").astype(jnp.int32).reshape(1)
+    half = jax.ShapeDtypeStruct((rows // CORES, count), jnp.bfloat16)
+    return pl.pallas_call(
+        kernel,
+        out_shape=[
+            jax.ShapeDtypeStruct((rows, width), jnp.bfloat16),
+            half,
+            half,
+            pltpu.VMEM((features - count, width), back.dtype),
+        ],
+        in_specs=[pl.BlockSpec(memory_space=pltpu.SMEM)]
+        + [whole_block()] * (len(pieces) + 1)
+        + [hbm_block(), whole_block(), hbm_block()],
+        out_specs=[whole_block()] * 4,
+        scratch_shapes=[
+            pltpu.VMEM((rows, features), jnp.bfloat16),
+            pltpu.VMEM((rows, 1), jnp.float32),
+            pltpu.VMEM((width - first, features), weight.dtype),
+            pltpu.VMEM((count, width), back.dtype),
+            pltpu.SemaphoreType.DMA((parts,)),
+            pltpu.SemaphoreType.DMA((parts,)),
+            pltpu.SemaphoreType.DMA((1,)),
+        ],
+        compiler_params=pltpu.CompilerParams(vmem_limit_bytes=VMEM_LIMIT),
+        cost_estimate=NO_COST,
+    )(expert, *pieces, in_vmem(head), in_hbm(weight), slope, in_hbm(back))
+
+
+def partial_product(scaled_ref, weight_ref, copies, out_refs):
+    half = scaled_ref.shape[0] // len(out_refs)
+    tile = weight_ref.shape[0] // len(copies)
+    for step, copy in enumerate(copies):
+        cols = pl.ds(step * tile, tile)
+        if copy is not None:
+            copy.wait()
+        product = lax.dot_general(
+            scaled_ref[...], weight_ref[cols, :], NT, preferred_element_type=jnp.float32
+        ).astype(jnp.bfloat16)
+        for place, out_ref in enumerate(out_refs):
+            out_ref[:, cols] = product[place * half : (place + 1) * half]
+
+
+def partial_rows(scaled, weight):
+    rows, count = scaled.shape[0], weight.shape[0]
+
+    def kernel(scaled_ref, weight_ref, kept_ref, sent_ref):
+        partial_product(scaled_ref, weight_ref, [None], (kept_ref, sent_ref))
+
+    half = jax.ShapeDtypeStruct((rows // CORES, count), jnp.bfloat16)
+    return pl.pallas_call(
+        kernel,
+        out_shape=[half, half],
+        in_specs=[whole_block()] * 2,
+        out_specs=[whole_block()] * 2,
+        compiler_params=pltpu.CompilerParams(vmem_limit_bytes=VMEM_LIMIT),
+        cost_estimate=NO_COST,
+    )(scaled, in_vmem(weight))
+
+
+def beside(array, axis, step):
+    size = lax.axis_size(axis)
+    return lax.ppermute(array, axis, [(i, i ^ step) for i in range(size)])
+
+
+def scatter_rows(kept, sent, rows):
+    kept, sent = added([kept, beside(sent, "tensor", 1)], [rows * EXPERTS] * 2)
+    kept, *sent = added([kept, beside(sent, "tensor", CORES)], [rows] * EXPERTS)
+    return [kept] + [beside(block, "expert", step) for step, block in zip((*FAR, NEAR), sent)]
+
+
+def dense(tokens_in, out_grad, expert_ids, gate_probs, w_in, w_out):
+    local_rows, features = tokens_in.shape
+    together = lax.optimization_barrier
+    w_in, w_out = w_in[0], w_out[0]
+
+    grads, both = with_gates(tokens_in, out_grad, expert_ids, gate_probs)
+    *far_tokens, near, across, grads, w_in = together(
+        (
+            *[beside(tokens_in, "expert", step) for step in FAR],
+            beside(both, "expert", NEAR),
+            beside(both, "tensor", CORES),
+            grads,
+            w_in,
+        )
+    )
+    far_tokens = stacked(*far_tokens)
+    far_tokens, far_tokens_across, near_across, *far_grads, held_in = together(
+        (
+            far_tokens,
+            beside(far_tokens, "tensor", CORES),
+            beside(near, "tensor", CORES),
+            *[beside(grads, "expert", step) for step in FAR],
+            prefetched(w_in, features),
+        )
+    )
+    token_half = stacked(
+        both, far_tokens, near, across, far_tokens_across, near_across, width=features
+    )
+    slope = slope_rows([token_half, beside(token_half, "tensor", 1)], held_in)
+    far_grads = stacked(*far_grads)
+    far_grads_across, slope = together((beside(far_grads, "tensor", CORES), slope))
+    grad_half = stacked(
+        both,
+        far_grads,
+        near,
+        across,
+        far_grads_across,
+        near_across,
+        width=grads.shape[1],
+        offsets=[features, 0, features, features, 0, features],
+    )
+    grad_half, w_out = together((grad_half, w_out))
+    grad_other, head = together(
+        (beside(grad_half, "tensor", 1), prefetched(w_out, w_out.shape[0] // 2))
+    )
+    scaled, *halves, rest = scaled_rows(
+        [grad_half, grad_other], head, w_out, slope, w_in, features // 2
+    )
+    chunks = [halves, partial_rows(scaled, rest)]
+    return added_beside([scatter_rows(*halves, local_rows) for halves in chunks])
+
+
+def local(*args):
+    if lax.axis_size("expert") == EXPERTS and lax.axis_size("tensor") == 2 * CORES:
+        return dense(*args)
+    return routed(*args)
+
+
 def solution(mesh):
     return jax.shard_map(
         local,

time: 204 us -> 70.7 us (0.35)
  waiting for transfers between devices: 84.1 us -> 24.6 us
  blocking collectives: 59 us -> 0 us
  Pallas kernels: 0 us -> 24.5 us
  matrix products: 23.6 us -> 0 us
  between operations: 13.5 us -> 0.13 us
  starting transfers between devices: 13.3 us -> 21.2 us
  local copies, waits for them, and re-layouts: 6.41 us -> 0 us
  other arithmetic: 3.28 us -> 0 us
    all_to_all x3 -> x0, waiting for transfers between devices: 47.8 us -> none  [the longest x1 28.1 us: local(): lax.all_to_all(outgoing, 'expert', split_axis=0, concat_axis=0, tiled=True)]
    psum x1 -> x0, waiting for transfers between devices: 36.2 us -> none  [local(): summed = lax.psum(partial_rows, 'tensor').astype(jnp.float32)]
    all_to_all x1 -> x0, blocking collectives: 33.9 us -> none  [local(): lax.all_to_all(send_in, 'expert', split_axis=0, concat_axis=0, tiled=True)]
    all_gather x4 -> x0, blocking collectives: 25.1 us -> none  [the longest x1 6.78 us: local(): lax.all_gather(out_grad, 'tensor', axis=0, tiled=True)]
    ppermute x0 -> x21, waiting for transfers between devices: none -> 24.6 us  [beside(): return lax.ppermute(array, axis, [(i, i ^ step) for i in range(size)])]
    pallas_call x0 -> x15, Pallas kernels: none -> 24.5 us  [the longest x1 8.57 us: scaled_rows(): pl.pallas_call(kernel, out_shape=[jax.ShapeDtypeStruct((rows, width), jnp...]
    dot_general x2 -> x0, matrix products: 23.6 us -> none  [the longest x1 15.2 us: local(): jnp.einsum('rh,dh->rd', scaled, w_in[0], preferred_element_type=jnp.float32)]
    ppermute x0 -> x21, starting transfers between devices: none -> 21.2 us  [beside(): return lax.ppermute(array, axis, [(i, i ^ step) for i in range(size)])]
  transfers between devices with their start and end apart: 4 -> 21, of which waited for: 3 -> 12; matrix products, arithmetic and copies ran while one was open for 6% -> 0% of each run, Pallas kernels for 0% -> 20%
where the time goes in v2:
time: 70.7 us; the launch traced here: 70.5 us
  waiting for transfers between devices  24.6 us (35%)
  Pallas kernels  24.5 us (35%)
  starting transfers between devices  21.2 us (30%)
    ppermute x21, waiting for transfers between devices, beside(): return lax.ppermute(array, axis, [(i, i ^ step) for i in range(size)])  24.6 us
    ppermute x21, starting transfers between devices, beside(): return lax.ppermute(array, axis, [(i, i ^ step) for i in range(size)])  21.2 us
    pallas_call x1, Pallas kernels, scaled_rows(): pl.pallas_call(kernel, out_shape=[jax.ShapeDtypeStruct((rows, width), jnp...  8.57 us
    pallas_call x2, Pallas kernels, prefetched(): pl.pallas_call(kernel, out_shape=pltpu.VMEM((rows, weight.shape[1]), weig...  7.49 us
    pallas_call x1, Pallas kernels, slope_rows(): pl.pallas_call(kernel, out_shape=jax.ShapeDtypeStruct((rows, width), jnp....  4.49 us
    pallas_call x1, Pallas kernels, partial_rows(): pl.pallas_call(kernel, out_shape=[half, half], in_specs=[whole_block()] *...  1.82 us
  transfers between devices with their start and end apart: 21, of which 12 were waited for; matrix products, arithmetic and copies ran while one was open for 0% of the time, Pallas kernels for 20%

profile of v2, /device:TPU:0, one launch (start us, length us, event | category | flops | bytes accessed | tf_op | source)
XLA Modules:
  0.0 70.5 jit_solution(9951495836285003602)
XLA Ops:
  0.0 1.1 %shard_map.64 = (bf16[16,3200]{1,0:T(8,128)(2,1)S(1)}, bf16[16,6272]{1,0:T(8,128)(2,1)S(1)}) custom-call(bf16[16,3072]{1,0:T(8,128)(2,1)} %tokens_ref.1, bf16[16,3072]{1,0:T(8,128)(2,1)} %grads_ref.1, s32[2,16]{1,0:T(2,128)} %bitcast.9, bf16[2,16]{1,0:T(2,128)(2,1)} %bitcast.10), custom_call_target="tpu_custom_call" | custom-call | tf_op jit(solution)/shard_map/pallas_call | solution.py:217
  1.1 3.0 %collective-permute-start.3 = (bf16[16,6272]{1,0:T(8,128)(2,1)S(1)}, bf16[16,6272]{1,0:T(8,128)(2,1)S(1)}, u32[]{:S(2)}, u32[]{:S(2)}) collective-permute-start(bf16[16,6272]{1,0:T(8,128)(2,1)S(1)} %get-tuple-element.43.refs_0_), channel_id=1, source_target_pairs={{0,2},{1,3},{2,0},{3,1},{4,6},{5,7},{6,4},{7,5},{8,10},{9,11},{10,... | collective-permute-start | bytes 602120 | tf_op jit(solution)/shard_map/ppermute | solution.py:393
  4.1 1.6 %collective-permute-start.2 = (bf16[16,6272]{1,0:T(8,128)(2,1)S(1)}, bf16[16,6272]{1,0:T(8,128)(2,1)S(1)}, u32[]{:S(2)}, u32[]{:S(2)}) collective-permute-start(bf16[16,6272]{1,0:T(8,128)(2,1)S(1)} %get-tuple-element.43.refs_0_), channel_id=1, source_target_pairs={{0,4},{4,0},{8,12},{12,8},{1,5},{5,1},{9,13},{13,9},{2,6},{6,2},{1... | collective-permute-start | bytes 602120 | tf_op jit(solution)/shard_map/ppermute | solution.py:393
  5.7 2.5 %collective-permute-start.1 = (bf16[16,3072]{1,0:T(8,128)(2,1)}, bf16[16,3072]{1,0:T(8,128)(2,1)S(1)}, u32[]{:S(2)}, u32[]{:S(2)}) collective-permute-start(bf16[16,3072]{1,0:T(8,128)(2,1)} %tokens_ref.1), channel_id=1, source_target_pairs={{0,12},{4,8},{8,4},{12,0},{1,13},{5,9},{9,5},{13,1},{2,14},{6,10},... | collective-permute-start | bytes 294920 | tf_op jit(solution)/shard_map/ppermute | solution.py:393
  8.1 0.1 collective-permute-start
  8.2 7.6 %collective-permute-done.1.refs_1_ = bf16[16,3072]{1,0:T(8,128)(2,1)S(1)} collective-permute-done((bf16[16,3072]{1,0:T(8,128)(2,1)}, bf16[16,3072]{1,0:T(8,128)(2,1)S(1)}, u32[]{:S(2)}, u32[]{:S(2)}) %collective-permute-start.1) | collective-permute-done | bytes 98336 | tf_op jit(solution)/shard_map/ppermute | solution.py:393
  15.8 1.6 %collective-permute-done.refs_0_ = bf16[16,3072]{1,0:T(8,128)(2,1)S(1)} collective-permute-done((bf16[16,3072]{1,0:T(8,128)(2,1)}, bf16[16,3072]{1,0:T(8,128)(2,1)S(1)}, u32[]{:S(2)}, u32[]{:S(2)}) %collective-permute-start) | collective-permute-done | bytes 98336 | tf_op jit(solution)/shard_map/ppermute | solution.py:393
  17.4 0.0 collective-permute-done.3.refs_3_
  17.4 0.0 collective-permute-done.2.refs_2_
  17.4 0.5 collective-permute-start.5
  17.9 1.6 %collective-permute-start.4 = (bf16[32,3072]{1,0:T(8,128)(2,1)S(1)}, bf16[32,3072]{1,0:T(8,128)(2,1)S(1)}, u32[]{:S(2)}, u32[]{:S(2)}) collective-permute-start(bf16[32,3072]{1,0:T(8,128)(2,1)S(1)} %shard_map.65.refs_1_), channel_id=1, source_target_pairs={{0,2},{1,3},{2,0},{3,1},{4,6},{5,7},{6,4},{7,5},{8,10},{9,11},{10,... | collective-permute-start | bytes 589832 | tf_op jit(solution)/shard_map/ppermute | solution.py:393
  19.5 2.3 %collective-permute-start.7 = (bf16[16,3200]{1,0:T(8,128)(2,1)S(1)}, bf16[16,3200]{1,0:T(8,128)(2,1)S(1)}, u32[]{:S(2)}, u32[]{:S(2)}) collective-permute-start(bf16[16,3200]{1,0:T(8,128)(2,1)S(1)} %get-tuple-element.48), channel_id=1, source_target_pairs={{0,12},{4,8},{8,4},{12,0},{1,13},{5,9},{9,5},{13,1},{2,14},{6,10},... | collective-permute-start | bytes 307208 | tf_op jit(solution)/shard_map/ppermute | solution.py:393
  21.8 0.0 collective-permute-start.6
  21.8 4.6 %shard_map.66.refs_2_ = bf16[3072,2048]{1,0:T(8,128)(2,1)S(1)} custom-call(bf16[3072,2048]{1,0:T(8,128)(2,1)} %bitcast.7), custom_call_target="tpu_custom_call" | custom-call | tf_op jit(solution)/shard_map/pallas_call | solution.py:254
  26.4 1.7 %collective-permute-done.6.refs_0_ = bf16[16,3200]{1,0:T(8,128)(2,1)S(1)} collective-permute-done((bf16[16,3200]{1,0:T(8,128)(2,1)S(1)}, bf16[16,3200]{1,0:T(8,128)(2,1)S(1)}, u32[]{:S(2)}, u32[]{:S(2)}) %collective-permute-start.6) | collective-permute-done | bytes 102432 | tf_op jit(solution)/shard_map/ppermute | solution.py:393
  28.1 0.1 shard_map.68.refs_0_
  28.2 0.1 collective-permute-start.9
  28.3 0.6 collective-permute-start.8
  28.9 1.6 %collective-permute-done.9.refs_1_ = bf16[128,3072]{1,0:T(8,128)(2,1)S(1)} collective-permute-done((bf16[128,3072]{1,0:T(8,128)(2,1)S(1)}, bf16[128,3072]{1,0:T(8,128)(2,1)S(1)}, u32[]{:S(2)}, u32[]{:S(2)}) %collective-permute-start.9) | collective-permute-done | bytes 786464 | tf_op jit(solution)/shard_map/ppermute | solution.py:393
  30.6 4.5 %shard_map.69.refs_4_ = f32[256,2048]{1,0:T(8,128)S(1)} custom-call(bf16[128,3072]{1,0:T(8,128)(2,1)S(1)} %shard_map.68.refs_0_, bf16[128,3072]{1,0:T(8,128)(2,1)S(1)} %collective-permute-done.9.refs_1_, bf16[3072,2048]{1,0:T(8,128)(2,1)S(1)} %shard_map.66.refs_2_), custom_call_target="tpu_custom_call" | custom-call | tf_op jit(solution)/shard_map/pallas_call | solution.py:279
  35.0 0.8 %collective-permute-done.8.refs_4_ = bf16[32,3200]{1,0:T(8,128)(2,1)S(1)} collective-permute-done((bf16[32,3200]{1,0:T(8,128)(2,1)S(1)}, bf16[32,3200]{1,0:T(8,128)(2,1)S(1)}, u32[]{:S(2)}, u32[]{:S(2)}) %collective-permute-start.8) | collective-permute-done | bytes 204832 | tf_op jit(solution)/shard_map/ppermute | solution.py:393
  35.8 0.1 shard_map.70.refs_0_
  35.9 0.1 collective-permute-start.10
  36.0 2.9 %shard_map.71.refs_2_ = bf16[1024,3072]{1,0:T(8,128)(2,1)S(1)} custom-call(bf16[2048,3072]{1,0:T(8,128)(2,1)} %bitcast.5), custom_call_target="tpu_custom_call" | custom-call | tf_op jit(solution)/shard_map/pallas_call | solution.py:254
  38.9 8.6 %shard_map.72 = (bf16[256,2048]{1,0:T(8,128)(2,1)S(1)}, bf16[128,1536]{1,0:T(8,128)(2,1)S(1)}, bf16[128,1536]{1,0:T(8,128)(2,1)S(1)}, bf16[1536,2048]{1,0:T(8,128)(2,1)S(1)}) custom-call(s32[1]{0:T(128)} %bitcast.expert_ref, bf16[128,3200]{1,0:T(8,128)(2,1)S(1)} %shard_map.70.refs_0_, bf16[128,3200]{1,0:T(8,128)(2,1)} %collective-permute-done.10.refs_1_, ...), custom_call_target="tpu_custom_call" | custom-call | tf_op jit(solution)/shard_map/pallas_call | solution.py:334
  47.4 0.6 collective-permute-start.11
  48.0 1.8 %shard_map.75 = (bf16[128,1536]{1,0:T(8,128)(2,1)S(1)}, bf16[128,1536]{1,0:T(8,128)(2,1)S(1)}) custom-call(bf16[256,2048]{1,0:T(8,128)(2,1)S(1)} %get-tuple-element.71.scaled_ref, bf16[1536,2048]{1,0:T(8,128)(2,1)S(1)} %get-tuple-element.72.weight_ref), custom_call_target="tpu_custom_call" | custom-call | tf_op jit(solution)/shard_map/pallas_call | solution.py:381
  49.8 0.1 collective-permute-start.16
  49.9 0.0 collective-permute-done.11.refs_1_
  49.9 0.1 shard_map.73
  50.0 0.6 collective-permute-start.12
  50.6 1.0 %collective-permute-done.16.refs_1_ = bf16[128,1536]{1,0:T(8,128)(2,1)S(1)} collective-permute-done((bf16[128,1536]{1,0:T(8,128)(2,1)S(1)}, bf16[128,1536]{1,0:T(8,128)(2,1)S(1)}, u32[]{:S(2)}, u32[]{:S(2)}) %collective-permute-start.16) | collective-permute-done | bytes 393248 | tf_op jit(solution)/shard_map/ppermute | solution.py:393
  51.6 0.1 shard_map.76
  51.7 0.6 collective-permute-start.17
  52.3 5.5 %collective-permute-done.12.refs_1_ = bf16[64,1536]{1,0:T(8,128)(2,1)S(1)} collective-permute-done((bf16[64,1536]{1,0:T(8,128)(2,1)S(1)}, bf16[64,1536]{1,0:T(8,128)(2,1)S(1)}, u32[]{:S(2)}, u32[]{:S(2)}) %collective-permute-start.12) | collective-permute-done | bytes 196640 | tf_op jit(solution)/shard_map/ppermute | solution.py:393
  57.8 1.3 %collective-permute-start.13 = (bf16[16,1536]{1,0:T(8,128)(2,1)S(1)}, bf16[16,1536]{1,0:T(8,128)(2,1)S(1)}, u32[]{:S(2)}, u32[]{:S(2)}) collective-permute-start(bf16[16,1536]{1,0:T(8,128)(2,1)S(1)} %get-tuple-element.68), channel_id=1, source_target_pairs={{0,8},{4,12},{8,0},{12,4},{1,9},{5,13},{9,1},{13,5},{2,10},{6,14},... | collective-permute-start | bytes 147464 | tf_op jit(solution)/shard_map/ppermute | solution.py:393
  59.1 1.6 %collective-permute-start.14 = (bf16[16,1536]{1,0:T(8,128)(2,1)S(1)}, bf16[16,1536]{1,0:T(8,128)(2,1)S(1)}, u32[]{:S(2)}, u32[]{:S(2)}) collective-permute-start(bf16[16,1536]{1,0:T(8,128)(2,1)S(1)} %get-tuple-element.69), channel_id=1, source_target_pairs={{0,12},{4,8},{8,4},{12,0},{1,13},{5,9},{9,5},{13,1},{2,14},{6,10},... | collective-permute-start | bytes 147464 | tf_op jit(solution)/shard_map/ppermute | solution.py:393
  60.7 0.7 %collective-permute-start.15 = (bf16[16,1536]{1,0:T(8,128)(2,1)S(1)}, bf16[16,1536]{1,0:T(8,128)(2,1)S(1)}, u32[]{:S(2)}, u32[]{:S(2)}) collective-permute-start(bf16[16,1536]{1,0:T(8,128)(2,1)S(1)} %get-tuple-element.70), channel_id=1, source_target_pairs={{0,4},{4,0},{8,12},{12,8},{1,5},{5,1},{9,13},{13,9},{2,6},{6,2},{1... | collective-permute-start | bytes 147464 | tf_op jit(solution)/shard_map/ppermute | solution.py:393
  61.4 0.2 collective-permute-done.17.refs_1_
  61.7 2.0 %collective-permute-start.18 = (bf16[16,1536]{1,0:T(8,128)(2,1)S(1)}, bf16[16,1536]{1,0:T(8,128)(2,1)S(1)}, u32[]{:S(2)}, u32[]{:S(2)}) collective-permute-start(bf16[16,1536]{1,0:T(8,128)(2,1)S(1)} %get-tuple-element.78), channel_id=1, source_target_pairs={{0,8},{4,12},{8,0},{12,4},{1,9},{5,13},{9,1},{13,5},{2,10},{6,14},... | collective-permute-start | bytes 147464 | tf_op jit(solution)/shard_map/ppermute | solution.py:393
  63.6 1.6 %collective-permute-start.19 = (bf16[16,1536]{1,0:T(8,128)(2,1)S(1)}, bf16[16,1536]{1,0:T(8,128)(2,1)S(1)}, u32[]{:S(2)}, u32[]{:S(2)}) collective-permute-start(bf16[16,1536]{1,0:T(8,128)(2,1)S(1)} %get-tuple-element.79), channel_id=1, source_target_pairs={{0,12},{4,8},{8,4},{12,0},{1,13},{5,9},{9,5},{13,1},{2,14},{6,10},... | collective-permute-start | bytes 147464 | tf_op jit(solution)/shard_map/ppermute | solution.py:393
  65.2 0.0 collective-permute-start.20
  65.2 0.1 collective-permute-done.14.refs_2_
  65.3 0.0 collective-permute-done.15.refs_3_
  65.3 2.8 %collective-permute-done.18.refs_5_ = bf16[16,1536]{1,0:T(8,128)(2,1)S(1)} collective-permute-done((bf16[16,1536]{1,0:T(8,128)(2,1)S(1)}, bf16[16,1536]{1,0:T(8,128)(2,1)S(1)}, u32[]{:S(2)}, u32[]{:S(2)}) %collective-permute-start.18) | collective-permute-done | bytes 49184 | tf_op jit(solution)/shard_map/ppermute | solution.py:393
  68.2 1.5 %collective-permute-done.19.refs_6_ = bf16[16,1536]{1,0:T(8,128)(2,1)S(1)} collective-permute-done((bf16[16,1536]{1,0:T(8,128)(2,1)S(1)}, bf16[16,1536]{1,0:T(8,128)(2,1)S(1)}, u32[]{:S(2)}, u32[]{:S(2)}) %collective-permute-start.19) | collective-permute-done | bytes 49184 | tf_op jit(solution)/shard_map/ppermute | solution.py:393
  69.6 0.2 collective-permute-done.20.refs_7_
  69.8 0.7 shard_map.78
  (9 shorter events, 0.1 us)
Async XLA Ops:
  1.1 16.3 %collective-permute-start.3 = (bf16[16,6272]{1,0:T(8,128)(2,1)S(1)}, bf16[16,6272]{1,0:T(8,128)(2,1)S(1)}, u32[]{:S(2)}, u32[]{:S(2)}) collective-permute-start(bf16[16,6272]{1,0:T(8,128)(2,1)S(1)} %get-tuple-element.43.refs_0_), channel_id=1, source_target_pairs={{0,2},{1,3},{2,0},{3,1},{4,6},{5,7},{6,4},{7,5},{8,10},{9,11},{10,... | collective-permute-start | bytes 602120 | tf_op jit(solution)/shard_map/ppermute | solution.py:393
  4.1 13.3 %collective-permute-start.2 = (bf16[16,6272]{1,0:T(8,128)(2,1)S(1)}, bf16[16,6272]{1,0:T(8,128)(2,1)S(1)}, u32[]{:S(2)}, u32[]{:S(2)}) collective-permute-start(bf16[16,6272]{1,0:T(8,128)(2,1)S(1)} %get-tuple-element.43.refs_0_), channel_id=1, source_target_pairs={{0,4},{4,0},{8,12},{12,8},{1,5},{5,1},{9,13},{13,9},{2,6},{6,2},{1... | collective-permute-start | bytes 602120 | tf_op jit(solution)/shard_map/ppermute | solution.py:393
  5.7 10.2 %collective-permute-start.1 = (bf16[16,3072]{1,0:T(8,128)(2,1)}, bf16[16,3072]{1,0:T(8,128)(2,1)S(1)}, u32[]{:S(2)}, u32[]{:S(2)}) collective-permute-start(bf16[16,3072]{1,0:T(8,128)(2,1)} %tokens_ref.1), channel_id=1, source_target_pairs={{0,12},{4,8},{8,4},{12,0},{1,13},{5,9},{9,5},{13,1},{2,14},{6,10},... | collective-permute-start | bytes 294920 | tf_op jit(solution)/shard_map/ppermute | solution.py:393
  8.1 9.2 %collective-permute-start = (bf16[16,3072]{1,0:T(8,128)(2,1)}, bf16[16,3072]{1,0:T(8,128)(2,1)S(1)}, u32[]{:S(2)}, u32[]{:S(2)}) collective-permute-start(bf16[16,3072]{1,0:T(8,128)(2,1)} %tokens_ref.1), channel_id=1, source_target_pairs={{0,8},{4,12},{8,0},{12,4},{1,9},{5,13},{9,1},{13,5},{2,10},{6,14},... | collective-permute-start | bytes 294920 | tf_op jit(solution)/shard_map/ppermute | solution.py:393
  17.4 10.8 %collective-permute-start.5 = (bf16[16,6272]{1,0:T(8,128)(2,1)S(1)}, bf16[16,6272]{1,0:T(8,128)(2,1)S(1)}, u32[]{:S(2)}, u32[]{:S(2)}) collective-permute-start(bf16[16,6272]{1,0:T(8,128)(2,1)S(1)} %collective-permute-done.2.refs_2_), channel_id=1, source_target_pairs={{0,2},{1,3},{2,0},{3,1},{4,6},{5,7},{6,4},{7,5},{8,10},{9,11},{10,... | collective-permute-start | bytes 602120 | tf_op jit(solution)/shard_map/ppermute | solution.py:393
  17.9 10.2 %collective-permute-start.4 = (bf16[32,3072]{1,0:T(8,128)(2,1)S(1)}, bf16[32,3072]{1,0:T(8,128)(2,1)S(1)}, u32[]{:S(2)}, u32[]{:S(2)}) collective-permute-start(bf16[32,3072]{1,0:T(8,128)(2,1)S(1)} %shard_map.65.refs_1_), channel_id=1, source_target_pairs={{0,2},{1,3},{2,0},{3,1},{4,6},{5,7},{6,4},{7,5},{8,10},{9,11},{10,... | collective-permute-start | bytes 589832 | tf_op jit(solution)/shard_map/ppermute | solution.py:393
  19.5 6.9 %collective-permute-start.7 = (bf16[16,3200]{1,0:T(8,128)(2,1)S(1)}, bf16[16,3200]{1,0:T(8,128)(2,1)S(1)}, u32[]{:S(2)}, u32[]{:S(2)}) collective-permute-start(bf16[16,3200]{1,0:T(8,128)(2,1)S(1)} %get-tuple-element.48), channel_id=1, source_target_pairs={{0,12},{4,8},{8,4},{12,0},{1,13},{5,9},{9,5},{13,1},{2,14},{6,10},... | collective-permute-start | bytes 307208 | tf_op jit(solution)/shard_map/ppermute | solution.py:393
  21.8 6.4 %collective-permute-start.6 = (bf16[16,3200]{1,0:T(8,128)(2,1)S(1)}, bf16[16,3200]{1,0:T(8,128)(2,1)S(1)}, u32[]{:S(2)}, u32[]{:S(2)}) collective-permute-start(bf16[16,3200]{1,0:T(8,128)(2,1)S(1)} %get-tuple-element.48), channel_id=1, source_target_pairs={{0,8},{4,12},{8,0},{12,4},{1,9},{5,13},{9,1},{13,5},{2,10},{6,14},... | collective-permute-start | bytes 307208 | tf_op jit(solution)/shard_map/ppermute | solution.py:393
  28.2 2.4 %collective-permute-start.9 = (bf16[128,3072]{1,0:T(8,128)(2,1)S(1)}, bf16[128,3072]{1,0:T(8,128)(2,1)S(1)}, u32[]{:S(2)}, u32[]{:S(2)}) collective-permute-start(bf16[128,3072]{1,0:T(8,128)(2,1)S(1)} %shard_map.68.refs_0_), channel_id=1, source_target_pairs={{0,1},{1,0},{2,3},{3,2},{4,5},{5,4},{6,7},{7,6},{8,9},{9,8},{10,11... | collective-permute-start | bytes 2359304 | tf_op jit(solution)/shard_map/ppermute | solution.py:393
  28.3 7.5 %collective-permute-start.8 = (bf16[32,3200]{1,0:T(8,128)(2,1)S(1)}, bf16[32,3200]{1,0:T(8,128)(2,1)S(1)}, u32[]{:S(2)}, u32[]{:S(2)}) collective-permute-start(bf16[32,3200]{1,0:T(8,128)(2,1)S(1)} %shard_map.67.refs_1_), channel_id=1, source_target_pairs={{0,2},{1,3},{2,0},{3,1},{4,6},{5,7},{6,4},{7,5},{8,10},{9,11},{10,... | collective-permute-start | bytes 614408 | tf_op jit(solution)/shard_map/ppermute | solution.py:393
  35.9 3.0 %collective-permute-start.10 = (bf16[128,3200]{1,0:T(8,128)(2,1)S(1)}, bf16[128,3200]{1,0:T(8,128)(2,1)}, u32[]{:S(2)}, u32[]{:S(2)}) collective-permute-start(bf16[128,3200]{1,0:T(8,128)(2,1)S(1)} %shard_map.70.refs_0_), channel_id=1, source_target_pairs={{0,1},{1,0},{2,3},{3,2},{4,5},{5,4},{6,7},{7,6},{8,9},{9,8},{10,11... | collective-permute-start | bytes 2457608 | tf_op jit(solution)/shard_map/ppermute | solution.py:393
  47.4 2.5 %collective-permute-start.11 = (bf16[128,1536]{1,0:T(8,128)(2,1)S(1)}, bf16[128,1536]{1,0:T(8,128)(2,1)S(1)}, u32[]{:S(2)}, u32[]{:S(2)}) collective-permute-start(bf16[128,1536]{1,0:T(8,128)(2,1)S(1)} %get-tuple-element.64), channel_id=1, source_target_pairs={{0,1},{1,0},{2,3},{3,2},{4,5},{5,4},{6,7},{7,6},{8,9},{9,8},{10,11... | collective-permute-start | bytes 1179656 | tf_op jit(solution)/shard_map/ppermute | solution.py:393
  49.8 1.8 %collective-permute-start.16 = (bf16[128,1536]{1,0:T(8,128)(2,1)S(1)}, bf16[128,1536]{1,0:T(8,128)(2,1)S(1)}, u32[]{:S(2)}, u32[]{:S(2)}) collective-permute-start(bf16[128,1536]{1,0:T(8,128)(2,1)S(1)} %get-tuple-element.74), channel_id=1, source_target_pairs={{0,1},{1,0},{2,3},{3,2},{4,5},{5,4},{6,7},{7,6},{8,9},{9,8},{10,11... | collective-permute-start | bytes 1179656 | tf_op jit(solution)/shard_map/ppermute | solution.py:393
  50.0 7.8 %collective-permute-start.12 = (bf16[64,1536]{1,0:T(8,128)(2,1)S(1)}, bf16[64,1536]{1,0:T(8,128)(2,1)S(1)}, u32[]{:S(2)}, u32[]{:S(2)}) collective-permute-start(bf16[64,1536]{1,0:T(8,128)(2,1)S(1)} %get-tuple-element.66), channel_id=1, source_target_pairs={{0,2},{1,3},{2,0},{3,1},{4,6},{5,7},{6,4},{7,5},{8,10},{9,11},{10,... | collective-permute-start | bytes 589832 | tf_op jit(solution)/shard_map/ppermute | solution.py:393
  51.7 9.9 %collective-permute-start.17 = (bf16[64,1536]{1,0:T(8,128)(2,1)S(1)}, bf16[64,1536]{1,0:T(8,128)(2,1)S(1)}, u32[]{:S(2)}, u32[]{:S(2)}) collective-permute-start(bf16[64,1536]{1,0:T(8,128)(2,1)S(1)} %get-tuple-element.76), channel_id=1, source_target_pairs={{0,2},{1,3},{2,0},{3,1},{4,6},{5,7},{6,4},{7,5},{8,10},{9,11},{10,... | collective-permute-start | bytes 589832 | tf_op jit(solution)/shard_map/ppermute | solution.py:393
  57.8 7.4 %collective-permute-start.13 = (bf16[16,1536]{1,0:T(8,128)(2,1)S(1)}, bf16[16,1536]{1,0:T(8,128)(2,1)S(1)}, u32[]{:S(2)}, u32[]{:S(2)}) collective-permute-start(bf16[16,1536]{1,0:T(8,128)(2,1)S(1)} %get-tuple-element.68), channel_id=1, source_target_pairs={{0,8},{4,12},{8,0},{12,4},{1,9},{5,13},{9,1},{13,5},{2,10},{6,14},... | collective-permute-start | bytes 147464 | tf_op jit(solution)/shard_map/ppermute | solution.py:393
  59.1 6.2 %collective-permute-start.14 = (bf16[16,1536]{1,0:T(8,128)(2,1)S(1)}, bf16[16,1536]{1,0:T(8,128)(2,1)S(1)}, u32[]{:S(2)}, u32[]{:S(2)}) collective-permute-start(bf16[16,1536]{1,0:T(8,128)(2,1)S(1)} %get-tuple-element.69), channel_id=1, source_target_pairs={{0,12},{4,8},{8,4},{12,0},{1,13},{5,9},{9,5},{13,1},{2,14},{6,10},... | collective-permute-start | bytes 147464 | tf_op jit(solution)/shard_map/ppermute | solution.py:393
  60.7 4.7 %collective-permute-start.15 = (bf16[16,1536]{1,0:T(8,128)(2,1)S(1)}, bf16[16,1536]{1,0:T(8,128)(2,1)S(1)}, u32[]{:S(2)}, u32[]{:S(2)}) collective-permute-start(bf16[16,1536]{1,0:T(8,128)(2,1)S(1)} %get-tuple-element.70), channel_id=1, source_target_pairs={{0,4},{4,0},{8,12},{12,8},{1,5},{5,1},{9,13},{13,9},{2,6},{6,2},{1... | collective-permute-start | bytes 147464 | tf_op jit(solution)/shard_map/ppermute | solution.py:393
  61.7 6.5 %collective-permute-start.18 = (bf16[16,1536]{1,0:T(8,128)(2,1)S(1)}, bf16[16,1536]{1,0:T(8,128)(2,1)S(1)}, u32[]{:S(2)}, u32[]{:S(2)}) collective-permute-start(bf16[16,1536]{1,0:T(8,128)(2,1)S(1)} %get-tuple-element.78), channel_id=1, source_target_pairs={{0,8},{4,12},{8,0},{12,4},{1,9},{5,13},{9,1},{13,5},{2,10},{6,14},... | collective-permute-start | bytes 147464 | tf_op jit(solution)/shard_map/ppermute | solution.py:393
  63.6 6.0 %collective-permute-start.19 = (bf16[16,1536]{1,0:T(8,128)(2,1)S(1)}, bf16[16,1536]{1,0:T(8,128)(2,1)S(1)}, u32[]{:S(2)}, u32[]{:S(2)}) collective-permute-start(bf16[16,1536]{1,0:T(8,128)(2,1)S(1)} %get-tuple-element.79), channel_id=1, source_target_pairs={{0,12},{4,8},{8,4},{12,0},{1,13},{5,9},{9,5},{13,1},{2,14},{6,10},... | collective-permute-start | bytes 147464 | tf_op jit(solution)/shard_map/ppermute | solution.py:393
  65.2 4.6 %collective-permute-start.20 = (bf16[16,1536]{1,0:T(8,128)(2,1)S(1)}, bf16[16,1536]{1,0:T(8,128)(2,1)S(1)}, u32[]{:S(2)}, u32[]{:S(2)}) collective-permute-start(bf16[16,1536]{1,0:T(8,128)(2,1)S(1)} %get-tuple-element.80), channel_id=1, source_target_pairs={{0,4},{4,0},{8,12},{12,8},{1,5},{5,1},{9,13},{13,9},{2,6},{6,2},{1... | collective-permute-start | bytes 147464 | tf_op jit(solution)/shard_map/ppermute | solution.py:393

commit v3 on v2

--- a/solution.py
+++ b/solution.py
@@ -84,7 +84,7 @@
 NEAR, FAR = 1, (2, 3)
 LANES = 128
 NT = (((1,), (1,)), ((), ()))
-VMEM_LIMIT = 24 * 2**20
+VMEM_LIMIT = 10 * 2**20
 NO_COST = pl.CostEstimate(flops=0, bytes_accessed=0, transcendentals=0)
 
 
@@ -262,12 +262,13 @@
     )(in_hbm(weight))
 
 
-def slope_rows(pieces, weight, tile=1024):
+def slope_rows(pieces, weight, later, head, tile=1024):
     rows = sum(piece.shape[0] for piece in pieces)
     features, width = weight.shape
 
     def kernel(*refs):
-        *piece_refs, weight_ref, out_ref, rows_ref = refs
+        *piece_refs, weight_ref, later_ref, out_ref, head_ref, rows_ref, sems = refs
+        copies = streamed(later_ref, head_ref, sems, 0, 1)
         assemble(piece_refs, rows_ref)
         for start in range(0, width, tile):
             cols = pl.ds(start, tile)
@@ -275,30 +276,33 @@
                 rows_ref[...], weight_ref[:, cols], preferred_element_type=jnp.float32
             )
             out_ref[:, cols] = gelu_slope(preact)
-
-    return pl.pallas_call(
-        kernel,
-        out_shape=jax.ShapeDtypeStruct((rows, width), jnp.float32),
-        in_specs=[whole_block()] * (len(pieces) + 1),
-        out_specs=whole_block(),
-        scratch_shapes=[pltpu.VMEM((rows, features), jnp.bfloat16)],
-        compiler_params=pltpu.CompilerParams(vmem_limit_bytes=VMEM_LIMIT),
-        cost_estimate=NO_COST,
-    )(*pieces, in_vmem(weight))
-
-
-def scaled_rows(pieces, head, weight, slope, back, count, parts=2):
+        for copy in copies:
+            copy.wait()
+
+    return pl.pallas_call(
+        kernel,
+        out_shape=[
+            jax.ShapeDtypeStruct((rows, width), jnp.float32),
+            pltpu.VMEM((head, later.shape[1]), later.dtype),
+        ],
+        in_specs=[whole_block()] * (len(pieces) + 1) + [hbm_block()],
+        out_specs=[whole_block()] * 2,
+        scratch_shapes=[
+            pltpu.VMEM((rows, features), jnp.bfloat16),
+            pltpu.SemaphoreType.DMA((1,)),
+        ],
+        compiler_params=pltpu.CompilerParams(vmem_limit_bytes=VMEM_LIMIT),
+        cost_estimate=NO_COST,
+    )(*pieces, in_vmem(weight), in_hbm(later))
+
+
+def scaled_rows(pieces, expert, weight, slope, back, count, tile=1024):
     rows, width = slope.shape
     features = weight.shape[1]
-    first = head.shape[0]
 
     def kernel(expert_ref, *refs):
-        *piece_refs, head_ref, weight_ref, slope_ref, back_ref = refs[: len(pieces) + 4]
-        out_ref, kept_ref, sent_ref, rest_ref = refs[len(pieces) + 4 : len(pieces) + 8]
-        rows_ref, gate_ref, held_ref, held_back_ref, sems, back_sems, rest_sems = refs[
-            len(pieces) + 8 :
-        ]
-        copies = streamed(weight_ref, held_ref, sems, first, parts)
+        *piece_refs, weight_ref, slope_ref, back_ref, out_ref, kept_ref, sent_ref = refs[:-2]
+        rows_ref, gate_ref = refs[-2:]
         assemble(piece_refs, rows_ref)
         start = 0
         for piece in piece_refs:
@@ -308,74 +312,48 @@
                 jnp.where(lane == expert_ref[0], gates, 0.0), axis=1, keepdims=True
             )
             start += piece.shape[0]
-
-        def scale(block, cols):
+        for start in range(0, width, tile):
+            cols = pl.ds(start, tile)
             hidden_grad = lax.dot_general(
-                rows_ref[...], block, NT, preferred_element_type=jnp.float32
+                rows_ref[...], weight_ref[cols, :], NT, preferred_element_type=jnp.float32
             )
             out_ref[:, cols] = (gate_ref[...] * hidden_grad * slope_ref[:, cols]).astype(
                 jnp.bfloat16
             )
-
-        size = (width - first) // parts
-        for start in range(0, first, size):
-            scale(head_ref[pl.ds(start, size), :], pl.ds(start, size))
-        back_copies = streamed(back_ref, held_back_ref, back_sems, 0, parts)
-        for part, copy in enumerate(copies):
-            copy.wait()
-            scale(held_ref[pl.ds(part * size, size), :], pl.ds(first + part * size, size))
-        rest_copies = streamed(back_ref, rest_ref, rest_sems, count, 1)
-        partial_product(out_ref, held_back_ref, back_copies, (kept_ref, sent_ref))
-        for copy in rest_copies:
-            copy.wait()
-
-    expert = lax.axis_index("expert").astype(jnp.int32).reshape(1)
+        partial_product(out_ref, back_ref, 0, (kept_ref, sent_ref))
+
     half = jax.ShapeDtypeStruct((rows // CORES, count), jnp.bfloat16)
     return pl.pallas_call(
         kernel,
-        out_shape=[
-            jax.ShapeDtypeStruct((rows, width), jnp.bfloat16),
-            half,
-            half,
-            pltpu.VMEM((features - count, width), back.dtype),
-        ],
-        in_specs=[pl.BlockSpec(memory_space=pltpu.SMEM)]
-        + [whole_block()] * (len(pieces) + 1)
-        + [hbm_block(), whole_block(), hbm_block()],
-        out_specs=[whole_block()] * 4,
+        out_shape=[jax.ShapeDtypeStruct((rows, width), jnp.bfloat16), half, half],
+        in_specs=[pl.BlockSpec(memory_space=pltpu.SMEM)] + [whole_block()] * (len(pieces) + 3),
+        out_specs=[whole_block()] * 3,
         scratch_shapes=[
             pltpu.VMEM((rows, features), jnp.bfloat16),
             pltpu.VMEM((rows, 1), jnp.float32),
-            pltpu.VMEM((width - first, features), weight.dtype),
-            pltpu.VMEM((count, width), back.dtype),
-            pltpu.SemaphoreType.DMA((parts,)),
-            pltpu.SemaphoreType.DMA((parts,)),
-            pltpu.SemaphoreType.DMA((1,)),
         ],
         compiler_params=pltpu.CompilerParams(vmem_limit_bytes=VMEM_LIMIT),
         cost_estimate=NO_COST,
-    )(expert, *pieces, in_vmem(head), in_hbm(weight), slope, in_hbm(back))
-
-
-def partial_product(scaled_ref, weight_ref, copies, out_refs):
-    half = scaled_ref.shape[0] // len(out_refs)
-    tile = weight_ref.shape[0] // len(copies)
-    for step, copy in enumerate(copies):
-        cols = pl.ds(step * tile, tile)
-        if copy is not None:
-            copy.wait()
-        product = lax.dot_general(
-            scaled_ref[...], weight_ref[cols, :], NT, preferred_element_type=jnp.float32
-        ).astype(jnp.bfloat16)
-        for place, out_ref in enumerate(out_refs):
-            out_ref[:, cols] = product[place * half : (place + 1) * half]
-
-
-def partial_rows(scaled, weight):
-    rows, count = scaled.shape[0], weight.shape[0]
+    )(expert, *pieces, in_vmem(weight), slope, in_vmem(back))
+
+
+def partial_product(scaled_ref, weight_ref, first, out_refs):
+    half, count = out_refs[0].shape
+    product = lax.dot_general(
+        scaled_ref[...],
+        weight_ref[pl.ds(first, count), :],
+        NT,
+        preferred_element_type=jnp.float32,
+    ).astype(jnp.bfloat16)
+    for place, out_ref in enumerate(out_refs):
+        out_ref[...] = product[place * half : (place + 1) * half]
+
+
+def partial_rows(scaled, weight, first):
+    rows, count = scaled.shape[0], weight.shape[0] - first
 
     def kernel(scaled_ref, weight_ref, kept_ref, sent_ref):
-        partial_product(scaled_ref, weight_ref, [None], (kept_ref, sent_ref))
+        partial_product(scaled_ref, weight_ref, first, (kept_ref, sent_ref))
 
     half = jax.ShapeDtypeStruct((rows // CORES, count), jnp.bfloat16)
     return pl.pallas_call(
@@ -405,13 +383,15 @@
     w_in, w_out = w_in[0], w_out[0]
 
     grads, both = with_gates(tokens_in, out_grad, expert_ids, gate_probs)
-    *far_tokens, near, across, grads, w_in = together(
+    expert = lax.axis_index("expert").astype(jnp.int32).reshape(1)
+    *far_tokens, near, across, grads, w_in, expert = together(
         (
             *[beside(tokens_in, "expert", step) for step in FAR],
             beside(both, "expert", NEAR),
             beside(both, "tensor", CORES),
             grads,
             w_in,
+            expert,
         )
     )
     far_tokens = stacked(*far_tokens)
@@ -427,7 +407,9 @@
     token_half = stacked(
         both, far_tokens, near, across, far_tokens_across, near_across, width=features
     )
-    slope = slope_rows([token_half, beside(token_half, "tensor", 1)], held_in)
+    slope, held_out = slope_rows(
+        [token_half, beside(token_half, "tensor", 1)], held_in, w_out, w_out.shape[0]
+    )
     far_grads = stacked(*far_grads)
     far_grads_across, slope = together((beside(far_grads, "tensor", CORES), slope))
     grad_half = stacked(
@@ -440,14 +422,12 @@
         width=grads.shape[1],
         offsets=[features, 0, features, features, 0, features],
     )
-    grad_half, w_out = together((grad_half, w_out))
-    grad_other, head = together(
-        (beside(grad_half, "tensor", 1), prefetched(w_out, w_out.shape[0] // 2))
-    )
-    scaled, *halves, rest = scaled_rows(
-        [grad_half, grad_other], head, w_out, slope, w_in, features // 2
-    )
-    chunks = [halves, partial_rows(scaled, rest)]
+    grad_other = beside(grad_half, "tensor", 1)
+    count = features // 2
+    scaled, *halves = scaled_rows(
+        [grad_half, grad_other], expert, held_out, slope, held_in, count
+    )
+    chunks = [halves, partial_rows(scaled, held_in, count)]
     return added_beside([scatter_rows(*halves, local_rows) for halves in chunks])
 
 

time: 70.7 us -> 66.5 us (0.941)
  Pallas kernels: 24.5 us -> 18.4 us
  waiting for transfers between devices: 24.6 us -> 25.9 us
    pallas_call x1, Pallas kernels: 8.57 us -> 5.18 us  [scaled_rows(): pl.pallas_call(kernel, out_shape=[jax.ShapeDtypeStruct((rows, width), jnp...]
    pallas_call x2 -> x1, Pallas kernels: 7.49 us -> 4.62 us  [prefetched(): pl.pallas_call(kernel, out_shape=pltpu.VMEM((rows, weight.shape[1]), weig...]
    ppermute x21, waiting for transfers between devices: 24.6 us -> 25.9 us  [beside(): return lax.ppermute(array, axis, [(i, i ^ step) for i in range(size)])]
  transfers between devices with their start and end apart: 21 -> 21, of which waited for: 12 -> 11; matrix products, arithmetic and copies ran while one was open for 0% -> 0% of each run, Pallas kernels for 20% -> 17%
where the time goes in v3:
time: 66.5 us; the launch traced here: 66.4 us
  waiting for transfers between devices  25.9 us (39%)
  starting transfers between devices  21.9 us (33%)
  Pallas kernels  18.4 us (28%)
    ppermute x21, waiting for transfers between devices, beside(): return lax.ppermute(array, axis, [(i, i ^ step) for i in range(size)])  25.9 us
    ppermute x21, starting transfers between devices, beside(): return lax.ppermute(array, axis, [(i, i ^ step) for i in range(size)])  21.9 us
    pallas_call x1, Pallas kernels, scaled_rows(): pl.pallas_call(kernel, out_shape=[jax.ShapeDtypeStruct((rows, width), jnp...  5.18 us
    pallas_call x1, Pallas kernels, prefetched(): pl.pallas_call(kernel, out_shape=pltpu.VMEM((rows, weight.shape[1]), weig...  4.62 us
    pallas_call x1, Pallas kernels, slope_rows(): pl.pallas_call(kernel, out_shape=[jax.ShapeDtypeStruct((rows, width), jnp...  4.59 us
    pallas_call x1, Pallas kernels, partial_rows(): pl.pallas_call(kernel, out_shape=[half, half], in_specs=[whole_block()] *...  1.82 us
  transfers between devices with their start and end apart: 21, of which 11 were waited for; matrix products, arithmetic and copies ran while one was open for 0% of the time, Pallas kernels for 17%

profile of v3, /device:TPU:0, one launch (start us, length us, event | category | flops | bytes accessed | tf_op | source)
XLA Modules:
  0.0 66.4 jit_solution(11863662804267988313)
XLA Ops:
  0.0 1.1 %shard_map.64 = (bf16[16,3200]{1,0:T(8,128)(2,1)S(1)}, bf16[16,6272]{1,0:T(8,128)(2,1)S(1)}) custom-call(bf16[16,3072]{1,0:T(8,128)(2,1)} %tokens_ref.1, bf16[16,3072]{1,0:T(8,128)(2,1)} %grads_ref.1, s32[2,16]{1,0:T(2,128)} %bitcast.7, bf16[2,16]{1,0:T(2,128)(2,1)} %bitcast.8), custom_call_target="tpu_custom_call" | custom-call | tf_op jit(solution)/shard_map/pallas_call | solution.py:217
  1.1 3.0 %collective-permute-start.3 = (bf16[16,6272]{1,0:T(8,128)(2,1)S(1)}, bf16[16,6272]{1,0:T(8,128)(2,1)S(1)}, u32[]{:S(2)}, u32[]{:S(2)}) collective-permute-start(bf16[16,6272]{1,0:T(8,128)(2,1)S(1)} %get-tuple-element.41.refs_0_), channel_id=1, source_target_pairs={{0,2},{1,3},{2,0},{3,1},{4,6},{5,7},{6,4},{7,5},{8,10},{9,11},{10,... | collective-permute-start | bytes 602120 | tf_op jit(solution)/shard_map/ppermute | solution.py:371
  4.1 1.6 %collective-permute-start.2 = (bf16[16,6272]{1,0:T(8,128)(2,1)S(1)}, bf16[16,6272]{1,0:T(8,128)(2,1)S(1)}, u32[]{:S(2)}, u32[]{:S(2)}) collective-permute-start(bf16[16,6272]{1,0:T(8,128)(2,1)S(1)} %get-tuple-element.41.refs_0_), channel_id=1, source_target_pairs={{0,4},{4,0},{8,12},{12,8},{1,5},{5,1},{9,13},{13,9},{2,6},{6,2},{1... | collective-permute-start | bytes 602120 | tf_op jit(solution)/shard_map/ppermute | solution.py:371
  5.7 2.6 %collective-permute-start = (bf16[16,3072]{1,0:T(8,128)(2,1)}, bf16[16,3072]{1,0:T(8,128)(2,1)S(1)}, u32[]{:S(2)}, u32[]{:S(2)}) collective-permute-start(bf16[16,3072]{1,0:T(8,128)(2,1)} %tokens_ref.1), channel_id=1, source_target_pairs={{0,8},{4,12},{8,0},{12,4},{1,9},{5,13},{9,1},{13,5},{2,10},{6,14},... | collective-permute-start | bytes 294920 | tf_op jit(solution)/shard_map/ppermute | solution.py:371
  8.2 0.2 collective-permute-start.1
  8.5 4.5 %collective-permute-done.refs_0_ = bf16[16,3072]{1,0:T(8,128)(2,1)S(1)} collective-permute-done((bf16[16,3072]{1,0:T(8,128)(2,1)}, bf16[16,3072]{1,0:T(8,128)(2,1)S(1)}, u32[]{:S(2)}, u32[]{:S(2)}) %collective-permute-start) | collective-permute-done | bytes 98336 | tf_op jit(solution)/shard_map/ppermute | solution.py:371
  13.0 3.9 %collective-permute-done.1.refs_1_ = bf16[16,3072]{1,0:T(8,128)(2,1)S(1)} collective-permute-done((bf16[16,3072]{1,0:T(8,128)(2,1)}, bf16[16,3072]{1,0:T(8,128)(2,1)S(1)}, u32[]{:S(2)}, u32[]{:S(2)}) %collective-permute-start.1) | collective-permute-done | bytes 98336 | tf_op jit(solution)/shard_map/ppermute | solution.py:371
  16.9 0.0 collective-permute-done.3.refs_3_
  16.9 0.5 collective-permute-start.5
  17.4 1.6 %collective-permute-start.4 = (bf16[32,3072]{1,0:T(8,128)(2,1)S(1)}, bf16[32,3072]{1,0:T(8,128)(2,1)S(1)}, u32[]{:S(2)}, u32[]{:S(2)}) collective-permute-start(bf16[32,3072]{1,0:T(8,128)(2,1)S(1)} %shard_map.65.refs_1_), channel_id=1, source_target_pairs={{0,2},{1,3},{2,0},{3,1},{4,6},{5,7},{6,4},{7,5},{8,10},{9,11},{10,... | collective-permute-start | bytes 589832 | tf_op jit(solution)/shard_map/ppermute | solution.py:371
  19.0 1.7 %collective-permute-start.7 = (bf16[16,3200]{1,0:T(8,128)(2,1)S(1)}, bf16[16,3200]{1,0:T(8,128)(2,1)S(1)}, u32[]{:S(2)}, u32[]{:S(2)}) collective-permute-start(bf16[16,3200]{1,0:T(8,128)(2,1)S(1)} %get-tuple-element.47), channel_id=1, source_target_pairs={{0,12},{4,8},{8,4},{12,0},{1,13},{5,9},{9,5},{13,1},{2,14},{6,10},... | collective-permute-start | bytes 307208 | tf_op jit(solution)/shard_map/ppermute | solution.py:371
  20.7 0.7 %collective-permute-start.6 = (bf16[16,3200]{1,0:T(8,128)(2,1)S(1)}, bf16[16,3200]{1,0:T(8,128)(2,1)S(1)}, u32[]{:S(2)}, u32[]{:S(2)}) collective-permute-start(bf16[16,3200]{1,0:T(8,128)(2,1)S(1)} %get-tuple-element.47), channel_id=1, source_target_pairs={{0,8},{4,12},{8,0},{12,4},{1,9},{5,13},{9,1},{13,5},{2,10},{6,14},... | collective-permute-start | bytes 307208 | tf_op jit(solution)/shard_map/ppermute | solution.py:371
  21.4 4.6 %shard_map.66.refs_2_.refs_4_.weight_ref = bf16[3072,2048]{1,0:T(8,128)(2,1)S(1)} custom-call(bf16[3072,2048]{1,0:T(8,128)(2,1)} %bitcast.5), custom_call_target="tpu_custom_call" | custom-call | tf_op jit(solution)/shard_map/pallas_call | solution.py:254
  26.1 2.8 %collective-permute-done.6.refs_0_ = bf16[16,3200]{1,0:T(8,128)(2,1)S(1)} collective-permute-done((bf16[16,3200]{1,0:T(8,128)(2,1)S(1)}, bf16[16,3200]{1,0:T(8,128)(2,1)S(1)}, u32[]{:S(2)}, u32[]{:S(2)}) %collective-permute-start.6) | collective-permute-done | bytes 102432 | tf_op jit(solution)/shard_map/ppermute | solution.py:371
  28.8 0.0 collective-permute-done.4.refs_4_
  28.8 0.0 collective-permute-done.5.refs_5_
  28.9 0.1 shard_map.68.refs_0_
  28.9 0.1 collective-permute-start.9
  29.0 0.6 collective-permute-start.8
  29.6 1.6 %collective-permute-done.9.refs_1_ = bf16[128,3072]{1,0:T(8,128)(2,1)S(1)} collective-permute-done((bf16[128,3072]{1,0:T(8,128)(2,1)S(1)}, bf16[128,3072]{1,0:T(8,128)(2,1)S(1)}, u32[]{:S(2)}, u32[]{:S(2)}) %collective-permute-start.9) | collective-permute-done | bytes 786464 | tf_op jit(solution)/shard_map/ppermute | solution.py:371
  31.3 4.6 %shard_map.69 = (f32[256,2048]{1,0:T(8,128)S(1)}, bf16[2048,3072]{1,0:T(8,128)(2,1)S(1)}) custom-call(bf16[128,3072]{1,0:T(8,128)(2,1)S(1)} %shard_map.68.refs_0_, bf16[128,3072]{1,0:T(8,128)(2,1)S(1)} %collective-permute-done.9.refs_1_, bf16[3072,2048]{1,0:T(8,128)(2,1)S(1)} %shard_map.66.refs_2_.refs_4_.weight_ref, bf16[2048,3072]{1,0:T(8,128)(2,1)} %bitcast.6), custom_call_target="tpu_custom_call" | custom-call | tf_op jit(solution)/shard_map/pallas_call | solution.py:282
  35.9 0.7 %collective-permute-done.8.refs_4_ = bf16[32,3200]{1,0:T(8,128)(2,1)S(1)} collective-permute-done((bf16[32,3200]{1,0:T(8,128)(2,1)S(1)}, bf16[32,3200]{1,0:T(8,128)(2,1)S(1)}, u32[]{:S(2)}, u32[]{:S(2)}) %collective-permute-start.8) | collective-permute-done | bytes 204832 | tf_op jit(solution)/shard_map/ppermute | solution.py:371
  36.6 0.1 shard_map.70.refs_0_
  36.6 0.1 collective-permute-start.10
  36.7 2.3 %collective-permute-done.10.refs_1_ = bf16[128,3200]{1,0:T(8,128)(2,1)S(1)} collective-permute-done((bf16[128,3200]{1,0:T(8,128)(2,1)S(1)}, bf16[128,3200]{1,0:T(8,128)(2,1)S(1)}, u32[]{:S(2)}, u32[]{:S(2)}) %collective-permute-start.10) | collective-permute-done | bytes 819232 | tf_op jit(solution)/shard_map/ppermute | solution.py:371
  39.0 5.2 %shard_map.71 = (bf16[256,2048]{1,0:T(8,128)(2,1)S(1)}, bf16[128,1536]{1,0:T(8,128)(2,1)S(1)}, bf16[128,1536]{1,0:T(8,128)(2,1)S(1)}) custom-call(s32[1]{0:T(128)} %bitcast.3.expert_ref, bf16[128,3200]{1,0:T(8,128)(2,1)S(1)} %shard_map.70.refs_0_, bf16[128,3200]{1,0:T(8,128)(2,1)S(1)} %collective-permute-done.10.refs_1_, ...), custom_call_target="tpu_custom_call" | custom-call | tf_op jit(solution)/shard_map/pallas_call | solution.py:326
  44.2 0.2 collective-permute-start.11
  44.4 1.8 %shard_map.74 = (bf16[128,1536]{1,0:T(8,128)(2,1)S(1)}, bf16[128,1536]{1,0:T(8,128)(2,1)S(1)}) custom-call(bf16[256,2048]{1,0:T(8,128)(2,1)S(1)} %get-tuple-element.68.scaled_ref, bf16[3072,2048]{1,0:T(8,128)(2,1)S(1)} %shard_map.66.refs_2_.refs_4_.weight_ref), custom_call_target="tpu_custom_call" | custom-call | tf_op jit(solution)/shard_map/pallas_call | solution.py:359
  46.2 0.4 collective-permute-start.16
  46.7 0.1 shard_map.72
  46.8 0.6 collective-permute-start.12
  47.4 0.6 collective-permute-done.16.refs_1_
  48.0 0.1 shard_map.75
  48.1 0.9 %collective-permute-start.17 = (bf16[64,1536]{1,0:T(8,128)(2,1)S(1)}, bf16[64,1536]{1,0:T(8,128)(2,1)S(1)}, u32[]{:S(2)}, u32[]{:S(2)}) collective-permute-start(bf16[64,1536]{1,0:T(8,128)(2,1)S(1)} %get-tuple-element.72), channel_id=1, source_target_pairs={{0,2},{1,3},{2,0},{3,1},{4,6},{5,7},{6,4},{7,5},{8,10},{9,11},{10,... | collective-permute-start | bytes 589832 | tf_op jit(solution)/shard_map/ppermute | solution.py:371
  49.0 5.6 %collective-permute-done.12.refs_1_ = bf16[64,1536]{1,0:T(8,128)(2,1)S(1)} collective-permute-done((bf16[64,1536]{1,0:T(8,128)(2,1)S(1)}, bf16[64,1536]{1,0:T(8,128)(2,1)S(1)}, u32[]{:S(2)}, u32[]{:S(2)}) %collective-permute-start.12) | collective-permute-done | bytes 196640 | tf_op jit(solution)/shard_map/ppermute | solution.py:371
  54.6 0.1 collective-permute-start.13
  54.7 1.8 %collective-permute-start.14 = (bf16[16,1536]{1,0:T(8,128)(2,1)S(1)}, bf16[16,1536]{1,0:T(8,128)(2,1)S(1)}, u32[]{:S(2)}, u32[]{:S(2)}) collective-permute-start(bf16[16,1536]{1,0:T(8,128)(2,1)S(1)} %get-tuple-element.66), channel_id=1, source_target_pairs={{0,12},{4,8},{8,4},{12,0},{1,13},{5,9},{9,5},{13,1},{2,14},{6,10},... | collective-permute-start | bytes 147464 | tf_op jit(solution)/shard_map/ppermute | solution.py:371
  56.5 1.7 %collective-permute-start.15 = (bf16[16,1536]{1,0:T(8,128)(2,1)S(1)}, bf16[16,1536]{1,0:T(8,128)(2,1)S(1)}, u32[]{:S(2)}, u32[]{:S(2)}) collective-permute-start(bf16[16,1536]{1,0:T(8,128)(2,1)S(1)} %get-tuple-element.67), channel_id=1, source_target_pairs={{0,4},{4,0},{8,12},{12,8},{1,5},{5,1},{9,13},{13,9},{2,6},{6,2},{1... | collective-permute-start | bytes 147464 | tf_op jit(solution)/shard_map/ppermute | solution.py:371
  58.2 0.0 collective-permute-done.17.refs_1_
  58.2 1.0 %collective-permute-start.18 = (bf16[16,1536]{1,0:T(8,128)(2,1)S(1)}, bf16[16,1536]{1,0:T(8,128)(2,1)S(1)}, u32[]{:S(2)}, u32[]{:S(2)}) collective-permute-start(bf16[16,1536]{1,0:T(8,128)(2,1)S(1)} %get-tuple-element.74), channel_id=1, source_target_pairs={{0,8},{4,12},{8,0},{12,4},{1,9},{5,13},{9,1},{13,5},{2,10},{6,14},... | collective-permute-start | bytes 147464 | tf_op jit(solution)/shard_map/ppermute | solution.py:371
  59.3 1.8 %collective-permute-start.19 = (bf16[16,1536]{1,0:T(8,128)(2,1)S(1)}, bf16[16,1536]{1,0:T(8,128)(2,1)S(1)}, u32[]{:S(2)}, u32[]{:S(2)}) collective-permute-start(bf16[16,1536]{1,0:T(8,128)(2,1)S(1)} %get-tuple-element.75), channel_id=1, source_target_pairs={{0,12},{4,8},{8,4},{12,0},{1,13},{5,9},{9,5},{13,1},{2,14},{6,10},... | collective-permute-start | bytes 147464 | tf_op jit(solution)/shard_map/ppermute | solution.py:371
  61.0 0.8 %collective-permute-start.20 = (bf16[16,1536]{1,0:T(8,128)(2,1)S(1)}, bf16[16,1536]{1,0:T(8,128)(2,1)S(1)}, u32[]{:S(2)}, u32[]{:S(2)}) collective-permute-start(bf16[16,1536]{1,0:T(8,128)(2,1)S(1)} %get-tuple-element.76), channel_id=1, source_target_pairs={{0,4},{4,0},{8,12},{12,8},{1,5},{5,1},{9,13},{13,9},{2,6},{6,2},{1... | collective-permute-start | bytes 147464 | tf_op jit(solution)/shard_map/ppermute | solution.py:371
  61.8 0.0 collective-permute-done.14.refs_2_
  61.8 0.0 collective-permute-done.15.refs_3_
  61.8 2.1 %collective-permute-done.18.refs_5_ = bf16[16,1536]{1,0:T(8,128)(2,1)S(1)} collective-permute-done((bf16[16,1536]{1,0:T(8,128)(2,1)S(1)}, bf16[16,1536]{1,0:T(8,128)(2,1)S(1)}, u32[]{:S(2)}, u32[]{:S(2)}) %collective-permute-start.18) | collective-permute-done | bytes 49184 | tf_op jit(solution)/shard_map/ppermute | solution.py:371
  63.9 1.4 %collective-permute-done.19.refs_6_ = bf16[16,1536]{1,0:T(8,128)(2,1)S(1)} collective-permute-done((bf16[16,1536]{1,0:T(8,128)(2,1)S(1)}, bf16[16,1536]{1,0:T(8,128)(2,1)S(1)}, u32[]{:S(2)}, u32[]{:S(2)}) %collective-permute-start.19) | collective-permute-done | bytes 49184 | tf_op jit(solution)/shard_map/ppermute | solution.py:371
  65.3 0.4 collective-permute-done.20.refs_7_
  65.7 0.7 %shard_map.77 = bf16[16,3072]{1,0:T(8,128)(2,1)} custom-call(bf16[16,1536]{1,0:T(8,128)(2,1)S(1)} %get-tuple-element.64.refs_0_, bf16[16,1536]{1,0:T(8,128)(2,1)S(1)} %collective-permute-done.13.refs_1_, bf16[16,1536]{1,0:T(8,128)(2,1)S(1)} %collective-permute-done.14.refs_2_, bf16[16,1536]{1,0:T(8,128)(2,1)S(1)} %collective-permute-done.15.refs_3_, ...), custom_call_target="tpu_custom_call" | custom-call | tf_op jit(solution)/shard_map/pallas_call | solution.py:111
  (8 shorter events, 0.1 us)
Async XLA Ops:
  1.1 15.8 %collective-permute-start.3 = (bf16[16,6272]{1,0:T(8,128)(2,1)S(1)}, bf16[16,6272]{1,0:T(8,128)(2,1)S(1)}, u32[]{:S(2)}, u32[]{:S(2)}) collective-permute-start(bf16[16,6272]{1,0:T(8,128)(2,1)S(1)} %get-tuple-element.41.refs_0_), channel_id=1, source_target_pairs={{0,2},{1,3},{2,0},{3,1},{4,6},{5,7},{6,4},{7,5},{8,10},{9,11},{10,... | collective-permute-start | bytes 602120 | tf_op jit(solution)/shard_map/ppermute | solution.py:371
  4.1 12.8 %collective-permute-start.2 = (bf16[16,6272]{1,0:T(8,128)(2,1)S(1)}, bf16[16,6272]{1,0:T(8,128)(2,1)S(1)}, u32[]{:S(2)}, u32[]{:S(2)}) collective-permute-start(bf16[16,6272]{1,0:T(8,128)(2,1)S(1)} %get-tuple-element.41.refs_0_), channel_id=1, source_target_pairs={{0,4},{4,0},{8,12},{12,8},{1,5},{5,1},{9,13},{13,9},{2,6},{6,2},{1... | collective-permute-start | bytes 602120 | tf_op jit(solution)/shard_map/ppermute | solution.py:371
  5.7 7.3 %collective-permute-start = (bf16[16,3072]{1,0:T(8,128)(2,1)}, bf16[16,3072]{1,0:T(8,128)(2,1)S(1)}, u32[]{:S(2)}, u32[]{:S(2)}) collective-permute-start(bf16[16,3072]{1,0:T(8,128)(2,1)} %tokens_ref.1), channel_id=1, source_target_pairs={{0,8},{4,12},{8,0},{12,4},{1,9},{5,13},{9,1},{13,5},{2,10},{6,14},... | collective-permute-start | bytes 294920 | tf_op jit(solution)/shard_map/ppermute | solution.py:371
  8.2 8.6 %collective-permute-start.1 = (bf16[16,3072]{1,0:T(8,128)(2,1)}, bf16[16,3072]{1,0:T(8,128)(2,1)S(1)}, u32[]{:S(2)}, u32[]{:S(2)}) collective-permute-start(bf16[16,3072]{1,0:T(8,128)(2,1)} %tokens_ref.1), channel_id=1, source_target_pairs={{0,12},{4,8},{8,4},{12,0},{1,13},{5,9},{9,5},{13,1},{2,14},{6,10},... | collective-permute-start | bytes 294920 | tf_op jit(solution)/shard_map/ppermute | solution.py:371
  16.9 12.0 %collective-permute-start.5 = (bf16[16,6272]{1,0:T(8,128)(2,1)S(1)}, bf16[16,6272]{1,0:T(8,128)(2,1)S(1)}, u32[]{:S(2)}, u32[]{:S(2)}) collective-permute-start(bf16[16,6272]{1,0:T(8,128)(2,1)S(1)} %collective-permute-done.2.refs_2_), channel_id=1, source_target_pairs={{0,2},{1,3},{2,0},{3,1},{4,6},{5,7},{6,4},{7,5},{8,10},{9,11},{10,... | collective-permute-start | bytes 602120 | tf_op jit(solution)/shard_map/ppermute | solution.py:371
  17.4 11.4 %collective-permute-start.4 = (bf16[32,3072]{1,0:T(8,128)(2,1)S(1)}, bf16[32,3072]{1,0:T(8,128)(2,1)S(1)}, u32[]{:S(2)}, u32[]{:S(2)}) collective-permute-start(bf16[32,3072]{1,0:T(8,128)(2,1)S(1)} %shard_map.65.refs_1_), channel_id=1, source_target_pairs={{0,2},{1,3},{2,0},{3,1},{4,6},{5,7},{6,4},{7,5},{8,10},{9,11},{10,... | collective-permute-start | bytes 589832 | tf_op jit(solution)/shard_map/ppermute | solution.py:371
  19.0 7.1 %collective-permute-start.7 = (bf16[16,3200]{1,0:T(8,128)(2,1)S(1)}, bf16[16,3200]{1,0:T(8,128)(2,1)S(1)}, u32[]{:S(2)}, u32[]{:S(2)}) collective-permute-start(bf16[16,3200]{1,0:T(8,128)(2,1)S(1)} %get-tuple-element.47), channel_id=1, source_target_pairs={{0,12},{4,8},{8,4},{12,0},{1,13},{5,9},{9,5},{13,1},{2,14},{6,10},... | collective-permute-start | bytes 307208 | tf_op jit(solution)/shard_map/ppermute | solution.py:371
  20.7 8.1 %collective-permute-start.6 = (bf16[16,3200]{1,0:T(8,128)(2,1)S(1)}, bf16[16,3200]{1,0:T(8,128)(2,1)S(1)}, u32[]{:S(2)}, u32[]{:S(2)}) collective-permute-start(bf16[16,3200]{1,0:T(8,128)(2,1)S(1)} %get-tuple-element.47), channel_id=1, source_target_pairs={{0,8},{4,12},{8,0},{12,4},{1,9},{5,13},{9,1},{13,5},{2,10},{6,14},... | collective-permute-start | bytes 307208 | tf_op jit(solution)/shard_map/ppermute | solution.py:371
  28.9 2.4 %collective-permute-start.9 = (bf16[128,3072]{1,0:T(8,128)(2,1)S(1)}, bf16[128,3072]{1,0:T(8,128)(2,1)S(1)}, u32[]{:S(2)}, u32[]{:S(2)}) collective-permute-start(bf16[128,3072]{1,0:T(8,128)(2,1)S(1)} %shard_map.68.refs_0_), channel_id=1, source_target_pairs={{0,1},{1,0},{2,3},{3,2},{4,5},{5,4},{6,7},{7,6},{8,9},{9,8},{10,11... | collective-permute-start | bytes 2359304 | tf_op jit(solution)/shard_map/ppermute | solution.py:371
  29.0 7.5 %collective-permute-start.8 = (bf16[32,3200]{1,0:T(8,128)(2,1)S(1)}, bf16[32,3200]{1,0:T(8,128)(2,1)S(1)}, u32[]{:S(2)}, u32[]{:S(2)}) collective-permute-start(bf16[32,3200]{1,0:T(8,128)(2,1)S(1)} %shard_map.67.refs_1_), channel_id=1, source_target_pairs={{0,2},{1,3},{2,0},{3,1},{4,6},{5,7},{6,4},{7,5},{8,10},{9,11},{10,... | collective-permute-start | bytes 614408 | tf_op jit(solution)/shard_map/ppermute | solution.py:371
  36.6 2.4 %collective-permute-start.10 = (bf16[128,3200]{1,0:T(8,128)(2,1)S(1)}, bf16[128,3200]{1,0:T(8,128)(2,1)S(1)}, u32[]{:S(2)}, u32[]{:S(2)}) collective-permute-start(bf16[128,3200]{1,0:T(8,128)(2,1)S(1)} %shard_map.70.refs_0_), channel_id=1, source_target_pairs={{0,1},{1,0},{2,3},{3,2},{4,5},{5,4},{6,7},{7,6},{8,9},{9,8},{10,11... | collective-permute-start | bytes 2457608 | tf_op jit(solution)/shard_map/ppermute | solution.py:371
  44.2 2.5 %collective-permute-start.11 = (bf16[128,1536]{1,0:T(8,128)(2,1)S(1)}, bf16[128,1536]{1,0:T(8,128)(2,1)S(1)}, u32[]{:S(2)}, u32[]{:S(2)}) collective-permute-start(bf16[128,1536]{1,0:T(8,128)(2,1)S(1)} %get-tuple-element.61), channel_id=1, source_target_pairs={{0,1},{1,0},{2,3},{3,2},{4,5},{5,4},{6,7},{7,6},{8,9},{9,8},{10,11... | collective-permute-start | bytes 1179656 | tf_op jit(solution)/shard_map/ppermute | solution.py:371
  46.2 1.8 %collective-permute-start.16 = (bf16[128,1536]{1,0:T(8,128)(2,1)S(1)}, bf16[128,1536]{1,0:T(8,128)(2,1)S(1)}, u32[]{:S(2)}, u32[]{:S(2)}) collective-permute-start(bf16[128,1536]{1,0:T(8,128)(2,1)S(1)} %get-tuple-element.70), channel_id=1, source_target_pairs={{0,1},{1,0},{2,3},{3,2},{4,5},{5,4},{6,7},{7,6},{8,9},{9,8},{10,11... | collective-permute-start | bytes 1179656 | tf_op jit(solution)/shard_map/ppermute | solution.py:371
  46.8 7.8 %collective-permute-start.12 = (bf16[64,1536]{1,0:T(8,128)(2,1)S(1)}, bf16[64,1536]{1,0:T(8,128)(2,1)S(1)}, u32[]{:S(2)}, u32[]{:S(2)}) collective-permute-start(bf16[64,1536]{1,0:T(8,128)(2,1)S(1)} %get-tuple-element.63), channel_id=1, source_target_pairs={{0,2},{1,3},{2,0},{3,1},{4,6},{5,7},{6,4},{7,5},{8,10},{9,11},{10,... | collective-permute-start | bytes 589832 | tf_op jit(solution)/shard_map/ppermute | solution.py:371
  48.1 10.1 %collective-permute-start.17 = (bf16[64,1536]{1,0:T(8,128)(2,1)S(1)}, bf16[64,1536]{1,0:T(8,128)(2,1)S(1)}, u32[]{:S(2)}, u32[]{:S(2)}) collective-permute-start(bf16[64,1536]{1,0:T(8,128)(2,1)S(1)} %get-tuple-element.72), channel_id=1, source_target_pairs={{0,2},{1,3},{2,0},{3,1},{4,6},{5,7},{6,4},{7,5},{8,10},{9,11},{10,... | collective-permute-start | bytes 589832 | tf_op jit(solution)/shard_map/ppermute | solution.py:371
  54.6 6.4 %collective-permute-start.13 = (bf16[16,1536]{1,0:T(8,128)(2,1)S(1)}, bf16[16,1536]{1,0:T(8,128)(2,1)S(1)}, u32[]{:S(2)}, u32[]{:S(2)}) collective-permute-start(bf16[16,1536]{1,0:T(8,128)(2,1)S(1)} %get-tuple-element.65), channel_id=1, source_target_pairs={{0,8},{4,12},{8,0},{12,4},{1,9},{5,13},{9,1},{13,5},{2,10},{6,14},... | collective-permute-start | bytes 147464 | tf_op jit(solution)/shard_map/ppermute | solution.py:371
  54.7 7.1 %collective-permute-start.14 = (bf16[16,1536]{1,0:T(8,128)(2,1)S(1)}, bf16[16,1536]{1,0:T(8,128)(2,1)S(1)}, u32[]{:S(2)}, u32[]{:S(2)}) collective-permute-start(bf16[16,1536]{1,0:T(8,128)(2,1)S(1)} %get-tuple-element.66), channel_id=1, source_target_pairs={{0,12},{4,8},{8,4},{12,0},{1,13},{5,9},{9,5},{13,1},{2,14},{6,10},... | collective-permute-start | bytes 147464 | tf_op jit(solution)/shard_map/ppermute | solution.py:371
  56.5 5.3 %collective-permute-start.15 = (bf16[16,1536]{1,0:T(8,128)(2,1)S(1)}, bf16[16,1536]{1,0:T(8,128)(2,1)S(1)}, u32[]{:S(2)}, u32[]{:S(2)}) collective-permute-start(bf16[16,1536]{1,0:T(8,128)(2,1)S(1)} %get-tuple-element.67), channel_id=1, source_target_pairs={{0,4},{4,0},{8,12},{12,8},{1,5},{5,1},{9,13},{13,9},{2,6},{6,2},{1... | collective-permute-start | bytes 147464 | tf_op jit(solution)/shard_map/ppermute | solution.py:371
  58.2 5.7 %collective-permute-start.18 = (bf16[16,1536]{1,0:T(8,128)(2,1)S(1)}, bf16[16,1536]{1,0:T(8,128)(2,1)S(1)}, u32[]{:S(2)}, u32[]{:S(2)}) collective-permute-start(bf16[16,1536]{1,0:T(8,128)(2,1)S(1)} %get-tuple-element.74), channel_id=1, source_target_pairs={{0,8},{4,12},{8,0},{12,4},{1,9},{5,13},{9,1},{13,5},{2,10},{6,14},... | collective-permute-start | bytes 147464 | tf_op jit(solution)/shard_map/ppermute | solution.py:371
  59.3 6.0 %collective-permute-start.19 = (bf16[16,1536]{1,0:T(8,128)(2,1)S(1)}, bf16[16,1536]{1,0:T(8,128)(2,1)S(1)}, u32[]{:S(2)}, u32[]{:S(2)}) collective-permute-start(bf16[16,1536]{1,0:T(8,128)(2,1)S(1)} %get-tuple-element.75), channel_id=1, source_target_pairs={{0,12},{4,8},{8,4},{12,0},{1,13},{5,9},{9,5},{13,1},{2,14},{6,10},... | collective-permute-start | bytes 147464 | tf_op jit(solution)/shard_map/ppermute | solution.py:371
  61.0 4.6 %collective-permute-start.20 = (bf16[16,1536]{1,0:T(8,128)(2,1)S(1)}, bf16[16,1536]{1,0:T(8,128)(2,1)S(1)}, u32[]{:S(2)}, u32[]{:S(2)}) collective-permute-start(bf16[16,1536]{1,0:T(8,128)(2,1)S(1)} %get-tuple-element.76), channel_id=1, source_target_pairs={{0,4},{4,0},{8,12},{12,8},{1,5},{5,1},{9,13},{13,9},{2,6},{6,2},{1... | collective-permute-start | bytes 147464 | tf_op jit(solution)/shard_map/ppermute | solution.py:371

commit v4 on v3

--- a/solution.py
+++ b/solution.py
@@ -86,6 +86,7 @@
 NT = (((1,), (1,)), ((), ()))
 VMEM_LIMIT = 10 * 2**20
 NO_COST = pl.CostEstimate(flops=0, bytes_accessed=0, transcendentals=0)
+LONG = pl.CostEstimate(flops=10**11, bytes_accessed=10**9, transcendentals=0)
 
 
 def in_vmem(array):
@@ -107,18 +108,18 @@
         start += piece.shape[0]
 
 
-def small_kernel(kernel, out_shape, operands):
+def small_kernel(kernel, out_shape, operands, cost=NO_COST):
     return pl.pallas_call(
         kernel,
         out_shape=out_shape,
         in_specs=[whole_block()] * len(operands),
         out_specs=jax.tree.map(lambda _: whole_block(), out_shape),
         compiler_params=pltpu.CompilerParams(vmem_limit_bytes=VMEM_LIMIT),
-        cost_estimate=NO_COST,
+        cost_estimate=cost,
     )(*operands)
 
 
-def stacked(*pieces, width=None, offsets=None):
+def stacked(*pieces, width=None, offsets=None, cost=NO_COST):
     width = width or pieces[0].shape[1]
     offsets = offsets or [0] * len(pieces)
     rows = sum(piece.shape[0] for piece in pieces)
@@ -130,45 +131,64 @@
             out_ref[pl.ds(start, piece.shape[0]), :] = piece[:, offset : offset + width]
             start += piece.shape[0]
 
-    return small_kernel(kernel, jax.ShapeDtypeStruct((rows, width), jnp.bfloat16), pieces)
-
-
-def added(terms, sizes):
+    return small_kernel(kernel, jax.ShapeDtypeStruct((rows, width), jnp.bfloat16), pieces, cost)
+
+
+def passed(*arrays, cost=NO_COST):
+    def kernel(*refs):
+        for array_ref, out_ref in zip(refs[: len(arrays)], refs[len(arrays) :]):
+            out_ref[...] = array_ref[...]
+
+    out_shape = [jax.ShapeDtypeStruct(array.shape, array.dtype) for array in arrays]
+    return small_kernel(kernel, out_shape, arrays, cost)
+
+
+def added(terms, sizes, joined=None, cost=NO_COST):
     width = terms[0].shape[1]
+    widths = [width] * len(sizes)
+    if joined is not None:
+        widths[-1] += joined.shape[1]
 
     def kernel(*refs):
-        term_refs, out_refs = refs[: len(terms)], refs[len(terms) :]
+        term_refs, out_refs = refs[: len(terms)], refs[-len(sizes) :]
         start = 0
         for out_ref in out_refs:
             rows = pl.ds(start, out_ref.shape[0])
             total = term_refs[0][rows, :].astype(jnp.float32)
             for term_ref in term_refs[1:]:
                 total += term_ref[rows, :].astype(jnp.float32)
-            out_ref[...] = total.astype(jnp.bfloat16)
+            out_ref[:, out_ref.shape[1] - width :] = total.astype(jnp.bfloat16)
             start += out_ref.shape[0]
+        if joined is not None:
+            out_refs[-1][:, : joined.shape[1]] = refs[len(terms)][...]
 
     return small_kernel(
-        kernel, [jax.ShapeDtypeStruct((size, width), jnp.bfloat16) for size in sizes], terms
-    )
-
-
-def added_beside(chunks):
+        kernel,
+        [jax.ShapeDtypeStruct((size, wide), jnp.bfloat16) for size, wide in zip(sizes, widths)],
+        terms if joined is None else [*terms, joined],
+        cost,
+    )
+
+
+def added_beside(chunks, wide):
     rows = chunks[0][0].shape[0]
     widths = [chunk[0].shape[1] for chunk in chunks]
     terms = [term for chunk in chunks for term in chunk]
 
     def kernel(*refs):
-        *term_refs, out_ref = refs
+        *term_refs, wide_ref, out_ref = refs
         start = 0
         for chunk, width in zip(chunks, widths):
             group, term_refs = term_refs[: len(chunk)], term_refs[len(chunk) :]
-            total = group[0][...].astype(jnp.float32)
-            for term_ref in group[1:]:
+            total = wide_ref[:, start : start + width].astype(jnp.float32)
+            for term_ref in group:
                 total += term_ref[...].astype(jnp.float32)
             out_ref[:, start : start + width] = total.astype(jnp.bfloat16)
             start += width
 
-    return small_kernel(kernel, jax.ShapeDtypeStruct((rows, sum(widths)), jnp.bfloat16), terms)
+    return small_kernel(
+        kernel, jax.ShapeDtypeStruct((rows, sum(widths)), jnp.bfloat16), [*terms, wide]
+    )
 
 
 def in_hbm(array):
@@ -371,10 +391,16 @@
     return lax.ppermute(array, axis, [(i, i ^ step) for i in range(size)])
 
 
-def scatter_rows(kept, sent, rows):
-    kept, sent = added([kept, beside(sent, "tensor", 1)], [rows * EXPERTS] * 2)
-    kept, *sent = added([kept, beside(sent, "tensor", CORES)], [rows] * EXPERTS)
-    return [kept] + [beside(block, "expert", step) for step, block in zip((*FAR, NEAR), sent)]
+def scatter_rows(chunks, rows):
+    terms, near = [], None
+    for kept, sent in chunks:
+        kept, sent = added([kept, beside(sent, "tensor", 1)], [rows * EXPERTS] * 2)
+        kept, *sent, near = added(
+            [kept, beside(sent, "tensor", CORES)], [rows] * EXPERTS, near
+        )
+        terms.append([kept] + [beside(block, "expert", step) for step, block in zip(FAR, sent)])
+    terms[0] = added(terms[0], [rows], cost=LONG)
+    return added_beside(terms, beside(near, "expert", NEAR))
 
 
 def dense(tokens_in, out_grad, expert_ids, gate_probs, w_in, w_out):
@@ -384,51 +410,38 @@
 
     grads, both = with_gates(tokens_in, out_grad, expert_ids, gate_probs)
     expert = lax.axis_index("expert").astype(jnp.int32).reshape(1)
-    *far_tokens, near, across, grads, w_in, expert = together(
+    near = beside(both, "expert", NEAR)
+    across = beside(both, "tensor", CORES)
+    far_tokens = passed(*[beside(tokens_in, "expert", step) for step in FAR], cost=LONG)
+    *far_tokens, across, grads, w_in, expert = together((*far_tokens, across, grads, w_in, expert))
+    far_grads = stacked(*[beside(grads, "expert", step) for step in FAR])
+    *far_tokens_across, near_across, far_grads, held_in = together(
         (
-            *[beside(tokens_in, "expert", step) for step in FAR],
-            beside(both, "expert", NEAR),
-            beside(both, "tensor", CORES),
-            grads,
-            w_in,
-            expert,
-        )
-    )
-    far_tokens = stacked(*far_tokens)
-    far_tokens, far_tokens_across, near_across, *far_grads, held_in = together(
-        (
-            far_tokens,
-            beside(far_tokens, "tensor", CORES),
+            *[beside(tokens, "tensor", CORES) for tokens in far_tokens],
             beside(near, "tensor", CORES),
-            *[beside(grads, "expert", step) for step in FAR],
+            far_grads,
             prefetched(w_in, features),
         )
     )
     token_half = stacked(
-        both, far_tokens, near, across, far_tokens_across, near_across, width=features
+        both, *far_tokens, near, across, *far_tokens_across, near_across, width=features
     )
     slope, held_out = slope_rows(
         [token_half, beside(token_half, "tensor", 1)], held_in, w_out, w_out.shape[0]
     )
-    far_grads = stacked(*far_grads)
-    far_grads_across, slope = together((beside(far_grads, "tensor", CORES), slope))
-    grad_half = stacked(
-        both,
-        far_grads,
-        near,
-        across,
-        far_grads_across,
-        near_across,
-        width=grads.shape[1],
-        offsets=[features, 0, features, features, 0, features],
-    )
-    grad_other = beside(grad_half, "tensor", 1)
+    grad_column = stacked(both, far_grads, near, width=grads.shape[1], offsets=[features, 0, features])
+    far_grads_across, slope, grad_column_other = together(
+        (beside(far_grads, "tensor", CORES), slope, beside(grad_column, "tensor", 1))
+    )
+    grad_across = stacked(
+        across, far_grads_across, near_across, width=grads.shape[1], offsets=[features, 0, features]
+    )
+    grad_pieces = [grad_column, grad_across, grad_column_other, beside(grad_across, "tensor", 1)]
     count = features // 2
     scaled, *halves = scaled_rows(
-        [grad_half, grad_other], expert, held_out, slope, held_in, count
-    )
-    chunks = [halves, partial_rows(scaled, held_in, count)]
-    return added_beside([scatter_rows(*halves, local_rows) for halves in chunks])
+        grad_pieces, expert, held_out, slope, held_in, count
+    )
+    return scatter_rows([halves, partial_rows(scaled, held_in, count)], local_rows)
 
 
 def local(*args):

time: 66.5 us -> 64 us (0.962)
  waiting for transfers between devices: 25.9 us -> 19.1 us
  starting transfers between devices: 21.9 us -> 26.2 us
    ppermute x21 -> x22, waiting for transfers between devices: 25.9 us -> 19.1 us  [beside(): return lax.ppermute(array, axis, [(i, i ^ step) for i in range(size)])]
    ppermute x21 -> x22, starting transfers between devices: 21.9 us -> 26.2 us  [beside(): return lax.ppermute(array, axis, [(i, i ^ step) for i in range(size)])]
  transfers between devices with their start and end apart: 21 -> 22, of which waited for: 11 -> 12; matrix products, arithmetic and copies ran while one was open for 0% -> 0% of each run, Pallas kernels for 17% -> 18%
where the time goes in v4:
time: 64 us; the launch traced here: 63.8 us
  starting transfers between devices  26.2 us (41%)
  waiting for transfers between devices  19.1 us (30%)
  Pallas kernels  18.4 us (29%)
    ppermute x22, starting transfers between devices, beside(): return lax.ppermute(array, axis, [(i, i ^ step) for i in range(size)])  26.2 us
    ppermute x22, waiting for transfers between devices, beside(): return lax.ppermute(array, axis, [(i, i ^ step) for i in range(size)])  19.1 us
    pallas_call x1, Pallas kernels, scaled_rows(): pl.pallas_call(kernel, out_shape=[jax.ShapeDtypeStruct((rows, width), jnp...  5.19 us
    pallas_call x1, Pallas kernels, prefetched(): pl.pallas_call(kernel, out_shape=pltpu.VMEM((rows, weight.shape[1]), weig...  4.62 us
    pallas_call x1, Pallas kernels, slope_rows(): pl.pallas_call(kernel, out_shape=[jax.ShapeDtypeStruct((rows, width), jnp...  4.6 us
    pallas_call x1, Pallas kernels, partial_rows(): pl.pallas_call(kernel, out_shape=[half, half], in_specs=[whole_block()] *...  1.83 us
  transfers between devices with their start and end apart: 22, of which 12 were waited for; matrix products, arithmetic and copies ran while one was open for 0% of the time, Pallas kernels for 18%

profile of v4, /device:TPU:0, one launch (start us, length us, event | category | flops | bytes accessed | tf_op | source)
XLA Modules:
  0.0 63.8 jit_solution(14991690120647765055)
XLA Ops:
  0.0 1.1 %shard_map.65 = (bf16[16,3200]{1,0:T(8,128)(2,1)S(1)}, bf16[16,6272]{1,0:T(8,128)(2,1)S(1)}) custom-call(bf16[16,3072]{1,0:T(8,128)(2,1)} %tokens_ref.1, bf16[16,3072]{1,0:T(8,128)(2,1)} %grads_ref.1, s32[2,16]{1,0:T(2,128)} %bitcast.7, bf16[2,16]{1,0:T(2,128)(2,1)} %bitcast.8), custom_call_target="tpu_custom_call" | custom-call | tf_op jit(solution)/shard_map/pallas_call | solution.py:237
  1.1 3.1 %collective-permute-start.5 = (bf16[16,6272]{1,0:T(8,128)(2,1)S(1)}, bf16[16,6272]{1,0:T(8,128)(2,1)S(1)}, u32[]{:S(2)}, u32[]{:S(2)}) collective-permute-start(bf16[16,6272]{1,0:T(8,128)(2,1)S(1)} %get-tuple-element.44.refs_0_), channel_id=1, source_target_pairs={{0,4},{4,0},{8,12},{12,8},{1,5},{5,1},{9,13},{13,9},{2,6},{6,2},{1... | collective-permute-start | bytes 602120 | tf_op jit(solution)/shard_map/ppermute | solution.py:391
  4.2 2.6 %collective-permute-start = (bf16[16,3072]{1,0:T(8,128)(2,1)}, bf16[16,3072]{1,0:T(8,128)(2,1)S(1)}, u32[]{:S(2)}, u32[]{:S(2)}) collective-permute-start(bf16[16,3072]{1,0:T(8,128)(2,1)} %tokens_ref.1), channel_id=1, source_target_pairs={{0,8},{4,12},{8,0},{12,4},{1,9},{5,13},{9,1},{13,5},{2,10},{6,14},... | collective-permute-start | bytes 294920 | tf_op jit(solution)/shard_map/ppermute | solution.py:391
  6.7 0.0 collective-permute-start.1
  6.8 1.7 %collective-permute-start.2 = (bf16[16,6272]{1,0:T(8,128)(2,1)S(1)}, bf16[16,6272]{1,0:T(8,128)(2,1)S(1)}, u32[]{:S(2)}, u32[]{:S(2)}) collective-permute-start(bf16[16,6272]{1,0:T(8,128)(2,1)S(1)} %get-tuple-element.44.refs_0_), channel_id=1, source_target_pairs={{0,2},{1,3},{2,0},{3,1},{4,6},{5,7},{6,4},{7,5},{8,10},{9,11},{10,... | collective-permute-start | bytes 602120 | tf_op jit(solution)/shard_map/ppermute | solution.py:391
  8.5 2.6 %collective-permute-done.5.refs_2_.refs_3_ = bf16[16,6272]{1,0:T(8,128)(2,1)S(1)} collective-permute-done((bf16[16,6272]{1,0:T(8,128)(2,1)S(1)}, bf16[16,6272]{1,0:T(8,128)(2,1)S(1)}, u32[]{:S(2)}, u32[]{:S(2)}) %collective-permute-start.5) | collective-permute-done | bytes 200736 | tf_op jit(solution)/shard_map/ppermute | solution.py:391
  11.1 1.8 %collective-permute-start.6 = (bf16[16,6272]{1,0:T(8,128)(2,1)S(1)}, bf16[16,6272]{1,0:T(8,128)(2,1)S(1)}, u32[]{:S(2)}, u32[]{:S(2)}) collective-permute-start(bf16[16,6272]{1,0:T(8,128)(2,1)S(1)} %collective-permute-done.5.refs_2_.refs_3_), channel_id=1, source_target_pairs={{0,2},{1,3},{2,0},{3,1},{4,6},{5,7},{6,4},{7,5},{8,10},{9,11},{10,... | collective-permute-start | bytes 602120 | tf_op jit(solution)/shard_map/ppermute | solution.py:391
  12.9 0.0 collective-permute-done.refs_0_
  12.9 2.8 %collective-permute-done.1.refs_1_ = bf16[16,3072]{1,0:T(8,128)(2,1)S(1)} collective-permute-done((bf16[16,3072]{1,0:T(8,128)(2,1)}, bf16[16,3072]{1,0:T(8,128)(2,1)S(1)}, u32[]{:S(2)}, u32[]{:S(2)}) %collective-permute-start.1) | collective-permute-done | bytes 98336 | tf_op jit(solution)/shard_map/ppermute | solution.py:391
  15.7 0.0 collective-permute-done.2.refs_4_.refs_0_
  15.7 2.0 %collective-permute-start.8 = (bf16[16,3200]{1,0:T(8,128)(2,1)S(1)}, bf16[16,3200]{1,0:T(8,128)(2,1)S(1)}, u32[]{:S(2)}, u32[]{:S(2)}) collective-permute-start(bf16[16,3200]{1,0:T(8,128)(2,1)S(1)} %get-tuple-element.49), channel_id=1, source_target_pairs={{0,12},{4,8},{8,4},{12,0},{1,13},{5,9},{9,5},{13,1},{2,14},{6,10},... | collective-permute-start | bytes 307208 | tf_op jit(solution)/shard_map/ppermute | solution.py:391
  17.7 1.1 %collective-permute-start.7 = (bf16[16,3200]{1,0:T(8,128)(2,1)S(1)}, bf16[16,3200]{1,0:T(8,128)(2,1)S(1)}, u32[]{:S(2)}, u32[]{:S(2)}) collective-permute-start(bf16[16,3200]{1,0:T(8,128)(2,1)S(1)} %get-tuple-element.49), channel_id=1, source_target_pairs={{0,8},{4,12},{8,0},{12,4},{1,9},{5,13},{9,1},{13,5},{2,10},{6,14},... | collective-permute-start | bytes 307208 | tf_op jit(solution)/shard_map/ppermute | solution.py:391
  18.7 1.5 %collective-permute-start.3 = (bf16[16,3072]{1,0:T(8,128)(2,1)S(1)}, bf16[16,3072]{1,0:T(8,128)(2,1)S(1)}, u32[]{:S(2)}, u32[]{:S(2)}) collective-permute-start(bf16[16,3072]{1,0:T(8,128)(2,1)S(1)} %get-tuple-element.47.refs_1_), channel_id=1, source_target_pairs={{0,2},{1,3},{2,0},{3,1},{4,6},{5,7},{6,4},{7,5},{8,10},{9,11},{10,... | collective-permute-start | bytes 294920 | tf_op jit(solution)/shard_map/ppermute | solution.py:391
  20.2 0.5 collective-permute-start.4
  20.8 4.6 %shard_map.67.refs_2_.refs_6_.weight_ref = bf16[3072,2048]{1,0:T(8,128)(2,1)S(1)} custom-call(bf16[3072,2048]{1,0:T(8,128)(2,1)} %bitcast.5), custom_call_target="tpu_custom_call" | custom-call | tf_op jit(solution)/shard_map/pallas_call | solution.py:274
  25.4 0.0 collective-permute-done.8.refs_1_
  25.4 1.1 %collective-permute-done.7.refs_0_ = bf16[16,3200]{1,0:T(8,128)(2,1)S(1)} collective-permute-done((bf16[16,3200]{1,0:T(8,128)(2,1)S(1)}, bf16[16,3200]{1,0:T(8,128)(2,1)S(1)}, u32[]{:S(2)}, u32[]{:S(2)}) %collective-permute-start.7) | collective-permute-done | bytes 102432 | tf_op jit(solution)/shard_map/ppermute | solution.py:391
  26.5 0.0 collective-permute-done.3.refs_5_
  26.5 0.0 collective-permute-done.6.refs_7_.refs_2_
  26.5 0.1 shard_map.69.refs_0_
  26.6 0.1 collective-permute-start.10
  26.7 0.6 collective-permute-start.11
  27.3 1.5 %collective-permute-start.9 = (bf16[32,3200]{1,0:T(8,128)(2,1)S(1)}, bf16[32,3200]{1,0:T(8,128)(2,1)S(1)}, u32[]{:S(2)}, u32[]{:S(2)}) collective-permute-start(bf16[32,3200]{1,0:T(8,128)(2,1)S(1)} %shard_map.66.refs_1_), channel_id=1, source_target_pairs={{0,2},{1,3},{2,0},{3,1},{4,6},{5,7},{6,4},{7,5},{8,10},{9,11},{10,... | collective-permute-start | bytes 614408 | tf_op jit(solution)/shard_map/ppermute | solution.py:391
  28.8 0.2 collective-permute-done.10.refs_1_
  29.0 4.6 %shard_map.70 = (f32[256,2048]{1,0:T(8,128)S(1)}, bf16[2048,3072]{1,0:T(8,128)(2,1)S(1)}) custom-call(bf16[128,3072]{1,0:T(8,128)(2,1)S(1)} %shard_map.69.refs_0_, bf16[128,3072]{1,0:T(8,128)(2,1)S(1)} %collective-permute-done.10.refs_1_, bf16[3072,2048]{1,0:T(8,128)(2,1)S(1)} %shard_map.67.refs_2_.refs_6_.weight_ref, bf16[2048,3072]{1,0:T(8,128)(2,1)} %bitcast.6), custom_call_target="tpu_custom_call" | custom-call | tf_op jit(solution)/shard_map/pallas_call | solution.py:302
  33.6 0.8 %collective-permute-done.9.refs_1_ = bf16[32,3200]{1,0:T(8,128)(2,1)S(1)} collective-permute-done((bf16[32,3200]{1,0:T(8,128)(2,1)S(1)}, bf16[32,3200]{1,0:T(8,128)(2,1)S(1)}, u32[]{:S(2)}, u32[]{:S(2)}) %collective-permute-start.9) | collective-permute-done | bytes 204832 | tf_op jit(solution)/shard_map/ppermute | solution.py:391
  34.4 0.1 collective-permute-start.12
  34.4 1.7 %collective-permute-done.12.refs_3_ = bf16[64,3200]{1,0:T(8,128)(2,1)S(1)} collective-permute-done((bf16[64,3200]{1,0:T(8,128)(2,1)S(1)}, bf16[64,3200]{1,0:T(8,128)(2,1)S(1)}, u32[]{:S(2)}, u32[]{:S(2)}) %collective-permute-start.12) | collective-permute-done | bytes 409632 | tf_op jit(solution)/shard_map/ppermute | solution.py:391
  36.2 5.2 %shard_map.72 = (bf16[256,2048]{1,0:T(8,128)(2,1)S(1)}, bf16[128,1536]{1,0:T(8,128)(2,1)S(1)}, bf16[128,1536]{1,0:T(8,128)(2,1)S(1)}) custom-call(s32[1]{0:T(128)} %bitcast.3.expert_ref, bf16[64,3200]{1,0:T(8,128)(2,1)S(1)} %shard_map.68.refs_0_, bf16[64,3200]{1,0:T(8,128)(2,1)S(1)} %shard_map.71.refs_1_, ...), custom_call_target="tpu_custom_call" | custom-call | tf_op jit(solution)/shard_map/pallas_call | solution.py:346
  41.4 0.2 collective-permute-start.13
  41.6 1.8 %shard_map.76 = (bf16[128,1536]{1,0:T(8,128)(2,1)S(1)}, bf16[128,1536]{1,0:T(8,128)(2,1)S(1)}) custom-call(bf16[256,2048]{1,0:T(8,128)(2,1)S(1)} %get-tuple-element.69.scaled_ref, bf16[3072,2048]{1,0:T(8,128)(2,1)S(1)} %shard_map.67.refs_2_.refs_6_.weight_ref), custom_call_target="tpu_custom_call" | custom-call | tf_op jit(solution)/shard_map/pallas_call | solution.py:379
  43.4 0.4 collective-permute-start.17
  43.9 0.1 shard_map.73
  44.0 1.6 %collective-permute-start.14 = (bf16[64,1536]{1,0:T(8,128)(2,1)S(1)}, bf16[64,1536]{1,0:T(8,128)(2,1)S(1)}, u32[]{:S(2)}, u32[]{:S(2)}) collective-permute-start(bf16[64,1536]{1,0:T(8,128)(2,1)S(1)} %get-tuple-element.65), channel_id=1, source_target_pairs={{0,2},{1,3},{2,0},{3,1},{4,6},{5,7},{6,4},{7,5},{8,10},{9,11},{10,... | collective-permute-start | bytes 589832 | tf_op jit(solution)/shard_map/ppermute | solution.py:391
  45.5 0.1 shard_map.77
  45.6 1.2 %collective-permute-start.18 = (bf16[64,1536]{1,0:T(8,128)(2,1)S(1)}, bf16[64,1536]{1,0:T(8,128)(2,1)S(1)}, u32[]{:S(2)}, u32[]{:S(2)}) collective-permute-start(bf16[64,1536]{1,0:T(8,128)(2,1)S(1)} %get-tuple-element.73), channel_id=1, source_target_pairs={{0,2},{1,3},{2,0},{3,1},{4,6},{5,7},{6,4},{7,5},{8,10},{9,11},{10,... | collective-permute-start | bytes 589832 | tf_op jit(solution)/shard_map/ppermute | solution.py:391
  46.9 4.9 %collective-permute-done.14.refs_1_ = bf16[64,1536]{1,0:T(8,128)(2,1)S(1)} collective-permute-done((bf16[64,1536]{1,0:T(8,128)(2,1)S(1)}, bf16[64,1536]{1,0:T(8,128)(2,1)S(1)}, u32[]{:S(2)}, u32[]{:S(2)}) %collective-permute-start.14) | collective-permute-done | bytes 196640 | tf_op jit(solution)/shard_map/ppermute | solution.py:391
  51.8 0.8 %collective-permute-start.15 = (bf16[16,1536]{1,0:T(8,128)(2,1)S(1)}, bf16[16,1536]{1,0:T(8,128)(2,1)S(1)}, u32[]{:S(2)}, u32[]{:S(2)}) collective-permute-start(bf16[16,1536]{1,0:T(8,128)(2,1)S(1)} %get-tuple-element.67), channel_id=1, source_target_pairs={{0,8},{4,12},{8,0},{12,4},{1,9},{5,13},{9,1},{13,5},{2,10},{6,14},... | collective-permute-start | bytes 147464 | tf_op jit(solution)/shard_map/ppermute | solution.py:391
  52.7 1.9 %collective-permute-start.16 = (bf16[16,1536]{1,0:T(8,128)(2,1)S(1)}, bf16[16,1536]{1,0:T(8,128)(2,1)S(1)}, u32[]{:S(2)}, u32[]{:S(2)}) collective-permute-start(bf16[16,1536]{1,0:T(8,128)(2,1)S(1)} %get-tuple-element.68), channel_id=1, source_target_pairs={{0,12},{4,8},{8,4},{12,0},{1,13},{5,9},{9,5},{13,1},{2,14},{6,10},... | collective-permute-start | bytes 147464 | tf_op jit(solution)/shard_map/ppermute | solution.py:391
  54.6 0.6 collective-permute-done.18.refs_1_
  55.2 0.8 %collective-permute-start.19 = (bf16[16,1536]{1,0:T(8,128)(2,1)S(1)}, bf16[16,1536]{1,0:T(8,128)(2,1)S(1)}, u32[]{:S(2)}, u32[]{:S(2)}) collective-permute-start(bf16[16,1536]{1,0:T(8,128)(2,1)S(1)} %get-tuple-element.76), channel_id=1, source_target_pairs={{0,8},{4,12},{8,0},{12,4},{1,9},{5,13},{9,1},{13,5},{2,10},{6,14},... | collective-permute-start | bytes 147464 | tf_op jit(solution)/shard_map/ppermute | solution.py:391
  56.1 1.9 %collective-permute-start.20 = (bf16[16,1536]{1,0:T(8,128)(2,1)S(1)}, bf16[16,1536]{1,0:T(8,128)(2,1)S(1)}, u32[]{:S(2)}, u32[]{:S(2)}) collective-permute-start(bf16[16,1536]{1,0:T(8,128)(2,1)S(1)} %get-tuple-element.77), channel_id=1, source_target_pairs={{0,12},{4,8},{8,4},{12,0},{1,13},{5,9},{9,5},{13,1},{2,14},{6,10},... | collective-permute-start | bytes 147464 | tf_op jit(solution)/shard_map/ppermute | solution.py:391
  58.0 0.8 %collective-permute-start.21 = (bf16[16,3072]{1,0:T(8,128)(2,1)S(1)}, bf16[16,3072]{1,0:T(8,128)(2,1)S(1)}, u32[]{:S(2)}, u32[]{:S(2)}) collective-permute-start(bf16[16,3072]{1,0:T(8,128)(2,1)S(1)} %get-tuple-element.78), channel_id=1, source_target_pairs={{0,4},{4,0},{8,12},{12,8},{1,5},{5,1},{9,13},{13,9},{2,6},{6,2},{1... | collective-permute-start | bytes 294920 | tf_op jit(solution)/shard_map/ppermute | solution.py:391
  58.8 0.2 collective-permute-done.16.refs_2_
  59.0 2.6 %collective-permute-done.19.refs_2_ = bf16[16,1536]{1,0:T(8,128)(2,1)S(1)} collective-permute-done((bf16[16,1536]{1,0:T(8,128)(2,1)S(1)}, bf16[16,1536]{1,0:T(8,128)(2,1)S(1)}, u32[]{:S(2)}, u32[]{:S(2)}) %collective-permute-start.19) | collective-permute-done | bytes 49184 | tf_op jit(solution)/shard_map/ppermute | solution.py:391
  61.6 0.7 %collective-permute-done.20.refs_3_ = bf16[16,1536]{1,0:T(8,128)(2,1)S(1)} collective-permute-done((bf16[16,1536]{1,0:T(8,128)(2,1)S(1)}, bf16[16,1536]{1,0:T(8,128)(2,1)S(1)}, u32[]{:S(2)}, u32[]{:S(2)}) %collective-permute-start.20) | collective-permute-done | bytes 49184 | tf_op jit(solution)/shard_map/ppermute | solution.py:391
  62.3 0.8 %collective-permute-done.21.refs_4_ = bf16[16,3072]{1,0:T(8,128)(2,1)S(1)} collective-permute-done((bf16[16,3072]{1,0:T(8,128)(2,1)S(1)}, bf16[16,3072]{1,0:T(8,128)(2,1)S(1)}, u32[]{:S(2)}, u32[]{:S(2)}) %collective-permute-start.21) | collective-permute-done | bytes 98336 | tf_op jit(solution)/shard_map/ppermute | solution.py:391
  63.1 0.7 %shard_map.79 = bf16[16,3072]{1,0:T(8,128)(2,1)} custom-call(bf16[16,1536]{1,0:T(8,128)(2,1)S(1)} %shard_map.75.refs_0_, bf16[16,1536]{1,0:T(8,128)(2,1)S(1)} %get-tuple-element.75.refs_1_, bf16[16,1536]{1,0:T(8,128)(2,1)S(1)} %collective-permute-done.19.refs_2_, bf16[16,1536]{1,0:T(8,128)(2,1)S(1)} %collective-permute-done.20.refs_3_, ...), custom_call_target="tpu_custom_call" | custom-call | tf_op jit(solution)/shard_map/pallas_call | solution.py:112
  (12 shorter events, 0.2 us)
Async XLA Ops:
  1.1 10.0 %collective-permute-start.5 = (bf16[16,6272]{1,0:T(8,128)(2,1)S(1)}, bf16[16,6272]{1,0:T(8,128)(2,1)S(1)}, u32[]{:S(2)}, u32[]{:S(2)}) collective-permute-start(bf16[16,6272]{1,0:T(8,128)(2,1)S(1)} %get-tuple-element.44.refs_0_), channel_id=1, source_target_pairs={{0,4},{4,0},{8,12},{12,8},{1,5},{5,1},{9,13},{13,9},{2,6},{6,2},{1... | collective-permute-start | bytes 602120 | tf_op jit(solution)/shard_map/ppermute | solution.py:391
  4.2 8.7 %collective-permute-start = (bf16[16,3072]{1,0:T(8,128)(2,1)}, bf16[16,3072]{1,0:T(8,128)(2,1)S(1)}, u32[]{:S(2)}, u32[]{:S(2)}) collective-permute-start(bf16[16,3072]{1,0:T(8,128)(2,1)} %tokens_ref.1), channel_id=1, source_target_pairs={{0,8},{4,12},{8,0},{12,4},{1,9},{5,13},{9,1},{13,5},{2,10},{6,14},... | collective-permute-start | bytes 294920 | tf_op jit(solution)/shard_map/ppermute | solution.py:391
  6.7 8.9 %collective-permute-start.1 = (bf16[16,3072]{1,0:T(8,128)(2,1)}, bf16[16,3072]{1,0:T(8,128)(2,1)S(1)}, u32[]{:S(2)}, u32[]{:S(2)}) collective-permute-start(bf16[16,3072]{1,0:T(8,128)(2,1)} %tokens_ref.1), channel_id=1, source_target_pairs={{0,12},{4,8},{8,4},{12,0},{1,13},{5,9},{9,5},{13,1},{2,14},{6,10},... | collective-permute-start | bytes 294920 | tf_op jit(solution)/shard_map/ppermute | solution.py:391
  6.8 8.9 %collective-permute-start.2 = (bf16[16,6272]{1,0:T(8,128)(2,1)S(1)}, bf16[16,6272]{1,0:T(8,128)(2,1)S(1)}, u32[]{:S(2)}, u32[]{:S(2)}) collective-permute-start(bf16[16,6272]{1,0:T(8,128)(2,1)S(1)} %get-tuple-element.44.refs_0_), channel_id=1, source_target_pairs={{0,2},{1,3},{2,0},{3,1},{4,6},{5,7},{6,4},{7,5},{8,10},{9,11},{10,... | collective-permute-start | bytes 602120 | tf_op jit(solution)/shard_map/ppermute | solution.py:391
  11.1 15.4 %collective-permute-start.6 = (bf16[16,6272]{1,0:T(8,128)(2,1)S(1)}, bf16[16,6272]{1,0:T(8,128)(2,1)S(1)}, u32[]{:S(2)}, u32[]{:S(2)}) collective-permute-start(bf16[16,6272]{1,0:T(8,128)(2,1)S(1)} %collective-permute-done.5.refs_2_.refs_3_), channel_id=1, source_target_pairs={{0,2},{1,3},{2,0},{3,1},{4,6},{5,7},{6,4},{7,5},{8,10},{9,11},{10,... | collective-permute-start | bytes 602120 | tf_op jit(solution)/shard_map/ppermute | solution.py:391
  15.7 9.7 %collective-permute-start.8 = (bf16[16,3200]{1,0:T(8,128)(2,1)S(1)}, bf16[16,3200]{1,0:T(8,128)(2,1)S(1)}, u32[]{:S(2)}, u32[]{:S(2)}) collective-permute-start(bf16[16,3200]{1,0:T(8,128)(2,1)S(1)} %get-tuple-element.49), channel_id=1, source_target_pairs={{0,12},{4,8},{8,4},{12,0},{1,13},{5,9},{9,5},{13,1},{2,14},{6,10},... | collective-permute-start | bytes 307208 | tf_op jit(solution)/shard_map/ppermute | solution.py:391
  17.7 8.8 %collective-permute-start.7 = (bf16[16,3200]{1,0:T(8,128)(2,1)S(1)}, bf16[16,3200]{1,0:T(8,128)(2,1)S(1)}, u32[]{:S(2)}, u32[]{:S(2)}) collective-permute-start(bf16[16,3200]{1,0:T(8,128)(2,1)S(1)} %get-tuple-element.49), channel_id=1, source_target_pairs={{0,8},{4,12},{8,0},{12,4},{1,9},{5,13},{9,1},{13,5},{2,10},{6,14},... | collective-permute-start | bytes 307208 | tf_op jit(solution)/shard_map/ppermute | solution.py:391
  18.7 7.8 %collective-permute-start.3 = (bf16[16,3072]{1,0:T(8,128)(2,1)S(1)}, bf16[16,3072]{1,0:T(8,128)(2,1)S(1)}, u32[]{:S(2)}, u32[]{:S(2)}) collective-permute-start(bf16[16,3072]{1,0:T(8,128)(2,1)S(1)} %get-tuple-element.47.refs_1_), channel_id=1, source_target_pairs={{0,2},{1,3},{2,0},{3,1},{4,6},{5,7},{6,4},{7,5},{8,10},{9,11},{10,... | collective-permute-start | bytes 294920 | tf_op jit(solution)/shard_map/ppermute | solution.py:391
  20.2 6.3 %collective-permute-start.4 = (bf16[16,3072]{1,0:T(8,128)(2,1)S(1)}, bf16[16,3072]{1,0:T(8,128)(2,1)S(1)}, u32[]{:S(2)}, u32[]{:S(2)}) collective-permute-start(bf16[16,3072]{1,0:T(8,128)(2,1)S(1)} %get-tuple-element.48.refs_2_), channel_id=1, source_target_pairs={{0,2},{1,3},{2,0},{3,1},{4,6},{5,7},{6,4},{7,5},{8,10},{9,11},{10,... | collective-permute-start | bytes 294920 | tf_op jit(solution)/shard_map/ppermute | solution.py:391
  26.6 2.4 %collective-permute-start.10 = (bf16[128,3072]{1,0:T(8,128)(2,1)S(1)}, bf16[128,3072]{1,0:T(8,128)(2,1)S(1)}, u32[]{:S(2)}, u32[]{:S(2)}) collective-permute-start(bf16[128,3072]{1,0:T(8,128)(2,1)S(1)} %shard_map.69.refs_0_), channel_id=1, source_target_pairs={{0,1},{1,0},{2,3},{3,2},{4,5},{5,4},{6,7},{7,6},{8,9},{9,8},{10,11... | collective-permute-start | bytes 2359304 | tf_op jit(solution)/shard_map/ppermute | solution.py:391
  26.7 7.6 %collective-permute-start.11 = (bf16[64,3200]{1,0:T(8,128)(2,1)S(1)}, bf16[64,3200]{1,0:T(8,128)(2,1)S(1)}, u32[]{:S(2)}, u32[]{:S(2)}) collective-permute-start(bf16[64,3200]{1,0:T(8,128)(2,1)S(1)} %shard_map.68.refs_0_), channel_id=1, source_target_pairs={{0,1},{1,0},{2,3},{3,2},{4,5},{5,4},{6,7},{7,6},{8,9},{9,8},{10,11... | collective-permute-start | bytes 1228808 | tf_op jit(solution)/shard_map/ppermute | solution.py:391
  27.3 7.1 %collective-permute-start.9 = (bf16[32,3200]{1,0:T(8,128)(2,1)S(1)}, bf16[32,3200]{1,0:T(8,128)(2,1)S(1)}, u32[]{:S(2)}, u32[]{:S(2)}) collective-permute-start(bf16[32,3200]{1,0:T(8,128)(2,1)S(1)} %shard_map.66.refs_1_), channel_id=1, source_target_pairs={{0,2},{1,3},{2,0},{3,1},{4,6},{5,7},{6,4},{7,5},{8,10},{9,11},{10,... | collective-permute-start | bytes 614408 | tf_op jit(solution)/shard_map/ppermute | solution.py:391
  34.4 1.8 %collective-permute-start.12 = (bf16[64,3200]{1,0:T(8,128)(2,1)S(1)}, bf16[64,3200]{1,0:T(8,128)(2,1)S(1)}, u32[]{:S(2)}, u32[]{:S(2)}) collective-permute-start(bf16[64,3200]{1,0:T(8,128)(2,1)S(1)} %shard_map.71.refs_1_), channel_id=1, source_target_pairs={{0,1},{1,0},{2,3},{3,2},{4,5},{5,4},{6,7},{7,6},{8,9},{9,8},{10,11... | collective-permute-start | bytes 1228808 | tf_op jit(solution)/shard_map/ppermute | solution.py:391
  41.4 2.5 %collective-permute-start.13 = (bf16[128,1536]{1,0:T(8,128)(2,1)S(1)}, bf16[128,1536]{1,0:T(8,128)(2,1)S(1)}, u32[]{:S(2)}, u32[]{:S(2)}) collective-permute-start(bf16[128,1536]{1,0:T(8,128)(2,1)S(1)} %get-tuple-element.63), channel_id=1, source_target_pairs={{0,1},{1,0},{2,3},{3,2},{4,5},{5,4},{6,7},{7,6},{8,9},{9,8},{10,11... | collective-permute-start | bytes 1179656 | tf_op jit(solution)/shard_map/ppermute | solution.py:391
  43.4 2.1 %collective-permute-start.17 = (bf16[128,1536]{1,0:T(8,128)(2,1)S(1)}, bf16[128,1536]{1,0:T(8,128)(2,1)S(1)}, u32[]{:S(2)}, u32[]{:S(2)}) collective-permute-start(bf16[128,1536]{1,0:T(8,128)(2,1)S(1)} %get-tuple-element.71), channel_id=1, source_target_pairs={{0,1},{1,0},{2,3},{3,2},{4,5},{5,4},{6,7},{7,6},{8,9},{9,8},{10,11... | collective-permute-start | bytes 1179656 | tf_op jit(solution)/shard_map/ppermute | solution.py:391
  44.0 7.8 %collective-permute-start.14 = (bf16[64,1536]{1,0:T(8,128)(2,1)S(1)}, bf16[64,1536]{1,0:T(8,128)(2,1)S(1)}, u32[]{:S(2)}, u32[]{:S(2)}) collective-permute-start(bf16[64,1536]{1,0:T(8,128)(2,1)S(1)} %get-tuple-element.65), channel_id=1, source_target_pairs={{0,2},{1,3},{2,0},{3,1},{4,6},{5,7},{6,4},{7,5},{8,10},{9,11},{10,... | collective-permute-start | bytes 589832 | tf_op jit(solution)/shard_map/ppermute | solution.py:391
  45.6 9.6 %collective-permute-start.18 = (bf16[64,1536]{1,0:T(8,128)(2,1)S(1)}, bf16[64,1536]{1,0:T(8,128)(2,1)S(1)}, u32[]{:S(2)}, u32[]{:S(2)}) collective-permute-start(bf16[64,1536]{1,0:T(8,128)(2,1)S(1)} %get-tuple-element.73), channel_id=1, source_target_pairs={{0,2},{1,3},{2,0},{3,1},{4,6},{5,7},{6,4},{7,5},{8,10},{9,11},{10,... | collective-permute-start | bytes 589832 | tf_op jit(solution)/shard_map/ppermute | solution.py:391
  51.8 7.0 %collective-permute-start.15 = (bf16[16,1536]{1,0:T(8,128)(2,1)S(1)}, bf16[16,1536]{1,0:T(8,128)(2,1)S(1)}, u32[]{:S(2)}, u32[]{:S(2)}) collective-permute-start(bf16[16,1536]{1,0:T(8,128)(2,1)S(1)} %get-tuple-element.67), channel_id=1, source_target_pairs={{0,8},{4,12},{8,0},{12,4},{1,9},{5,13},{9,1},{13,5},{2,10},{6,14},... | collective-permute-start | bytes 147464 | tf_op jit(solution)/shard_map/ppermute | solution.py:391
  52.7 6.3 %collective-permute-start.16 = (bf16[16,1536]{1,0:T(8,128)(2,1)S(1)}, bf16[16,1536]{1,0:T(8,128)(2,1)S(1)}, u32[]{:S(2)}, u32[]{:S(2)}) collective-permute-start(bf16[16,1536]{1,0:T(8,128)(2,1)S(1)} %get-tuple-element.68), channel_id=1, source_target_pairs={{0,12},{4,8},{8,4},{12,0},{1,13},{5,9},{9,5},{13,1},{2,14},{6,10},... | collective-permute-start | bytes 147464 | tf_op jit(solution)/shard_map/ppermute | solution.py:391
  55.2 6.4 %collective-permute-start.19 = (bf16[16,1536]{1,0:T(8,128)(2,1)S(1)}, bf16[16,1536]{1,0:T(8,128)(2,1)S(1)}, u32[]{:S(2)}, u32[]{:S(2)}) collective-permute-start(bf16[16,1536]{1,0:T(8,128)(2,1)S(1)} %get-tuple-element.76), channel_id=1, source_target_pairs={{0,8},{4,12},{8,0},{12,4},{1,9},{5,13},{9,1},{13,5},{2,10},{6,14},... | collective-permute-start | bytes 147464 | tf_op jit(solution)/shard_map/ppermute | solution.py:391
  56.1 6.2 %collective-permute-start.20 = (bf16[16,1536]{1,0:T(8,128)(2,1)S(1)}, bf16[16,1536]{1,0:T(8,128)(2,1)S(1)}, u32[]{:S(2)}, u32[]{:S(2)}) collective-permute-start(bf16[16,1536]{1,0:T(8,128)(2,1)S(1)} %get-tuple-element.77), channel_id=1, source_target_pairs={{0,12},{4,8},{8,4},{12,0},{1,13},{5,9},{9,5},{13,1},{2,14},{6,10},... | collective-permute-start | bytes 147464 | tf_op jit(solution)/shard_map/ppermute | solution.py:391
  58.0 5.1 %collective-permute-start.21 = (bf16[16,3072]{1,0:T(8,128)(2,1)S(1)}, bf16[16,3072]{1,0:T(8,128)(2,1)S(1)}, u32[]{:S(2)}, u32[]{:S(2)}) collective-permute-start(bf16[16,3072]{1,0:T(8,128)(2,1)S(1)} %get-tuple-element.78), channel_id=1, source_target_pairs={{0,4},{4,0},{8,12},{12,8},{1,5},{5,1},{9,13},{13,9},{2,6},{6,2},{1... | collective-permute-start | bytes 294920 | tf_op jit(solution)/shard_map/ppermute | solution.py:391

commit v5 on v4

--- a/solution.py
+++ b/solution.py
@@ -143,52 +143,56 @@
     return small_kernel(kernel, out_shape, arrays, cost)
 
 
-def added(terms, sizes, joined=None, cost=NO_COST):
+def parted(array, width, cost=NO_COST):
+    def kernel(array_ref, left_ref, right_ref):
+        left_ref[...] = array_ref[:, :width]
+        right_ref[...] = array_ref[:, width:]
+
+    rows, columns = array.shape
+    out_shape = [
+        jax.ShapeDtypeStruct((rows, width), jnp.bfloat16),
+        jax.ShapeDtypeStruct((rows, columns - width), jnp.bfloat16),
+    ]
+    return small_kernel(kernel, out_shape, [array], cost)
+
+
+def added(terms, sizes, sides=1):
     width = terms[0].shape[1]
-    widths = [width] * len(sizes)
-    if joined is not None:
-        widths[-1] += joined.shape[1]
+    half = sum(sizes)
 
     def kernel(*refs):
-        term_refs, out_refs = refs[: len(terms)], refs[-len(sizes) :]
+        term_refs, out_refs = refs[: len(terms)], refs[len(terms) :]
         start = 0
-        for out_ref in out_refs:
-            rows = pl.ds(start, out_ref.shape[0])
-            total = term_refs[0][rows, :].astype(jnp.float32)
-            for term_ref in term_refs[1:]:
-                total += term_ref[rows, :].astype(jnp.float32)
-            out_ref[:, out_ref.shape[1] - width :] = total.astype(jnp.bfloat16)
-            start += out_ref.shape[0]
-        if joined is not None:
-            out_refs[-1][:, : joined.shape[1]] = refs[len(terms)][...]
-
-    return small_kernel(
-        kernel,
-        [jax.ShapeDtypeStruct((size, wide), jnp.bfloat16) for size, wide in zip(sizes, widths)],
-        terms if joined is None else [*terms, joined],
-        cost,
-    )
-
-
-def added_beside(chunks, wide):
+        for size, out_ref in zip(sizes, out_refs):
+            for side in range(sides):
+                rows = pl.ds(side * half + start, size)
+                total = term_refs[0][rows, :].astype(jnp.float32)
+                for term_ref in term_refs[1:]:
+                    total += term_ref[rows, :].astype(jnp.float32)
+                out_ref[pl.ds(side * size, size), :] = total.astype(jnp.bfloat16)
+            start += size
+
+    out_shape = [jax.ShapeDtypeStruct((sides * size, width), jnp.bfloat16) for size in sizes]
+    return small_kernel(kernel, out_shape, terms)
+
+
+def added_beside(chunks):
     rows = chunks[0][0].shape[0]
     widths = [chunk[0].shape[1] for chunk in chunks]
     terms = [term for chunk in chunks for term in chunk]
 
     def kernel(*refs):
-        *term_refs, wide_ref, out_ref = refs
+        *term_refs, out_ref = refs
         start = 0
         for chunk, width in zip(chunks, widths):
             group, term_refs = term_refs[: len(chunk)], term_refs[len(chunk) :]
-            total = wide_ref[:, start : start + width].astype(jnp.float32)
-            for term_ref in group:
+            total = group[0][...].astype(jnp.float32)
+            for term_ref in group[1:]:
                 total += term_ref[...].astype(jnp.float32)
             out_ref[:, start : start + width] = total.astype(jnp.bfloat16)
             start += width
 
-    return small_kernel(
-        kernel, jax.ShapeDtypeStruct((rows, sum(widths)), jnp.bfloat16), [*terms, wide]
-    )
+    return small_kernel(kernel, jax.ShapeDtypeStruct((rows, sum(widths)), jnp.bfloat16), terms)
 
 
 def in_hbm(array):
@@ -391,16 +395,18 @@
     return lax.ppermute(array, axis, [(i, i ^ step) for i in range(size)])
 
 
-def scatter_rows(chunks, rows):
-    terms, near = [], None
-    for kept, sent in chunks:
-        kept, sent = added([kept, beside(sent, "tensor", 1)], [rows * EXPERTS] * 2)
-        kept, *sent, near = added(
-            [kept, beside(sent, "tensor", CORES)], [rows] * EXPERTS, near
-        )
-        terms.append([kept] + [beside(block, "expert", step) for step, block in zip(FAR, sent)])
-    terms[0] = added(terms[0], [rows], cost=LONG)
-    return added_beside(terms, beside(near, "expert", NEAR))
+def scatter_rows(wide, narrow, rows):
+    steps = (*FAR, NEAR)
+    kept, sent = wide
+    kept, sent = added([kept, beside(sent, "tensor", 1)], [rows * EXPERTS] * 2)
+    across = beside(sent, "tensor", CORES)
+    narrow_kept, narrow_sent = narrow
+    blocks = added([narrow_kept, beside(narrow_sent, "tensor", 1)], [rows] * EXPERTS, sides=2)
+    blocks = [blocks[0]] + [beside(block, "expert", step) for step, block in zip(steps, blocks[1:])]
+    wide_kept, *sent = added([kept, across], [rows] * EXPERTS)
+    wide_terms = [wide_kept] + [beside(block, "expert", step) for step, block in zip(steps, sent)]
+    narrow_kept, sent = added(blocks, [rows] * 2)
+    return added_beside([wide_terms, [narrow_kept, beside(sent, "tensor", CORES)]])
 
 
 def dense(tokens_in, out_grad, expert_ids, gate_probs, w_in, w_out):
@@ -412,36 +418,46 @@
     expert = lax.axis_index("expert").astype(jnp.int32).reshape(1)
     near = beside(both, "expert", NEAR)
     across = beside(both, "tensor", CORES)
-    far_tokens = passed(*[beside(tokens_in, "expert", step) for step in FAR], cost=LONG)
-    *far_tokens, across, grads, w_in, expert = together((*far_tokens, across, grads, w_in, expert))
+    far_tokens = stacked(*[beside(tokens_in, "expert", step) for step in FAR], cost=LONG)
+    far_tokens, across, grads, w_in, expert = together((far_tokens, across, grads, w_in, expert))
+    near_tokens, near_grads = parted(near, features)
     far_grads = stacked(*[beside(grads, "expert", step) for step in FAR])
-    *far_tokens_across, near_across, far_grads, held_in = together(
+    far_tokens_across, near_tokens_across, near_grads_across, far_grads, held_in = together(
         (
-            *[beside(tokens, "tensor", CORES) for tokens in far_tokens],
-            beside(near, "tensor", CORES),
+            beside(far_tokens, "tensor", CORES),
+            beside(near_tokens, "tensor", CORES),
+            beside(near_grads, "tensor", CORES),
             far_grads,
             prefetched(w_in, features),
         )
     )
     token_half = stacked(
-        both, *far_tokens, near, across, *far_tokens_across, near_across, width=features
+        both,
+        far_tokens,
+        near_tokens,
+        across,
+        far_tokens_across,
+        near_tokens_across,
+        width=features,
     )
     slope, held_out = slope_rows(
         [token_half, beside(token_half, "tensor", 1)], held_in, w_out, w_out.shape[0]
     )
-    grad_column = stacked(both, far_grads, near, width=grads.shape[1], offsets=[features, 0, features])
+    grad_column = stacked(
+        both, far_grads, near_grads, width=grads.shape[1], offsets=[features, 0, 0]
+    )
     far_grads_across, slope, grad_column_other = together(
         (beside(far_grads, "tensor", CORES), slope, beside(grad_column, "tensor", 1))
     )
     grad_across = stacked(
-        across, far_grads_across, near_across, width=grads.shape[1], offsets=[features, 0, features]
+        across, far_grads_across, near_grads_across, width=grads.shape[1], offsets=[features, 0, 0]
     )
     grad_pieces = [grad_column, grad_across, grad_column_other, beside(grad_across, "tensor", 1)]
-    count = features // 2
+    count = features * 5 // 8
     scaled, *halves = scaled_rows(
         grad_pieces, expert, held_out, slope, held_in, count
     )
-    return scatter_rows([halves, partial_rows(scaled, held_in, count)], local_rows)
+    return scatter_rows(halves, partial_rows(scaled, held_in, count), local_rows)
 
 
 def local(*args):

time: 64 us -> 61 us (0.953)
  waiting for transfers between devices: 19.1 us -> 16.7 us
  starting transfers between devices: 26.2 us -> 25.2 us
    ppermute x22 -> x23, waiting for transfers between devices: 19.1 us -> 16.7 us  [beside(): return lax.ppermute(array, axis, [(i, i ^ step) for i in range(size)])]
    ppermute x22 -> x23, starting transfers between devices: 26.2 us -> 25.2 us  [beside(): return lax.ppermute(array, axis, [(i, i ^ step) for i in range(size)])]
  transfers between devices with their start and end apart: 22 -> 23, of which waited for: 12 -> 10; matrix products, arithmetic and copies ran while one was open for 0% -> 0% of each run, Pallas kernels for 18% -> 20%
where the time goes in v5:
time: 61 us; the launch traced here: 60.8 us
  starting transfers between devices  25.2 us (41%)
  Pallas kernels  18.7 us (31%)
  waiting for transfers between devices  16.7 us (27%)
    ppermute x23, starting transfers between devices, beside(): return lax.ppermute(array, axis, [(i, i ^ step) for i in range(size)])  25.2 us
    ppermute x23, waiting for transfers between devices, beside(): return lax.ppermute(array, axis, [(i, i ^ step) for i in range(size)])  16.7 us
    pallas_call x1, Pallas kernels, scaled_rows(): pl.pallas_call(kernel, out_shape=[jax.ShapeDtypeStruct((rows, width), jnp...  5.74 us
    pallas_call x1, Pallas kernels, prefetched(): pl.pallas_call(kernel, out_shape=pltpu.VMEM((rows, weight.shape[1]), weig...  4.62 us
    pallas_call x1, Pallas kernels, slope_rows(): pl.pallas_call(kernel, out_shape=[jax.ShapeDtypeStruct((rows, width), jnp...  4.59 us
    pallas_call x1, Pallas kernels, partial_rows(): pl.pallas_call(kernel, out_shape=[half, half], in_specs=[whole_block()] *...  1.55 us
  transfers between devices with their start and end apart: 23, of which 10 were waited for; matrix products, arithmetic and copies ran while one was open for 0% of the time, Pallas kernels for 20%

profile of v5, /device:TPU:0, one launch (start us, length us, event | category | flops | bytes accessed | tf_op | source)
XLA Modules:
  0.0 60.8 jit_solution(5947874171051925767)
XLA Ops:
  0.0 4.0 %collective-permute-start = (bf16[16,3072]{1,0:T(8,128)(2,1)}, bf16[16,3072]{1,0:T(8,128)(2,1)S(1)}, u32[]{:S(2)}, u32[]{:S(2)}) collective-permute-start(bf16[16,3072]{1,0:T(8,128)(2,1)} %tokens_ref.1), channel_id=1, source_target_pairs={{0,8},{4,12},{8,0},{12,4},{1,9},{5,13},{9,1},{13,5},{2,10},{6,14},... | collective-permute-start | bytes 294920 | tf_op jit(solution)/shard_map/ppermute | solution.py:395
  4.0 1.3 %collective-permute-start.1 = (bf16[16,3072]{1,0:T(8,128)(2,1)}, bf16[16,3072]{1,0:T(8,128)(2,1)S(1)}, u32[]{:S(2)}, u32[]{:S(2)}) collective-permute-start(bf16[16,3072]{1,0:T(8,128)(2,1)} %tokens_ref.1), channel_id=1, source_target_pairs={{0,12},{4,8},{8,4},{12,0},{1,13},{5,9},{9,5},{13,1},{2,14},{6,10},... | collective-permute-start | bytes 294920 | tf_op jit(solution)/shard_map/ppermute | solution.py:395
  5.4 1.1 %shard_map.65 = (bf16[16,3200]{1,0:T(8,128)(2,1)S(1)}, bf16[16,6272]{1,0:T(8,128)(2,1)S(1)}) custom-call(bf16[16,3072]{1,0:T(8,128)(2,1)} %tokens_ref.1, bf16[16,3072]{1,0:T(8,128)(2,1)} %grads_ref.1, s32[2,16]{1,0:T(2,128)} %bitcast.7, bf16[2,16]{1,0:T(2,128)(2,1)} %bitcast.8), custom_call_target="tpu_custom_call" | custom-call | tf_op jit(solution)/shard_map/pallas_call | solution.py:241
  6.5 0.3 collective-permute-start.4
  6.8 1.5 %collective-permute-start.2 = (bf16[16,6272]{1,0:T(8,128)(2,1)S(1)}, bf16[16,6272]{1,0:T(8,128)(2,1)S(1)}, u32[]{:S(2)}, u32[]{:S(2)}) collective-permute-start(bf16[16,6272]{1,0:T(8,128)(2,1)S(1)} %get-tuple-element.41.refs_0_), channel_id=1, source_target_pairs={{0,2},{1,3},{2,0},{3,1},{4,6},{5,7},{6,4},{7,5},{8,10},{9,11},{10,... | collective-permute-start | bytes 602120 | tf_op jit(solution)/shard_map/ppermute | solution.py:395
  8.2 3.8 %collective-permute-done.refs_0_ = bf16[16,3072]{1,0:T(8,128)(2,1)S(1)} collective-permute-done((bf16[16,3072]{1,0:T(8,128)(2,1)}, bf16[16,3072]{1,0:T(8,128)(2,1)S(1)}, u32[]{:S(2)}, u32[]{:S(2)}) %collective-permute-start) | collective-permute-done | bytes 98336 | tf_op jit(solution)/shard_map/ppermute | solution.py:395
  12.1 0.0 collective-permute-done.1.refs_1_
  12.1 0.8 %collective-permute-done.2.refs_3_.refs_0_ = bf16[16,6272]{1,0:T(8,128)(2,1)S(1)} collective-permute-done((bf16[16,6272]{1,0:T(8,128)(2,1)S(1)}, bf16[16,6272]{1,0:T(8,128)(2,1)S(1)}, u32[]{:S(2)}, u32[]{:S(2)}) %collective-permute-start.2) | collective-permute-done | bytes 200736 | tf_op jit(solution)/shard_map/ppermute | solution.py:395
  12.9 1.5 %collective-permute-start.3 = (bf16[32,3072]{1,0:T(8,128)(2,1)S(1)}, bf16[32,3072]{1,0:T(8,128)(2,1)S(1)}, u32[]{:S(2)}, u32[]{:S(2)}) collective-permute-start(bf16[32,3072]{1,0:T(8,128)(2,1)S(1)} %shard_map.64.refs_1_), channel_id=1, source_target_pairs={{0,2},{1,3},{2,0},{3,1},{4,6},{5,7},{6,4},{7,5},{8,10},{9,11},{10,... | collective-permute-start | bytes 589832 | tf_op jit(solution)/shard_map/ppermute | solution.py:395
  14.4 2.6 %collective-permute-start.8 = (bf16[16,3200]{1,0:T(8,128)(2,1)S(1)}, bf16[16,3200]{1,0:T(8,128)(2,1)S(1)}, u32[]{:S(2)}, u32[]{:S(2)}) collective-permute-start(bf16[16,3200]{1,0:T(8,128)(2,1)S(1)} %get-tuple-element.47), channel_id=1, source_target_pairs={{0,12},{4,8},{8,4},{12,0},{1,13},{5,9},{9,5},{13,1},{2,14},{6,10},... | collective-permute-start | bytes 307208 | tf_op jit(solution)/shard_map/ppermute | solution.py:395
  17.1 0.6 collective-permute-start.7
  17.7 0.6 collective-permute-start.6
  18.3 1.5 %collective-permute-start.5 = (bf16[16,3072]{1,0:T(8,128)(2,1)S(1)}, bf16[16,3072]{1,0:T(8,128)(2,1)S(1)}, u32[]{:S(2)}, u32[]{:S(2)}) collective-permute-start(bf16[16,3072]{1,0:T(8,128)(2,1)S(1)} %get-tuple-element.45.refs_2_), channel_id=1, source_target_pairs={{0,2},{1,3},{2,0},{3,1},{4,6},{5,7},{6,4},{7,5},{8,10},{9,11},{10,... | collective-permute-start | bytes 294920 | tf_op jit(solution)/shard_map/ppermute | solution.py:395
  19.8 4.6 %shard_map.68.refs_2_.refs_6_.weight_ref = bf16[3072,2048]{1,0:T(8,128)(2,1)S(1)} custom-call(bf16[3072,2048]{1,0:T(8,128)(2,1)} %bitcast.5), custom_call_target="tpu_custom_call" | custom-call | tf_op jit(solution)/shard_map/pallas_call | solution.py:278
  24.4 1.5 %collective-permute-done.7.refs_0_ = bf16[16,3200]{1,0:T(8,128)(2,1)S(1)} collective-permute-done((bf16[16,3200]{1,0:T(8,128)(2,1)S(1)}, bf16[16,3200]{1,0:T(8,128)(2,1)S(1)}, u32[]{:S(2)}, u32[]{:S(2)}) %collective-permute-start.7) | collective-permute-done | bytes 102432 | tf_op jit(solution)/shard_map/ppermute | solution.py:395
  25.9 0.0 collective-permute-done.5.refs_5_
  25.9 0.0 collective-permute-done.6.refs_2_
  26.0 0.1 shard_map.70.refs_0_
  26.0 0.1 collective-permute-start.10
  26.1 0.6 collective-permute-start.11
  26.7 0.5 collective-permute-start.9
  27.2 1.1 %collective-permute-done.10.refs_1_ = bf16[128,3072]{1,0:T(8,128)(2,1)S(1)} collective-permute-done((bf16[128,3072]{1,0:T(8,128)(2,1)S(1)}, bf16[128,3072]{1,0:T(8,128)(2,1)S(1)}, u32[]{:S(2)}, u32[]{:S(2)}) %collective-permute-start.10) | collective-permute-done | bytes 786464 | tf_op jit(solution)/shard_map/ppermute | solution.py:395
  28.4 4.6 %shard_map.71 = (f32[256,2048]{1,0:T(8,128)S(1)}, bf16[2048,3072]{1,0:T(8,128)(2,1)S(1)}) custom-call(bf16[128,3072]{1,0:T(8,128)(2,1)S(1)} %shard_map.70.refs_0_, bf16[128,3072]{1,0:T(8,128)(2,1)S(1)} %collective-permute-done.10.refs_1_, bf16[3072,2048]{1,0:T(8,128)(2,1)S(1)} %shard_map.68.refs_2_.refs_6_.weight_ref, bf16[2048,3072]{1,0:T(8,128)(2,1)} %bitcast.6), custom_call_target="tpu_custom_call" | custom-call | tf_op jit(solution)/shard_map/pallas_call | solution.py:306
  33.0 0.8 %collective-permute-done.9.refs_1_ = bf16[32,3200]{1,0:T(8,128)(2,1)S(1)} collective-permute-done((bf16[32,3200]{1,0:T(8,128)(2,1)S(1)}, bf16[32,3200]{1,0:T(8,128)(2,1)S(1)}, u32[]{:S(2)}, u32[]{:S(2)}) %collective-permute-start.9) | collective-permute-done | bytes 204832 | tf_op jit(solution)/shard_map/ppermute | solution.py:395
  33.8 0.1 collective-permute-start.12
  33.9 1.7 %collective-permute-done.12.refs_3_ = bf16[64,3200]{1,0:T(8,128)(2,1)S(1)} collective-permute-done((bf16[64,3200]{1,0:T(8,128)(2,1)S(1)}, bf16[64,3200]{1,0:T(8,128)(2,1)S(1)}, u32[]{:S(2)}, u32[]{:S(2)}) %collective-permute-start.12) | collective-permute-done | bytes 409632 | tf_op jit(solution)/shard_map/ppermute | solution.py:395
  35.6 5.7 %shard_map.73 = (bf16[256,2048]{1,0:T(8,128)(2,1)S(1)}, bf16[128,1920]{1,0:T(8,128)(2,1)S(1)}, bf16[128,1920]{1,0:T(8,128)(2,1)S(1)}) custom-call(s32[1]{0:T(128)} %bitcast.3.expert_ref, bf16[64,3200]{1,0:T(8,128)(2,1)S(1)} %shard_map.69.refs_0_, bf16[64,3200]{1,0:T(8,128)(2,1)S(1)} %shard_map.72.refs_1_, ...), custom_call_target="tpu_custom_call" | custom-call | tf_op jit(solution)/shard_map/pallas_call | solution.py:350
  41.3 0.2 collective-permute-start.13
  41.5 1.6 %shard_map.76 = (bf16[128,1152]{1,0:T(8,128)(2,1)S(1)}, bf16[128,1152]{1,0:T(8,128)(2,1)S(1)}) custom-call(bf16[256,2048]{1,0:T(8,128)(2,1)S(1)} %get-tuple-element.68.scaled_ref, bf16[3072,2048]{1,0:T(8,128)(2,1)S(1)} %shard_map.68.refs_2_.refs_6_.weight_ref), custom_call_target="tpu_custom_call" | custom-call | tf_op jit(solution)/shard_map/pallas_call | solution.py:383
  43.1 0.4 collective-permute-start.18
  43.5 0.0 collective-permute-done.13.refs_1_
  43.6 0.1 shard_map.74
  43.7 0.6 collective-permute-start.14
  44.3 0.5 collective-permute-done.18.refs_1_
  44.8 0.1 shard_map.77
  44.8 1.9 %collective-permute-start.19 = (bf16[32,1152]{1,0:T(8,128)(2,1)S(1)}, bf16[32,1152]{1,0:T(8,128)(2,1)S(1)}, u32[]{:S(2)}, u32[]{:S(2)}) collective-permute-start(bf16[32,1152]{1,0:T(8,128)(2,1)S(1)} %get-tuple-element.72), channel_id=1, source_target_pairs={{0,8},{4,12},{8,0},{12,4},{1,9},{5,13},{9,1},{13,5},{2,10},{6,14},... | collective-permute-start | bytes 221192 | tf_op jit(solution)/shard_map/ppermute | solution.py:395
  46.7 1.7 %collective-permute-start.20 = (bf16[32,1152]{1,0:T(8,128)(2,1)S(1)}, bf16[32,1152]{1,0:T(8,128)(2,1)S(1)}, u32[]{:S(2)}, u32[]{:S(2)}) collective-permute-start(bf16[32,1152]{1,0:T(8,128)(2,1)S(1)} %get-tuple-element.73), channel_id=1, source_target_pairs={{0,12},{4,8},{8,4},{12,0},{1,13},{5,9},{9,5},{13,1},{2,14},{6,10},... | collective-permute-start | bytes 221192 | tf_op jit(solution)/shard_map/ppermute | solution.py:395
  48.4 0.5 collective-permute-start.21
  48.9 2.8 %collective-permute-done.14.refs_1_ = bf16[64,1920]{1,0:T(8,128)(2,1)S(1)} collective-permute-done((bf16[64,1920]{1,0:T(8,128)(2,1)S(1)}, bf16[64,1920]{1,0:T(8,128)(2,1)S(1)}, u32[]{:S(2)}, u32[]{:S(2)}) %collective-permute-start.14) | collective-permute-done | bytes 245792 | tf_op jit(solution)/shard_map/ppermute | solution.py:395
  51.7 0.1 shard_map.75
  51.8 1.4 %collective-permute-start.15 = (bf16[16,1920]{1,0:T(8,128)(2,1)S(1)}, bf16[16,1920]{1,0:T(8,128)(2,1)S(1)}, u32[]{:S(2)}, u32[]{:S(2)}) collective-permute-start(bf16[16,1920]{1,0:T(8,128)(2,1)S(1)} %get-tuple-element.65), channel_id=1, source_target_pairs={{0,8},{4,12},{8,0},{12,4},{1,9},{5,13},{9,1},{13,5},{2,10},{6,14},... | collective-permute-start | bytes 184328 | tf_op jit(solution)/shard_map/ppermute | solution.py:395
  53.2 2.2 %collective-permute-start.16 = (bf16[16,1920]{1,0:T(8,128)(2,1)S(1)}, bf16[16,1920]{1,0:T(8,128)(2,1)S(1)}, u32[]{:S(2)}, u32[]{:S(2)}) collective-permute-start(bf16[16,1920]{1,0:T(8,128)(2,1)S(1)} %get-tuple-element.66), channel_id=1, source_target_pairs={{0,12},{4,8},{8,4},{12,0},{1,13},{5,9},{9,5},{13,1},{2,14},{6,10},... | collective-permute-start | bytes 184328 | tf_op jit(solution)/shard_map/ppermute | solution.py:395
  55.4 0.0 collective-permute-done.19.refs_1_
  55.4 0.5 collective-permute-start.17
  55.9 0.6 collective-permute-start.22
  56.5 3.4 %collective-permute-done.22.refs_5_ = bf16[16,1152]{1,0:T(8,128)(2,1)S(1)} collective-permute-done((bf16[16,1152]{1,0:T(8,128)(2,1)S(1)}, bf16[16,1152]{1,0:T(8,128)(2,1)S(1)}, u32[]{:S(2)}, u32[]{:S(2)}) %collective-permute-start.22) | collective-permute-done | bytes 36896 | tf_op jit(solution)/shard_map/ppermute | solution.py:395
  60.0 0.1 collective-permute-done.17.refs_3_
  60.1 0.7 %shard_map.79 = bf16[16,3072]{1,0:T(8,128)(2,1)} custom-call(bf16[16,1920]{1,0:T(8,128)(2,1)S(1)} %get-tuple-element.64.refs_0_, bf16[16,1920]{1,0:T(8,128)(2,1)S(1)} %collective-permute-done.15.refs_1_, bf16[16,1920]{1,0:T(8,128)(2,1)S(1)} %collective-permute-done.16.refs_2_, bf16[16,1920]{1,0:T(8,128)(2,1)S(1)} %collective-permute-done.17.refs_3_, ...), custom_call_target="tpu_custom_call" | custom-call | tf_op jit(solution)/shard_map/pallas_call | solution.py:112
  (14 shorter events, 0.2 us)
Async XLA Ops:
  0.0 12.1 %collective-permute-start = (bf16[16,3072]{1,0:T(8,128)(2,1)}, bf16[16,3072]{1,0:T(8,128)(2,1)S(1)}, u32[]{:S(2)}, u32[]{:S(2)}) collective-permute-start(bf16[16,3072]{1,0:T(8,128)(2,1)} %tokens_ref.1), channel_id=1, source_target_pairs={{0,8},{4,12},{8,0},{12,4},{1,9},{5,13},{9,1},{13,5},{2,10},{6,14},... | collective-permute-start | bytes 294920 | tf_op jit(solution)/shard_map/ppermute | solution.py:395
  4.0 8.0 %collective-permute-start.1 = (bf16[16,3072]{1,0:T(8,128)(2,1)}, bf16[16,3072]{1,0:T(8,128)(2,1)S(1)}, u32[]{:S(2)}, u32[]{:S(2)}) collective-permute-start(bf16[16,3072]{1,0:T(8,128)(2,1)} %tokens_ref.1), channel_id=1, source_target_pairs={{0,12},{4,8},{8,4},{12,0},{1,13},{5,9},{9,5},{13,1},{2,14},{6,10},... | collective-permute-start | bytes 294920 | tf_op jit(solution)/shard_map/ppermute | solution.py:395
  6.5 11.2 %collective-permute-start.4 = (bf16[16,6272]{1,0:T(8,128)(2,1)S(1)}, bf16[16,6272]{1,0:T(8,128)(2,1)S(1)}, u32[]{:S(2)}, u32[]{:S(2)}) collective-permute-start(bf16[16,6272]{1,0:T(8,128)(2,1)S(1)} %get-tuple-element.41.refs_0_), channel_id=1, source_target_pairs={{0,4},{4,0},{8,12},{12,8},{1,5},{5,1},{9,13},{13,9},{2,6},{6,2},{1... | collective-permute-start | bytes 602120 | tf_op jit(solution)/shard_map/ppermute | solution.py:395
  6.8 6.2 %collective-permute-start.2 = (bf16[16,6272]{1,0:T(8,128)(2,1)S(1)}, bf16[16,6272]{1,0:T(8,128)(2,1)S(1)}, u32[]{:S(2)}, u32[]{:S(2)}) collective-permute-start(bf16[16,6272]{1,0:T(8,128)(2,1)S(1)} %get-tuple-element.41.refs_0_), channel_id=1, source_target_pairs={{0,2},{1,3},{2,0},{3,1},{4,6},{5,7},{6,4},{7,5},{8,10},{9,11},{10,... | collective-permute-start | bytes 602120 | tf_op jit(solution)/shard_map/ppermute | solution.py:395
  12.9 13.0 %collective-permute-start.3 = (bf16[32,3072]{1,0:T(8,128)(2,1)S(1)}, bf16[32,3072]{1,0:T(8,128)(2,1)S(1)}, u32[]{:S(2)}, u32[]{:S(2)}) collective-permute-start(bf16[32,3072]{1,0:T(8,128)(2,1)S(1)} %shard_map.64.refs_1_), channel_id=1, source_target_pairs={{0,2},{1,3},{2,0},{3,1},{4,6},{5,7},{6,4},{7,5},{8,10},{9,11},{10,... | collective-permute-start | bytes 589832 | tf_op jit(solution)/shard_map/ppermute | solution.py:395
  14.4 10.0 %collective-permute-start.8 = (bf16[16,3200]{1,0:T(8,128)(2,1)S(1)}, bf16[16,3200]{1,0:T(8,128)(2,1)S(1)}, u32[]{:S(2)}, u32[]{:S(2)}) collective-permute-start(bf16[16,3200]{1,0:T(8,128)(2,1)S(1)} %get-tuple-element.47), channel_id=1, source_target_pairs={{0,12},{4,8},{8,4},{12,0},{1,13},{5,9},{9,5},{13,1},{2,14},{6,10},... | collective-permute-start | bytes 307208 | tf_op jit(solution)/shard_map/ppermute | solution.py:395
  17.1 8.8 %collective-permute-start.7 = (bf16[16,3200]{1,0:T(8,128)(2,1)S(1)}, bf16[16,3200]{1,0:T(8,128)(2,1)S(1)}, u32[]{:S(2)}, u32[]{:S(2)}) collective-permute-start(bf16[16,3200]{1,0:T(8,128)(2,1)S(1)} %get-tuple-element.47), channel_id=1, source_target_pairs={{0,8},{4,12},{8,0},{12,4},{1,9},{5,13},{9,1},{13,5},{2,10},{6,14},... | collective-permute-start | bytes 307208 | tf_op jit(solution)/shard_map/ppermute | solution.py:395
  17.7 8.3 %collective-permute-start.6 = (bf16[16,3200]{1,0:T(8,128)(2,1)S(1)}, bf16[16,3200]{1,0:T(8,128)(2,1)S(1)}, u32[]{:S(2)}, u32[]{:S(2)}) collective-permute-start(bf16[16,3200]{1,0:T(8,128)(2,1)S(1)} %get-tuple-element.46.refs_2_), channel_id=1, source_target_pairs={{0,2},{1,3},{2,0},{3,1},{4,6},{5,7},{6,4},{7,5},{8,10},{9,11},{10,... | collective-permute-start | bytes 307208 | tf_op jit(solution)/shard_map/ppermute | solution.py:395
  18.3 7.7 %collective-permute-start.5 = (bf16[16,3072]{1,0:T(8,128)(2,1)S(1)}, bf16[16,3072]{1,0:T(8,128)(2,1)S(1)}, u32[]{:S(2)}, u32[]{:S(2)}) collective-permute-start(bf16[16,3072]{1,0:T(8,128)(2,1)S(1)} %get-tuple-element.45.refs_2_), channel_id=1, source_target_pairs={{0,2},{1,3},{2,0},{3,1},{4,6},{5,7},{6,4},{7,5},{8,10},{9,11},{10,... | collective-permute-start | bytes 294920 | tf_op jit(solution)/shard_map/ppermute | solution.py:395
  26.0 2.4 %collective-permute-start.10 = (bf16[128,3072]{1,0:T(8,128)(2,1)S(1)}, bf16[128,3072]{1,0:T(8,128)(2,1)S(1)}, u32[]{:S(2)}, u32[]{:S(2)}) collective-permute-start(bf16[128,3072]{1,0:T(8,128)(2,1)S(1)} %shard_map.70.refs_0_), channel_id=1, source_target_pairs={{0,1},{1,0},{2,3},{3,2},{4,5},{5,4},{6,7},{7,6},{8,9},{9,8},{10,11... | collective-permute-start | bytes 2359304 | tf_op jit(solution)/shard_map/ppermute | solution.py:395
  26.1 7.6 %collective-permute-start.11 = (bf16[64,3200]{1,0:T(8,128)(2,1)S(1)}, bf16[64,3200]{1,0:T(8,128)(2,1)S(1)}, u32[]{:S(2)}, u32[]{:S(2)}) collective-permute-start(bf16[64,3200]{1,0:T(8,128)(2,1)S(1)} %shard_map.69.refs_0_), channel_id=1, source_target_pairs={{0,1},{1,0},{2,3},{3,2},{4,5},{5,4},{6,7},{7,6},{8,9},{9,8},{10,11... | collective-permute-start | bytes 1228808 | tf_op jit(solution)/shard_map/ppermute | solution.py:395
  26.7 7.1 %collective-permute-start.9 = (bf16[32,3200]{1,0:T(8,128)(2,1)S(1)}, bf16[32,3200]{1,0:T(8,128)(2,1)S(1)}, u32[]{:S(2)}, u32[]{:S(2)}) collective-permute-start(bf16[32,3200]{1,0:T(8,128)(2,1)S(1)} %shard_map.67.refs_1_), channel_id=1, source_target_pairs={{0,2},{1,3},{2,0},{3,1},{4,6},{5,7},{6,4},{7,5},{8,10},{9,11},{10,... | collective-permute-start | bytes 614408 | tf_op jit(solution)/shard_map/ppermute | solution.py:395
  33.8 1.8 %collective-permute-start.12 = (bf16[64,3200]{1,0:T(8,128)(2,1)S(1)}, bf16[64,3200]{1,0:T(8,128)(2,1)S(1)}, u32[]{:S(2)}, u32[]{:S(2)}) collective-permute-start(bf16[64,3200]{1,0:T(8,128)(2,1)S(1)} %shard_map.72.refs_1_), channel_id=1, source_target_pairs={{0,1},{1,0},{2,3},{3,2},{4,5},{5,4},{6,7},{7,6},{8,9},{9,8},{10,11... | collective-permute-start | bytes 1228808 | tf_op jit(solution)/shard_map/ppermute | solution.py:395
  41.3 2.2 %collective-permute-start.13 = (bf16[128,1920]{1,0:T(8,128)(2,1)S(1)}, bf16[128,1920]{1,0:T(8,128)(2,1)S(1)}, u32[]{:S(2)}, u32[]{:S(2)}) collective-permute-start(bf16[128,1920]{1,0:T(8,128)(2,1)S(1)} %get-tuple-element.61), channel_id=1, source_target_pairs={{0,1},{1,0},{2,3},{3,2},{4,5},{5,4},{6,7},{7,6},{8,9},{9,8},{10,11... | collective-permute-start | bytes 1474568 | tf_op jit(solution)/shard_map/ppermute | solution.py:395
  43.1 1.7 %collective-permute-start.18 = (bf16[128,1152]{1,0:T(8,128)(2,1)S(1)}, bf16[128,1152]{1,0:T(8,128)(2,1)S(1)}, u32[]{:S(2)}, u32[]{:S(2)}) collective-permute-start(bf16[128,1152]{1,0:T(8,128)(2,1)S(1)} %get-tuple-element.70), channel_id=1, source_target_pairs={{0,1},{1,0},{2,3},{3,2},{4,5},{5,4},{6,7},{7,6},{8,9},{9,8},{10,11... | collective-permute-start | bytes 884744 | tf_op jit(solution)/shard_map/ppermute | solution.py:395
  43.7 8.1 %collective-permute-start.14 = (bf16[64,1920]{1,0:T(8,128)(2,1)S(1)}, bf16[64,1920]{1,0:T(8,128)(2,1)S(1)}, u32[]{:S(2)}, u32[]{:S(2)}) collective-permute-start(bf16[64,1920]{1,0:T(8,128)(2,1)S(1)} %get-tuple-element.63), channel_id=1, source_target_pairs={{0,2},{1,3},{2,0},{3,1},{4,6},{5,7},{6,4},{7,5},{8,10},{9,11},{10,... | collective-permute-start | bytes 737288 | tf_op jit(solution)/shard_map/ppermute | solution.py:395
  44.8 10.6 %collective-permute-start.19 = (bf16[32,1152]{1,0:T(8,128)(2,1)S(1)}, bf16[32,1152]{1,0:T(8,128)(2,1)S(1)}, u32[]{:S(2)}, u32[]{:S(2)}) collective-permute-start(bf16[32,1152]{1,0:T(8,128)(2,1)S(1)} %get-tuple-element.72), channel_id=1, source_target_pairs={{0,8},{4,12},{8,0},{12,4},{1,9},{5,13},{9,1},{13,5},{2,10},{6,14},... | collective-permute-start | bytes 221192 | tf_op jit(solution)/shard_map/ppermute | solution.py:395
  46.7 9.2 %collective-permute-start.20 = (bf16[32,1152]{1,0:T(8,128)(2,1)S(1)}, bf16[32,1152]{1,0:T(8,128)(2,1)S(1)}, u32[]{:S(2)}, u32[]{:S(2)}) collective-permute-start(bf16[32,1152]{1,0:T(8,128)(2,1)S(1)} %get-tuple-element.73), channel_id=1, source_target_pairs={{0,12},{4,8},{8,4},{12,0},{1,13},{5,9},{9,5},{13,1},{2,14},{6,10},... | collective-permute-start | bytes 221192 | tf_op jit(solution)/shard_map/ppermute | solution.py:395
  48.4 7.5 %collective-permute-start.21 = (bf16[32,1152]{1,0:T(8,128)(2,1)S(1)}, bf16[32,1152]{1,0:T(8,128)(2,1)S(1)}, u32[]{:S(2)}, u32[]{:S(2)}) collective-permute-start(bf16[32,1152]{1,0:T(8,128)(2,1)S(1)} %get-tuple-element.74), channel_id=1, source_target_pairs={{0,4},{4,0},{8,12},{12,8},{1,5},{5,1},{9,13},{13,9},{2,6},{6,2},{1... | collective-permute-start | bytes 221192 | tf_op jit(solution)/shard_map/ppermute | solution.py:395
  51.8 8.2 %collective-permute-start.15 = (bf16[16,1920]{1,0:T(8,128)(2,1)S(1)}, bf16[16,1920]{1,0:T(8,128)(2,1)S(1)}, u32[]{:S(2)}, u32[]{:S(2)}) collective-permute-start(bf16[16,1920]{1,0:T(8,128)(2,1)S(1)} %get-tuple-element.65), channel_id=1, source_target_pairs={{0,8},{4,12},{8,0},{12,4},{1,9},{5,13},{9,1},{13,5},{2,10},{6,14},... | collective-permute-start | bytes 184328 | tf_op jit(solution)/shard_map/ppermute | solution.py:395
  53.2 6.8 %collective-permute-start.16 = (bf16[16,1920]{1,0:T(8,128)(2,1)S(1)}, bf16[16,1920]{1,0:T(8,128)(2,1)S(1)}, u32[]{:S(2)}, u32[]{:S(2)}) collective-permute-start(bf16[16,1920]{1,0:T(8,128)(2,1)S(1)} %get-tuple-element.66), channel_id=1, source_target_pairs={{0,12},{4,8},{8,4},{12,0},{1,13},{5,9},{9,5},{13,1},{2,14},{6,10},... | collective-permute-start | bytes 184328 | tf_op jit(solution)/shard_map/ppermute | solution.py:395
  55.4 4.7 %collective-permute-start.17 = (bf16[16,1920]{1,0:T(8,128)(2,1)S(1)}, bf16[16,1920]{1,0:T(8,128)(2,1)S(1)}, u32[]{:S(2)}, u32[]{:S(2)}) collective-permute-start(bf16[16,1920]{1,0:T(8,128)(2,1)S(1)} %get-tuple-element.67), channel_id=1, source_target_pairs={{0,4},{4,0},{8,12},{12,8},{1,5},{5,1},{9,13},{13,9},{2,6},{6,2},{1... | collective-permute-start | bytes 184328 | tf_op jit(solution)/shard_map/ppermute | solution.py:395
  55.9 4.0 %collective-permute-start.22 = (bf16[16,1152]{1,0:T(8,128)(2,1)S(1)}, bf16[16,1152]{1,0:T(8,128)(2,1)S(1)}, u32[]{:S(2)}, u32[]{:S(2)}) collective-permute-start(bf16[16,1152]{1,0:T(8,128)(2,1)S(1)} %get-tuple-element.76), channel_id=1, source_target_pairs={{0,2},{1,3},{2,0},{3,1},{4,6},{5,7},{6,4},{7,5},{8,10},{9,11},{10,... | collective-permute-start | bytes 110600 | tf_op jit(solution)/shard_map/ppermute | solution.py:395

commit v6 on v5

--- a/solution.py
+++ b/solution.py
@@ -81,7 +81,7 @@
 
 CORES = 2
 EXPERTS = 4
-NEAR, FAR = 1, (2, 3)
+NEAR, FAR = 1, (3, 2)
 LANES = 128
 NT = (((1,), (1,)), ((), ()))
 VMEM_LIMIT = 10 * 2**20
@@ -416,41 +416,41 @@
 
     grads, both = with_gates(tokens_in, out_grad, expert_ids, gate_probs)
     expert = lax.axis_index("expert").astype(jnp.int32).reshape(1)
+    expert, w_in = together((expert, w_in))
     near = beside(both, "expert", NEAR)
     across = beside(both, "tensor", CORES)
-    far_tokens = stacked(*[beside(tokens_in, "expert", step) for step in FAR], cost=LONG)
-    far_tokens, across, grads, w_in, expert = together((far_tokens, across, grads, w_in, expert))
-    near_tokens, near_grads = parted(near, features)
+    far_tokens = passed(*[beside(tokens_in, "expert", step) for step in FAR], cost=LONG)
+    *far_tokens, across, grads, held_in, expert = together(
+        (*far_tokens, across, grads, prefetched(w_in, features), expert)
+    )
     far_grads = stacked(*[beside(grads, "expert", step) for step in FAR])
-    far_tokens_across, near_tokens_across, near_grads_across, far_grads, held_in = together(
+    *far_tokens_across, near_across, far_grads = together(
         (
-            beside(far_tokens, "tensor", CORES),
-            beside(near_tokens, "tensor", CORES),
-            beside(near_grads, "tensor", CORES),
+            *[beside(tokens, "tensor", CORES) for tokens in far_tokens],
+            beside(near, "tensor", CORES),
             far_grads,
-            prefetched(w_in, features),
         )
     )
     token_half = stacked(
         both,
-        far_tokens,
-        near_tokens,
+        *far_tokens,
+        near,
         across,
-        far_tokens_across,
-        near_tokens_across,
+        *far_tokens_across,
+        near_across,
         width=features,
     )
     slope, held_out = slope_rows(
         [token_half, beside(token_half, "tensor", 1)], held_in, w_out, w_out.shape[0]
     )
     grad_column = stacked(
-        both, far_grads, near_grads, width=grads.shape[1], offsets=[features, 0, 0]
+        both, far_grads, near, width=grads.shape[1], offsets=[features, 0, features]
     )
     far_grads_across, slope, grad_column_other = together(
         (beside(far_grads, "tensor", CORES), slope, beside(grad_column, "tensor", 1))
     )
     grad_across = stacked(
-        across, far_grads_across, near_grads_across, width=grads.shape[1], offsets=[features, 0, 0]
+        across, far_grads_across, near_across, width=grads.shape[1], offsets=[features, 0, features]
     )
     grad_pieces = [grad_column, grad_across, grad_column_other, beside(grad_across, "tensor", 1)]
     count = features * 5 // 8

time: 61 us -> 60 us (0.984)
  waiting for transfers between devices: 16.7 us -> 15.2 us
    ppermute x23, waiting for transfers between devices: 16.7 us -> 15.2 us  [beside(): return lax.ppermute(array, axis, [(i, i ^ step) for i in range(size)])]
  transfers between devices with their start and end apart: 23 -> 23, of which waited for: 10 -> 9; matrix products, arithmetic and copies ran while one was open for 0% -> 0% of each run, Pallas kernels for 20% -> 19%
where the time goes in v6:
time: 60 us; the launch traced here: 59.8 us
  starting transfers between devices  25.8 us (43%)
  Pallas kernels  18.7 us (31%)
  waiting for transfers between devices  15.2 us (25%)
    ppermute x23, starting transfers between devices, beside(): return lax.ppermute(array, axis, [(i, i ^ step) for i in range(size)])  25.8 us
    ppermute x23, waiting for transfers between devices, beside(): return lax.ppermute(array, axis, [(i, i ^ step) for i in range(size)])  15.2 us
    pallas_call x1, Pallas kernels, scaled_rows(): pl.pallas_call(kernel, out_shape=[jax.ShapeDtypeStruct((rows, width), jnp...  5.72 us
    pallas_call x1, Pallas kernels, prefetched(): pl.pallas_call(kernel, out_shape=pltpu.VMEM((rows, weight.shape[1]), weig...  4.62 us
    pallas_call x1, Pallas kernels, slope_rows(): pl.pallas_call(kernel, out_shape=[jax.ShapeDtypeStruct((rows, width), jnp...  4.6 us
    pallas_call x1, Pallas kernels, partial_rows(): pl.pallas_call(kernel, out_shape=[half, half], in_specs=[whole_block()] *...  1.55 us
  transfers between devices with their start and end apart: 23, of which 9 were waited for; matrix products, arithmetic and copies ran while one was open for 0% of the time, Pallas kernels for 19%

profile of v6, /device:TPU:0, one launch (start us, length us, event | category | flops | bytes accessed | tf_op | source)
XLA Modules:
  0.0 59.8 jit_solution(16035949492282573248)
XLA Ops:
  0.0 1.1 %shard_map.65 = (bf16[16,3200]{1,0:T(8,128)(2,1)S(1)}, bf16[16,6272]{1,0:T(8,128)(2,1)S(1)}) custom-call(bf16[16,3072]{1,0:T(8,128)(2,1)} %tokens_ref.1, bf16[16,3072]{1,0:T(8,128)(2,1)} %grads_ref.1, s32[2,16]{1,0:T(2,128)} %bitcast.7, bf16[2,16]{1,0:T(2,128)(2,1)} %bitcast.8), custom_call_target="tpu_custom_call" | custom-call | tf_op jit(solution)/shard_map/pallas_call | solution.py:241
  1.1 3.1 %collective-permute-start.5 = (bf16[16,6272]{1,0:T(8,128)(2,1)S(1)}, bf16[16,6272]{1,0:T(8,128)(2,1)S(1)}, u32[]{:S(2)}, u32[]{:S(2)}) collective-permute-start(bf16[16,6272]{1,0:T(8,128)(2,1)S(1)} %get-tuple-element.45.refs_0_), channel_id=1, source_target_pairs={{0,4},{4,0},{8,12},{12,8},{1,5},{5,1},{9,13},{13,9},{2,6},{6,2},{1... | collective-permute-start | bytes 602120 | tf_op jit(solution)/shard_map/ppermute | solution.py:395
  4.2 2.5 %collective-permute-start = (bf16[16,3072]{1,0:T(8,128)(2,1)}, bf16[16,3072]{1,0:T(8,128)(2,1)S(1)}, u32[]{:S(2)}, u32[]{:S(2)}) collective-permute-start(bf16[16,3072]{1,0:T(8,128)(2,1)} %tokens_ref.1), channel_id=1, source_target_pairs={{0,12},{4,8},{8,4},{12,0},{1,13},{5,9},{9,5},{13,1},{2,14},{6,10},... | collective-permute-start | bytes 294920 | tf_op jit(solution)/shard_map/ppermute | solution.py:395
  6.6 0.1 collective-permute-start.1
  6.8 1.5 %collective-permute-start.2 = (bf16[16,6272]{1,0:T(8,128)(2,1)S(1)}, bf16[16,6272]{1,0:T(8,128)(2,1)S(1)}, u32[]{:S(2)}, u32[]{:S(2)}) collective-permute-start(bf16[16,6272]{1,0:T(8,128)(2,1)S(1)} %get-tuple-element.45.refs_0_), channel_id=1, source_target_pairs={{0,2},{1,3},{2,0},{3,1},{4,6},{5,7},{6,4},{7,5},{8,10},{9,11},{10,... | collective-permute-start | bytes 602120 | tf_op jit(solution)/shard_map/ppermute | solution.py:395
  8.2 4.6 %shard_map.66.refs_2_.refs_6_.weight_ref = bf16[3072,2048]{1,0:T(8,128)(2,1)S(1)} custom-call(bf16[3072,2048]{1,0:T(8,128)(2,1)} %bitcast.5), custom_call_target="tpu_custom_call" | custom-call | tf_op jit(solution)/shard_map/pallas_call | solution.py:278
  12.9 0.0 collective-permute-done.5.refs_2_.refs_3_
  12.9 0.6 %collective-permute-start.6 = (bf16[16,6272]{1,0:T(8,128)(2,1)S(1)}, bf16[16,6272]{1,0:T(8,128)(2,1)S(1)}, u32[]{:S(2)}, u32[]{:S(2)}) collective-permute-start(bf16[16,6272]{1,0:T(8,128)(2,1)S(1)} %collective-permute-done.5.refs_2_.refs_3_), channel_id=1, source_target_pairs={{0,2},{1,3},{2,0},{3,1},{4,6},{5,7},{6,4},{7,5},{8,10},{9,11},{10,... | collective-permute-start | bytes 602120 | tf_op jit(solution)/shard_map/ppermute | solution.py:395
  13.5 1.1 %collective-permute-done.refs_0_ = bf16[16,3072]{1,0:T(8,128)(2,1)S(1)} collective-permute-done((bf16[16,3072]{1,0:T(8,128)(2,1)}, bf16[16,3072]{1,0:T(8,128)(2,1)S(1)}, u32[]{:S(2)}, u32[]{:S(2)}) %collective-permute-start) | collective-permute-done | bytes 98336 | tf_op jit(solution)/shard_map/ppermute | solution.py:395
  14.6 1.6 %collective-permute-done.1.refs_1_ = bf16[16,3072]{1,0:T(8,128)(2,1)S(1)} collective-permute-done((bf16[16,3072]{1,0:T(8,128)(2,1)}, bf16[16,3072]{1,0:T(8,128)(2,1)S(1)}, u32[]{:S(2)}, u32[]{:S(2)}) %collective-permute-start.1) | collective-permute-done | bytes 98336 | tf_op jit(solution)/shard_map/ppermute | solution.py:395
  16.2 0.0 collective-permute-done.2.refs_4_.refs_0_
  16.2 0.4 collective-permute-start.8
  16.6 2.1 %collective-permute-start.7 = (bf16[16,3200]{1,0:T(8,128)(2,1)S(1)}, bf16[16,3200]{1,0:T(8,128)(2,1)S(1)}, u32[]{:S(2)}, u32[]{:S(2)}) collective-permute-start(bf16[16,3200]{1,0:T(8,128)(2,1)S(1)} %get-tuple-element.52), channel_id=1, source_target_pairs={{0,12},{4,8},{8,4},{12,0},{1,13},{5,9},{9,5},{13,1},{2,14},{6,10},... | collective-permute-start | bytes 307208 | tf_op jit(solution)/shard_map/ppermute | solution.py:395
  18.7 1.5 %collective-permute-start.3 = (bf16[16,3072]{1,0:T(8,128)(2,1)S(1)}, bf16[16,3072]{1,0:T(8,128)(2,1)S(1)}, u32[]{:S(2)}, u32[]{:S(2)}) collective-permute-start(bf16[16,3072]{1,0:T(8,128)(2,1)S(1)} %get-tuple-element.50.refs_1_), channel_id=1, source_target_pairs={{0,2},{1,3},{2,0},{3,1},{4,6},{5,7},{6,4},{7,5},{8,10},{9,11},{10,... | collective-permute-start | bytes 294920 | tf_op jit(solution)/shard_map/ppermute | solution.py:395
  20.2 0.5 collective-permute-start.4
  20.7 3.5 %collective-permute-done.8.refs_1_ = bf16[16,3200]{1,0:T(8,128)(2,1)S(1)} collective-permute-done((bf16[16,3200]{1,0:T(8,128)(2,1)S(1)}, bf16[16,3200]{1,0:T(8,128)(2,1)S(1)}, u32[]{:S(2)}, u32[]{:S(2)}) %collective-permute-start.8) | collective-permute-done | bytes 102432 | tf_op jit(solution)/shard_map/ppermute | solution.py:395
  24.2 0.0 collective-permute-done.7.refs_0_
  24.2 0.6 collective-permute-done.4.refs_6_
  24.8 0.1 shard_map.69.refs_0_
  24.8 0.1 collective-permute-start.10
  25.0 0.6 collective-permute-start.11
  25.5 1.1 %collective-permute-start.9 = (bf16[32,3200]{1,0:T(8,128)(2,1)S(1)}, bf16[32,3200]{1,0:T(8,128)(2,1)S(1)}, u32[]{:S(2)}, u32[]{:S(2)}) collective-permute-start(bf16[32,3200]{1,0:T(8,128)(2,1)S(1)} %shard_map.67.refs_1_), channel_id=1, source_target_pairs={{0,2},{1,3},{2,0},{3,1},{4,6},{5,7},{6,4},{7,5},{8,10},{9,11},{10,... | collective-permute-start | bytes 614408 | tf_op jit(solution)/shard_map/ppermute | solution.py:395
  26.6 0.6 %collective-permute-done.10.refs_1_ = bf16[128,3072]{1,0:T(8,128)(2,1)S(1)} collective-permute-done((bf16[128,3072]{1,0:T(8,128)(2,1)S(1)}, bf16[128,3072]{1,0:T(8,128)(2,1)S(1)}, u32[]{:S(2)}, u32[]{:S(2)}) %collective-permute-start.10) | collective-permute-done | bytes 786464 | tf_op jit(solution)/shard_map/ppermute | solution.py:395
  27.2 4.6 %shard_map.70 = (f32[256,2048]{1,0:T(8,128)S(1)}, bf16[2048,3072]{1,0:T(8,128)(2,1)S(1)}) custom-call(bf16[128,3072]{1,0:T(8,128)(2,1)S(1)} %shard_map.69.refs_0_, bf16[128,3072]{1,0:T(8,128)(2,1)S(1)} %collective-permute-done.10.refs_1_, bf16[3072,2048]{1,0:T(8,128)(2,1)S(1)} %shard_map.66.refs_2_.refs_6_.weight_ref, bf16[2048,3072]{1,0:T(8,128)(2,1)} %bitcast.6), custom_call_target="tpu_custom_call" | custom-call | tf_op jit(solution)/shard_map/pallas_call | solution.py:306
  31.8 0.8 %collective-permute-done.9.refs_1_ = bf16[32,3200]{1,0:T(8,128)(2,1)S(1)} collective-permute-done((bf16[32,3200]{1,0:T(8,128)(2,1)S(1)}, bf16[32,3200]{1,0:T(8,128)(2,1)S(1)}, u32[]{:S(2)}, u32[]{:S(2)}) %collective-permute-start.9) | collective-permute-done | bytes 204832 | tf_op jit(solution)/shard_map/ppermute | solution.py:395
  32.6 0.0 collective-permute-done.11.refs_2_
  32.6 0.1 collective-permute-start.12
  32.7 1.7 %collective-permute-done.12.refs_3_ = bf16[64,3200]{1,0:T(8,128)(2,1)S(1)} collective-permute-done((bf16[64,3200]{1,0:T(8,128)(2,1)S(1)}, bf16[64,3200]{1,0:T(8,128)(2,1)S(1)}, u32[]{:S(2)}, u32[]{:S(2)}) %collective-permute-start.12) | collective-permute-done | bytes 409632 | tf_op jit(solution)/shard_map/ppermute | solution.py:395
  34.4 5.7 %shard_map.72 = (bf16[256,2048]{1,0:T(8,128)(2,1)S(1)}, bf16[128,1920]{1,0:T(8,128)(2,1)S(1)}, bf16[128,1920]{1,0:T(8,128)(2,1)S(1)}) custom-call(s32[1]{0:T(128)} %bitcast.2.expert_ref, bf16[64,3200]{1,0:T(8,128)(2,1)S(1)} %shard_map.68.refs_0_, bf16[64,3200]{1,0:T(8,128)(2,1)S(1)} %shard_map.71.refs_1_, ...), custom_call_target="tpu_custom_call" | custom-call | tf_op jit(solution)/shard_map/pallas_call | solution.py:350
  40.1 0.2 collective-permute-start.13
  40.4 1.6 %shard_map.75 = (bf16[128,1152]{1,0:T(8,128)(2,1)S(1)}, bf16[128,1152]{1,0:T(8,128)(2,1)S(1)}) custom-call(bf16[256,2048]{1,0:T(8,128)(2,1)S(1)} %get-tuple-element.72.scaled_ref, bf16[3072,2048]{1,0:T(8,128)(2,1)S(1)} %shard_map.66.refs_2_.refs_6_.weight_ref), custom_call_target="tpu_custom_call" | custom-call | tf_op jit(solution)/shard_map/pallas_call | solution.py:383
  41.9 0.4 collective-permute-start.18
  42.4 0.0 collective-permute-done.13.refs_1_
  42.4 0.1 shard_map.73
  42.5 1.1 %collective-permute-start.14 = (bf16[64,1920]{1,0:T(8,128)(2,1)S(1)}, bf16[64,1920]{1,0:T(8,128)(2,1)S(1)}, u32[]{:S(2)}, u32[]{:S(2)}) collective-permute-start(bf16[64,1920]{1,0:T(8,128)(2,1)S(1)} %get-tuple-element.67), channel_id=1, source_target_pairs={{0,2},{1,3},{2,0},{3,1},{4,6},{5,7},{6,4},{7,5},{8,10},{9,11},{10,... | collective-permute-start | bytes 737288 | tf_op jit(solution)/shard_map/ppermute | solution.py:395
  43.6 0.1 shard_map.76
  43.7 1.9 %collective-permute-start.19 = (bf16[32,1152]{1,0:T(8,128)(2,1)S(1)}, bf16[32,1152]{1,0:T(8,128)(2,1)S(1)}, u32[]{:S(2)}, u32[]{:S(2)}) collective-permute-start(bf16[32,1152]{1,0:T(8,128)(2,1)S(1)} %get-tuple-element.76), channel_id=1, source_target_pairs={{0,12},{4,8},{8,4},{12,0},{1,13},{5,9},{9,5},{13,1},{2,14},{6,10},... | collective-permute-start | bytes 221192 | tf_op jit(solution)/shard_map/ppermute | solution.py:395
  45.6 0.9 %collective-permute-start.20 = (bf16[32,1152]{1,0:T(8,128)(2,1)S(1)}, bf16[32,1152]{1,0:T(8,128)(2,1)S(1)}, u32[]{:S(2)}, u32[]{:S(2)}) collective-permute-start(bf16[32,1152]{1,0:T(8,128)(2,1)S(1)} %get-tuple-element.77), channel_id=1, source_target_pairs={{0,8},{4,12},{8,0},{12,4},{1,9},{5,13},{9,1},{13,5},{2,10},{6,14},... | collective-permute-start | bytes 221192 | tf_op jit(solution)/shard_map/ppermute | solution.py:395
  46.4 1.7 %collective-permute-start.21 = (bf16[32,1152]{1,0:T(8,128)(2,1)S(1)}, bf16[32,1152]{1,0:T(8,128)(2,1)S(1)}, u32[]{:S(2)}, u32[]{:S(2)}) collective-permute-start(bf16[32,1152]{1,0:T(8,128)(2,1)S(1)} %get-tuple-element.78), channel_id=1, source_target_pairs={{0,4},{4,0},{8,12},{12,8},{1,5},{5,1},{9,13},{13,9},{2,6},{6,2},{1... | collective-permute-start | bytes 221192 | tf_op jit(solution)/shard_map/ppermute | solution.py:395
  48.1 2.4 %collective-permute-done.14.refs_1_ = bf16[64,1920]{1,0:T(8,128)(2,1)S(1)} collective-permute-done((bf16[64,1920]{1,0:T(8,128)(2,1)S(1)}, bf16[64,1920]{1,0:T(8,128)(2,1)S(1)}, u32[]{:S(2)}, u32[]{:S(2)}) %collective-permute-start.14) | collective-permute-done | bytes 245792 | tf_op jit(solution)/shard_map/ppermute | solution.py:395
  50.5 0.1 shard_map.74
  50.6 1.8 %collective-permute-start.15 = (bf16[16,1920]{1,0:T(8,128)(2,1)S(1)}, bf16[16,1920]{1,0:T(8,128)(2,1)S(1)}, u32[]{:S(2)}, u32[]{:S(2)}) collective-permute-start(bf16[16,1920]{1,0:T(8,128)(2,1)S(1)} %get-tuple-element.69), channel_id=1, source_target_pairs={{0,12},{4,8},{8,4},{12,0},{1,13},{5,9},{9,5},{13,1},{2,14},{6,10},... | collective-permute-start | bytes 184328 | tf_op jit(solution)/shard_map/ppermute | solution.py:395
  52.4 0.8 %collective-permute-start.16 = (bf16[16,1920]{1,0:T(8,128)(2,1)S(1)}, bf16[16,1920]{1,0:T(8,128)(2,1)S(1)}, u32[]{:S(2)}, u32[]{:S(2)}) collective-permute-start(bf16[16,1920]{1,0:T(8,128)(2,1)S(1)} %get-tuple-element.70), channel_id=1, source_target_pairs={{0,8},{4,12},{8,0},{12,4},{1,9},{5,13},{9,1},{13,5},{2,10},{6,14},... | collective-permute-start | bytes 184328 | tf_op jit(solution)/shard_map/ppermute | solution.py:395
  53.2 0.0 collective-permute-done.19.refs_1_
  53.2 1.8 %collective-permute-start.17 = (bf16[16,1920]{1,0:T(8,128)(2,1)S(1)}, bf16[16,1920]{1,0:T(8,128)(2,1)S(1)}, u32[]{:S(2)}, u32[]{:S(2)}) collective-permute-start(bf16[16,1920]{1,0:T(8,128)(2,1)S(1)} %get-tuple-element.71), channel_id=1, source_target_pairs={{0,4},{4,0},{8,12},{12,8},{1,5},{5,1},{9,13},{13,9},{2,6},{6,2},{1... | collective-permute-start | bytes 184328 | tf_op jit(solution)/shard_map/ppermute | solution.py:395
  55.1 1.1 %collective-permute-start.22 = (bf16[16,1152]{1,0:T(8,128)(2,1)S(1)}, bf16[16,1152]{1,0:T(8,128)(2,1)S(1)}, u32[]{:S(2)}, u32[]{:S(2)}) collective-permute-start(bf16[16,1152]{1,0:T(8,128)(2,1)S(1)} %get-tuple-element.80), channel_id=1, source_target_pairs={{0,2},{1,3},{2,0},{3,1},{4,6},{5,7},{6,4},{7,5},{8,10},{9,11},{10,... | collective-permute-start | bytes 110600 | tf_op jit(solution)/shard_map/ppermute | solution.py:395
  56.2 2.9 %collective-permute-done.22.refs_5_ = bf16[16,1152]{1,0:T(8,128)(2,1)S(1)} collective-permute-done((bf16[16,1152]{1,0:T(8,128)(2,1)S(1)}, bf16[16,1152]{1,0:T(8,128)(2,1)S(1)}, u32[]{:S(2)}, u32[]{:S(2)}) %collective-permute-start.22) | collective-permute-done | bytes 36896 | tf_op jit(solution)/shard_map/ppermute | solution.py:395
  59.2 0.7 %shard_map.78 = bf16[16,3072]{1,0:T(8,128)(2,1)} custom-call(bf16[16,1920]{1,0:T(8,128)(2,1)S(1)} %get-tuple-element.68.refs_0_, bf16[16,1920]{1,0:T(8,128)(2,1)S(1)} %collective-permute-done.15.refs_1_, bf16[16,1920]{1,0:T(8,128)(2,1)S(1)} %collective-permute-done.16.refs_2_, bf16[16,1920]{1,0:T(8,128)(2,1)S(1)} %collective-permute-done.17.refs_3_, ...), custom_call_target="tpu_custom_call" | custom-call | tf_op jit(solution)/shard_map/pallas_call | solution.py:112
  (13 shorter events, 0.2 us)
Async XLA Ops:
  1.1 11.8 %collective-permute-start.5 = (bf16[16,6272]{1,0:T(8,128)(2,1)S(1)}, bf16[16,6272]{1,0:T(8,128)(2,1)S(1)}, u32[]{:S(2)}, u32[]{:S(2)}) collective-permute-start(bf16[16,6272]{1,0:T(8,128)(2,1)S(1)} %get-tuple-element.45.refs_0_), channel_id=1, source_target_pairs={{0,4},{4,0},{8,12},{12,8},{1,5},{5,1},{9,13},{13,9},{2,6},{6,2},{1... | collective-permute-start | bytes 602120 | tf_op jit(solution)/shard_map/ppermute | solution.py:395
  4.2 10.4 %collective-permute-start = (bf16[16,3072]{1,0:T(8,128)(2,1)}, bf16[16,3072]{1,0:T(8,128)(2,1)S(1)}, u32[]{:S(2)}, u32[]{:S(2)}) collective-permute-start(bf16[16,3072]{1,0:T(8,128)(2,1)} %tokens_ref.1), channel_id=1, source_target_pairs={{0,12},{4,8},{8,4},{12,0},{1,13},{5,9},{9,5},{13,1},{2,14},{6,10},... | collective-permute-start | bytes 294920 | tf_op jit(solution)/shard_map/ppermute | solution.py:395
  6.6 9.5 %collective-permute-start.1 = (bf16[16,3072]{1,0:T(8,128)(2,1)}, bf16[16,3072]{1,0:T(8,128)(2,1)S(1)}, u32[]{:S(2)}, u32[]{:S(2)}) collective-permute-start(bf16[16,3072]{1,0:T(8,128)(2,1)} %tokens_ref.1), channel_id=1, source_target_pairs={{0,8},{4,12},{8,0},{12,4},{1,9},{5,13},{9,1},{13,5},{2,10},{6,14},... | collective-permute-start | bytes 294920 | tf_op jit(solution)/shard_map/ppermute | solution.py:395
  6.8 9.4 %collective-permute-start.2 = (bf16[16,6272]{1,0:T(8,128)(2,1)S(1)}, bf16[16,6272]{1,0:T(8,128)(2,1)S(1)}, u32[]{:S(2)}, u32[]{:S(2)}) collective-permute-start(bf16[16,6272]{1,0:T(8,128)(2,1)S(1)} %get-tuple-element.45.refs_0_), channel_id=1, source_target_pairs={{0,2},{1,3},{2,0},{3,1},{4,6},{5,7},{6,4},{7,5},{8,10},{9,11},{10,... | collective-permute-start | bytes 602120 | tf_op jit(solution)/shard_map/ppermute | solution.py:395
  12.9 11.9 %collective-permute-start.6 = (bf16[16,6272]{1,0:T(8,128)(2,1)S(1)}, bf16[16,6272]{1,0:T(8,128)(2,1)S(1)}, u32[]{:S(2)}, u32[]{:S(2)}) collective-permute-start(bf16[16,6272]{1,0:T(8,128)(2,1)S(1)} %collective-permute-done.5.refs_2_.refs_3_), channel_id=1, source_target_pairs={{0,2},{1,3},{2,0},{3,1},{4,6},{5,7},{6,4},{7,5},{8,10},{9,11},{10,... | collective-permute-start | bytes 602120 | tf_op jit(solution)/shard_map/ppermute | solution.py:395
  16.2 8.0 %collective-permute-start.8 = (bf16[16,3200]{1,0:T(8,128)(2,1)S(1)}, bf16[16,3200]{1,0:T(8,128)(2,1)S(1)}, u32[]{:S(2)}, u32[]{:S(2)}) collective-permute-start(bf16[16,3200]{1,0:T(8,128)(2,1)S(1)} %get-tuple-element.52), channel_id=1, source_target_pairs={{0,8},{4,12},{8,0},{12,4},{1,9},{5,13},{9,1},{13,5},{2,10},{6,14},... | collective-permute-start | bytes 307208 | tf_op jit(solution)/shard_map/ppermute | solution.py:395
  16.6 7.6 %collective-permute-start.7 = (bf16[16,3200]{1,0:T(8,128)(2,1)S(1)}, bf16[16,3200]{1,0:T(8,128)(2,1)S(1)}, u32[]{:S(2)}, u32[]{:S(2)}) collective-permute-start(bf16[16,3200]{1,0:T(8,128)(2,1)S(1)} %get-tuple-element.52), channel_id=1, source_target_pairs={{0,12},{4,8},{8,4},{12,0},{1,13},{5,9},{9,5},{13,1},{2,14},{6,10},... | collective-permute-start | bytes 307208 | tf_op jit(solution)/shard_map/ppermute | solution.py:395
  18.7 5.5 %collective-permute-start.3 = (bf16[16,3072]{1,0:T(8,128)(2,1)S(1)}, bf16[16,3072]{1,0:T(8,128)(2,1)S(1)}, u32[]{:S(2)}, u32[]{:S(2)}) collective-permute-start(bf16[16,3072]{1,0:T(8,128)(2,1)S(1)} %get-tuple-element.50.refs_1_), channel_id=1, source_target_pairs={{0,2},{1,3},{2,0},{3,1},{4,6},{5,7},{6,4},{7,5},{8,10},{9,11},{10,... | collective-permute-start | bytes 294920 | tf_op jit(solution)/shard_map/ppermute | solution.py:395
  20.2 4.6 %collective-permute-start.4 = (bf16[16,3072]{1,0:T(8,128)(2,1)S(1)}, bf16[16,3072]{1,0:T(8,128)(2,1)S(1)}, u32[]{:S(2)}, u32[]{:S(2)}) collective-permute-start(bf16[16,3072]{1,0:T(8,128)(2,1)S(1)} %get-tuple-element.51.refs_2_), channel_id=1, source_target_pairs={{0,2},{1,3},{2,0},{3,1},{4,6},{5,7},{6,4},{7,5},{8,10},{9,11},{10,... | collective-permute-start | bytes 294920 | tf_op jit(solution)/shard_map/ppermute | solution.py:395
  24.8 2.4 %collective-permute-start.10 = (bf16[128,3072]{1,0:T(8,128)(2,1)S(1)}, bf16[128,3072]{1,0:T(8,128)(2,1)S(1)}, u32[]{:S(2)}, u32[]{:S(2)}) collective-permute-start(bf16[128,3072]{1,0:T(8,128)(2,1)S(1)} %shard_map.69.refs_0_), channel_id=1, source_target_pairs={{0,1},{1,0},{2,3},{3,2},{4,5},{5,4},{6,7},{7,6},{8,9},{9,8},{10,11... | collective-permute-start | bytes 2359304 | tf_op jit(solution)/shard_map/ppermute | solution.py:395
  25.0 7.6 %collective-permute-start.11 = (bf16[64,3200]{1,0:T(8,128)(2,1)S(1)}, bf16[64,3200]{1,0:T(8,128)(2,1)S(1)}, u32[]{:S(2)}, u32[]{:S(2)}) collective-permute-start(bf16[64,3200]{1,0:T(8,128)(2,1)S(1)} %shard_map.68.refs_0_), channel_id=1, source_target_pairs={{0,1},{1,0},{2,3},{3,2},{4,5},{5,4},{6,7},{7,6},{8,9},{9,8},{10,11... | collective-permute-start | bytes 1228808 | tf_op jit(solution)/shard_map/ppermute | solution.py:395
  25.5 7.1 %collective-permute-start.9 = (bf16[32,3200]{1,0:T(8,128)(2,1)S(1)}, bf16[32,3200]{1,0:T(8,128)(2,1)S(1)}, u32[]{:S(2)}, u32[]{:S(2)}) collective-permute-start(bf16[32,3200]{1,0:T(8,128)(2,1)S(1)} %shard_map.67.refs_1_), channel_id=1, source_target_pairs={{0,2},{1,3},{2,0},{3,1},{4,6},{5,7},{6,4},{7,5},{8,10},{9,11},{10,... | collective-permute-start | bytes 614408 | tf_op jit(solution)/shard_map/ppermute | solution.py:395
  32.6 1.8 %collective-permute-start.12 = (bf16[64,3200]{1,0:T(8,128)(2,1)S(1)}, bf16[64,3200]{1,0:T(8,128)(2,1)S(1)}, u32[]{:S(2)}, u32[]{:S(2)}) collective-permute-start(bf16[64,3200]{1,0:T(8,128)(2,1)S(1)} %shard_map.71.refs_1_), channel_id=1, source_target_pairs={{0,1},{1,0},{2,3},{3,2},{4,5},{5,4},{6,7},{7,6},{8,9},{9,8},{10,11... | collective-permute-start | bytes 1228808 | tf_op jit(solution)/shard_map/ppermute | solution.py:395
  40.1 2.2 %collective-permute-start.13 = (bf16[128,1920]{1,0:T(8,128)(2,1)S(1)}, bf16[128,1920]{1,0:T(8,128)(2,1)S(1)}, u32[]{:S(2)}, u32[]{:S(2)}) collective-permute-start(bf16[128,1920]{1,0:T(8,128)(2,1)S(1)} %get-tuple-element.65), channel_id=1, source_target_pairs={{0,1},{1,0},{2,3},{3,2},{4,5},{5,4},{6,7},{7,6},{8,9},{9,8},{10,11... | collective-permute-start | bytes 1474568 | tf_op jit(solution)/shard_map/ppermute | solution.py:395
  41.9 1.7 %collective-permute-start.18 = (bf16[128,1152]{1,0:T(8,128)(2,1)S(1)}, bf16[128,1152]{1,0:T(8,128)(2,1)S(1)}, u32[]{:S(2)}, u32[]{:S(2)}) collective-permute-start(bf16[128,1152]{1,0:T(8,128)(2,1)S(1)} %get-tuple-element.74), channel_id=1, source_target_pairs={{0,1},{1,0},{2,3},{3,2},{4,5},{5,4},{6,7},{7,6},{8,9},{9,8},{10,11... | collective-permute-start | bytes 884744 | tf_op jit(solution)/shard_map/ppermute | solution.py:395
  42.5 8.1 %collective-permute-start.14 = (bf16[64,1920]{1,0:T(8,128)(2,1)S(1)}, bf16[64,1920]{1,0:T(8,128)(2,1)S(1)}, u32[]{:S(2)}, u32[]{:S(2)}) collective-permute-start(bf16[64,1920]{1,0:T(8,128)(2,1)S(1)} %get-tuple-element.67), channel_id=1, source_target_pairs={{0,2},{1,3},{2,0},{3,1},{4,6},{5,7},{6,4},{7,5},{8,10},{9,11},{10,... | collective-permute-start | bytes 737288 | tf_op jit(solution)/shard_map/ppermute | solution.py:395
  43.7 9.6 %collective-permute-start.19 = (bf16[32,1152]{1,0:T(8,128)(2,1)S(1)}, bf16[32,1152]{1,0:T(8,128)(2,1)S(1)}, u32[]{:S(2)}, u32[]{:S(2)}) collective-permute-start(bf16[32,1152]{1,0:T(8,128)(2,1)S(1)} %get-tuple-element.76), channel_id=1, source_target_pairs={{0,12},{4,8},{8,4},{12,0},{1,13},{5,9},{9,5},{13,1},{2,14},{6,10},... | collective-permute-start | bytes 221192 | tf_op jit(solution)/shard_map/ppermute | solution.py:395
  45.6 9.5 %collective-permute-start.20 = (bf16[32,1152]{1,0:T(8,128)(2,1)S(1)}, bf16[32,1152]{1,0:T(8,128)(2,1)S(1)}, u32[]{:S(2)}, u32[]{:S(2)}) collective-permute-start(bf16[32,1152]{1,0:T(8,128)(2,1)S(1)} %get-tuple-element.77), channel_id=1, source_target_pairs={{0,8},{4,12},{8,0},{12,4},{1,9},{5,13},{9,1},{13,5},{2,10},{6,14},... | collective-permute-start | bytes 221192 | tf_op jit(solution)/shard_map/ppermute | solution.py:395
  46.4 8.7 %collective-permute-start.21 = (bf16[32,1152]{1,0:T(8,128)(2,1)S(1)}, bf16[32,1152]{1,0:T(8,128)(2,1)S(1)}, u32[]{:S(2)}, u32[]{:S(2)}) collective-permute-start(bf16[32,1152]{1,0:T(8,128)(2,1)S(1)} %get-tuple-element.78), channel_id=1, source_target_pairs={{0,4},{4,0},{8,12},{12,8},{1,5},{5,1},{9,13},{13,9},{2,6},{6,2},{1... | collective-permute-start | bytes 221192 | tf_op jit(solution)/shard_map/ppermute | solution.py:395
  50.6 8.5 %collective-permute-start.15 = (bf16[16,1920]{1,0:T(8,128)(2,1)S(1)}, bf16[16,1920]{1,0:T(8,128)(2,1)S(1)}, u32[]{:S(2)}, u32[]{:S(2)}) collective-permute-start(bf16[16,1920]{1,0:T(8,128)(2,1)S(1)} %get-tuple-element.69), channel_id=1, source_target_pairs={{0,12},{4,8},{8,4},{12,0},{1,13},{5,9},{9,5},{13,1},{2,14},{6,10},... | collective-permute-start | bytes 184328 | tf_op jit(solution)/shard_map/ppermute | solution.py:395
  52.4 6.7 %collective-permute-start.16 = (bf16[16,1920]{1,0:T(8,128)(2,1)S(1)}, bf16[16,1920]{1,0:T(8,128)(2,1)S(1)}, u32[]{:S(2)}, u32[]{:S(2)}) collective-permute-start(bf16[16,1920]{1,0:T(8,128)(2,1)S(1)} %get-tuple-element.70), channel_id=1, source_target_pairs={{0,8},{4,12},{8,0},{12,4},{1,9},{5,13},{9,1},{13,5},{2,10},{6,14},... | collective-permute-start | bytes 184328 | tf_op jit(solution)/shard_map/ppermute | solution.py:395
  53.2 5.9 %collective-permute-start.17 = (bf16[16,1920]{1,0:T(8,128)(2,1)S(1)}, bf16[16,1920]{1,0:T(8,128)(2,1)S(1)}, u32[]{:S(2)}, u32[]{:S(2)}) collective-permute-start(bf16[16,1920]{1,0:T(8,128)(2,1)S(1)} %get-tuple-element.71), channel_id=1, source_target_pairs={{0,4},{4,0},{8,12},{12,8},{1,5},{5,1},{9,13},{13,9},{2,6},{6,2},{1... | collective-permute-start | bytes 184328 | tf_op jit(solution)/shard_map/ppermute | solution.py:395
  55.1 4.0 %collective-permute-start.22 = (bf16[16,1152]{1,0:T(8,128)(2,1)S(1)}, bf16[16,1152]{1,0:T(8,128)(2,1)S(1)}, u32[]{:S(2)}, u32[]{:S(2)}) collective-permute-start(bf16[16,1152]{1,0:T(8,128)(2,1)S(1)} %get-tuple-element.80), channel_id=1, source_target_pairs={{0,2},{1,3},{2,0},{3,1},{4,6},{5,7},{6,4},{7,5},{8,10},{9,11},{10,... | collective-permute-start | bytes 110600 | tf_op jit(solution)/shard_map/ppermute | solution.py:395

commit v7 on v6

--- a/solution.py
+++ b/solution.py
@@ -81,8 +81,7 @@
 
 CORES = 2
 EXPERTS = 4
-NEAR, FAR = 1, (3, 2)
-LANES = 128
+NEAR, FAR = 1, (2, 3)
 NT = (((1,), (1,)), ((), ()))
 VMEM_LIMIT = 10 * 2**20
 NO_COST = pl.CostEstimate(flops=0, bytes_accessed=0, transcendentals=0)
@@ -141,19 +140,6 @@
 
     out_shape = [jax.ShapeDtypeStruct(array.shape, array.dtype) for array in arrays]
     return small_kernel(kernel, out_shape, arrays, cost)
-
-
-def parted(array, width, cost=NO_COST):
-    def kernel(array_ref, left_ref, right_ref):
-        left_ref[...] = array_ref[:, :width]
-        right_ref[...] = array_ref[:, width:]
-
-    rows, columns = array.shape
-    out_shape = [
-        jax.ShapeDtypeStruct((rows, width), jnp.bfloat16),
-        jax.ShapeDtypeStruct((rows, columns - width), jnp.bfloat16),
-    ]
-    return small_kernel(kernel, out_shape, [array], cost)
 
 
 def added(terms, sizes, sides=1):
@@ -203,57 +189,66 @@
     return pl.BlockSpec(memory_space=pltpu.HBM)
 
 
-def with_gates(tokens, grads, expert_ids, gate_probs):
+def gated_rows(tokens, grads, expert_ids, gate_probs, expert):
     rows, features = grads.shape
-
-    def kernel(tokens_ref, grads_ref, ids_ref, probs_ref, out_ref, both_ref, ids, probs, sems):
+    steps = (0, NEAR, *FAR)
+
+    def kernel(
+        expert_ref, tokens_ref, grads_ref, ids_ref, probs_ref, own_ref, near_ref, *refs
+    ):
+        far_refs, (held, ids, probs, sems) = refs[: len(FAR)], refs[len(FAR) :]
         copies = [
             pltpu.make_async_copy(source, target, sems.at[place])
             for place, (source, target) in enumerate(
                 (
+                    (grads_ref, held),
                     (ids_ref, ids),
                     (probs_ref, probs),
-                    (tokens_ref, both_ref.at[:, pl.ds(0, features)]),
-                    (grads_ref, both_ref.at[:, pl.ds(features, features)]),
-                    (grads_ref, out_ref.at[:, pl.ds(0, features)]),
+                    (tokens_ref, own_ref.at[:, pl.ds(0, features)]),
+                    (tokens_ref, near_ref.at[:, pl.ds(0, features)]),
                 )
             )
         ]
         for copy in copies:
             copy.start()
-        copies[0].wait()
-        copies[1].wait()
-        lane = lax.broadcasted_iota(jnp.int32, (rows, LANES), 1)
+        for copy in copies[:3]:
+            copy.wait()
         here = lax.broadcasted_iota(jnp.int32, (rows, rows), 0) == lax.broadcasted_iota(
             jnp.int32, (rows, rows), 1
         )
         upright = lambda row: jnp.sum(jnp.where(here, row, 0.0), axis=1, keepdims=True)
-        gates = jnp.zeros((rows, LANES), jnp.float32)
-        for k in range(ids.shape[0]):
-            named = upright(ids[k : k + 1, :].astype(jnp.float32)).astype(jnp.int32)
-            prob = upright(probs[k : k + 1, :].astype(jnp.float32))
-            gates += jnp.where(lane == named, prob, 0.0)
-        out_ref[:, features:] = gates.astype(jnp.bfloat16)
-        both_ref[:, 2 * features :] = gates.astype(jnp.bfloat16)
-        for copy in copies[2:]:
+        choices = range(ids.shape[0])
+        named = [upright(ids[k : k + 1, :].astype(jnp.float32)).astype(jnp.int32) for k in choices]
+        chosen = [upright(probs[k : k + 1, :].astype(jnp.float32)) for k in choices]
+        rows_grad = held[...].astype(jnp.float32)
+        places = (
+            own_ref.at[:, pl.ds(features, features)],
+            near_ref.at[:, pl.ds(features, features)],
+            *far_refs,
+        )
+        for step, place in zip(steps, places):
+            gate = jnp.zeros((rows, 1), jnp.float32)
+            for k in choices:
+                gate += jnp.where(named[k] == expert_ref[0] ^ step, chosen[k], 0.0)
+            place[...] = (gate * rows_grad).astype(jnp.bfloat16)
+        for copy in copies[3:]:
             copy.wait()
 
-    return pl.pallas_call(
-        kernel,
-        out_shape=[
-            jax.ShapeDtypeStruct((rows, features + LANES), jnp.bfloat16),
-            jax.ShapeDtypeStruct((rows, 2 * features + LANES), jnp.bfloat16),
-        ],
-        in_specs=[hbm_block()] * 4,
-        out_specs=[whole_block()] * 2,
+    wide = jax.ShapeDtypeStruct((rows, 2 * features), jnp.bfloat16)
+    return pl.pallas_call(
+        kernel,
+        out_shape=[wide, wide] + [jax.ShapeDtypeStruct((rows, features), jnp.bfloat16)] * len(FAR),
+        in_specs=[pl.BlockSpec(memory_space=pltpu.SMEM)] + [hbm_block()] * 4,
+        out_specs=[whole_block()] * (2 + len(FAR)),
         scratch_shapes=[
+            pltpu.VMEM((rows, features), jnp.bfloat16),
             pltpu.VMEM(expert_ids.shape[::-1], expert_ids.dtype),
             pltpu.VMEM(gate_probs.shape[::-1], gate_probs.dtype),
             pltpu.SemaphoreType.DMA((5,)),
         ],
         compiler_params=pltpu.CompilerParams(vmem_limit_bytes=VMEM_LIMIT),
         cost_estimate=NO_COST,
-    )(in_hbm(tokens), in_hbm(grads), in_hbm(expert_ids.T), in_hbm(gate_probs.T))
+    )(expert, in_hbm(tokens), in_hbm(grads), in_hbm(expert_ids.T), in_hbm(gate_probs.T))
 
 
 def streamed(source_ref, target_ref, sems, first, parts, axis=0):
@@ -320,28 +315,19 @@
     )(*pieces, in_vmem(weight), in_hbm(later))
 
 
-def scaled_rows(pieces, expert, weight, slope, back, count, tile=1024):
+def scaled_rows(pieces, weight, slope, back, count, tile=1024):
     rows, width = slope.shape
     features = weight.shape[1]
 
-    def kernel(expert_ref, *refs):
-        *piece_refs, weight_ref, slope_ref, back_ref, out_ref, kept_ref, sent_ref = refs[:-2]
-        rows_ref, gate_ref = refs[-2:]
+    def kernel(*refs):
+        *piece_refs, weight_ref, slope_ref, back_ref, out_ref, kept_ref, sent_ref, rows_ref = refs
         assemble(piece_refs, rows_ref)
-        start = 0
-        for piece in piece_refs:
-            gates = piece[:, features:].astype(jnp.float32)
-            lane = lax.broadcasted_iota(jnp.int32, gates.shape, 1)
-            gate_ref[pl.ds(start, piece.shape[0]), :] = jnp.sum(
-                jnp.where(lane == expert_ref[0], gates, 0.0), axis=1, keepdims=True
-            )
-            start += piece.shape[0]
         for start in range(0, width, tile):
             cols = pl.ds(start, tile)
             hidden_grad = lax.dot_general(
                 rows_ref[...], weight_ref[cols, :], NT, preferred_element_type=jnp.float32
             )
-            out_ref[:, cols] = (gate_ref[...] * hidden_grad * slope_ref[:, cols]).astype(
+            out_ref[:, cols] = (hidden_grad * slope_ref[:, cols]).astype(
                 jnp.bfloat16
             )
         partial_product(out_ref, back_ref, 0, (kept_ref, sent_ref))
@@ -350,15 +336,14 @@
     return pl.pallas_call(
         kernel,
         out_shape=[jax.ShapeDtypeStruct((rows, width), jnp.bfloat16), half, half],
-        in_specs=[pl.BlockSpec(memory_space=pltpu.SMEM)] + [whole_block()] * (len(pieces) + 3),
+        in_specs=[whole_block()] * (len(pieces) + 3),
         out_specs=[whole_block()] * 3,
         scratch_shapes=[
             pltpu.VMEM((rows, features), jnp.bfloat16),
-            pltpu.VMEM((rows, 1), jnp.float32),
         ],
         compiler_params=pltpu.CompilerParams(vmem_limit_bytes=VMEM_LIMIT),
         cost_estimate=NO_COST,
-    )(expert, *pieces, in_vmem(weight), slope, in_vmem(back))
+    )(*pieces, in_vmem(weight), slope, in_vmem(back))
 
 
 def partial_product(scaled_ref, weight_ref, first, out_refs):
@@ -414,16 +399,14 @@
     together = lax.optimization_barrier
     w_in, w_out = w_in[0], w_out[0]
 
-    grads, both = with_gates(tokens_in, out_grad, expert_ids, gate_probs)
     expert = lax.axis_index("expert").astype(jnp.int32).reshape(1)
-    expert, w_in = together((expert, w_in))
-    near = beside(both, "expert", NEAR)
+    both, both_near, *grads = gated_rows(tokens_in, out_grad, expert_ids, gate_probs, expert)
+    near = beside(both_near, "expert", NEAR)
     across = beside(both, "tensor", CORES)
     far_tokens = passed(*[beside(tokens_in, "expert", step) for step in FAR], cost=LONG)
-    *far_tokens, across, grads, held_in, expert = together(
-        (*far_tokens, across, grads, prefetched(w_in, features), expert)
-    )
-    far_grads = stacked(*[beside(grads, "expert", step) for step in FAR])
+    *values, held_in = together((*far_tokens, across, *grads, prefetched(w_in, features)))
+    far_tokens, across, grads = values[: len(FAR)], values[len(FAR)], values[len(FAR) + 1 :]
+    far_grads = stacked(*[beside(rows, "expert", step) for rows, step in zip(grads, FAR)])
     *far_tokens_across, near_across, far_grads = together(
         (
             *[beside(tokens, "tensor", CORES) for tokens in far_tokens],
@@ -444,18 +427,18 @@
         [token_half, beside(token_half, "tensor", 1)], held_in, w_out, w_out.shape[0]
     )
     grad_column = stacked(
-        both, far_grads, near, width=grads.shape[1], offsets=[features, 0, features]
+        both, far_grads, near, width=features, offsets=[features, 0, features]
     )
     far_grads_across, slope, grad_column_other = together(
         (beside(far_grads, "tensor", CORES), slope, beside(grad_column, "tensor", 1))
     )
     grad_across = stacked(
-        across, far_grads_across, near_across, width=grads.shape[1], offsets=[features, 0, features]
+        across, far_grads_across, near_across, width=features, offsets=[features, 0, features]
     )
     grad_pieces = [grad_column, grad_across, grad_column_other, beside(grad_across, "tensor", 1)]
     count = features * 5 // 8
     scaled, *halves = scaled_rows(
-        grad_pieces, expert, held_out, slope, held_in, count
+        grad_pieces, held_out, slope, held_in, count
     )
     return scatter_rows(halves, partial_rows(scaled, held_in, count), local_rows)
 

time: 60 us -> 59.6 us (level)
  starting transfers between devices: 25.8 us -> 25 us
    ppermute x23, starting transfers between devices: 25.8 us -> 25 us  [beside(): return lax.ppermute(array, axis, [(i, i ^ step) for i in range(size)])]
  transfers between devices with their start and end apart: 23 -> 23, of which waited for: 9 -> 11; matrix products, arithmetic and copies ran while one was open for 0% -> 0% of each run, Pallas kernels for 19% -> 19%
where the time goes in v7:
time: 59.6 us; the launch traced here: 59.4 us
  starting transfers between devices  25 us (42%)
  Pallas kernels  18.5 us (31%)
  waiting for transfers between devices  15.7 us (26%)
    ppermute x23, starting transfers between devices, beside(): return lax.ppermute(array, axis, [(i, i ^ step) for i in range(size)])  25 us
    ppermute x23, waiting for transfers between devices, beside(): return lax.ppermute(array, axis, [(i, i ^ step) for i in range(size)])  15.7 us
    pallas_call x1, Pallas kernels, scaled_rows(): pl.pallas_call(kernel, out_shape=[jax.ShapeDtypeStruct((rows, width), jnp...  5.61 us
    pallas_call x1, Pallas kernels, prefetched(): pl.pallas_call(kernel, out_shape=pltpu.VMEM((rows, weight.shape[1]), weig...  4.62 us
    pallas_call x1, Pallas kernels, slope_rows(): pl.pallas_call(kernel, out_shape=[jax.ShapeDtypeStruct((rows, width), jnp...  4.58 us
    pallas_call x1, Pallas kernels, partial_rows(): pl.pallas_call(kernel, out_shape=[half, half], in_specs=[whole_block()] *...  1.55 us
  transfers between devices with their start and end apart: 23, of which 11 were waited for; matrix products, arithmetic and copies ran while one was open for 0% of the time, Pallas kernels for 19%

profile of v7, /device:TPU:0, one launch (start us, length us, event | category | flops | bytes accessed | tf_op | source)
XLA Modules:
  0.0 59.4 jit_solution(1917014956524687988)
XLA Ops:
  0.0 1.1 %shard_map.64 = (bf16[16,6144]{1,0:T(8,128)(2,1)S(1)}, bf16[16,6144]{1,0:T(8,128)(2,1)S(1)}, bf16[16,3072]{1,0:T(8,128)(2,1)S(1)}, bf16[16,3072]{1,0:T(8,128)(2,1)S(1)}) custom-call(s32[1]{0:T(128)} %bitcast.expert_ref, bf16[16,3072]{1,0:T(8,128)(2,1)} %tokens_ref.1, bf16[16,3072]{1,0:T(8,128)(2,1)} %grads_ref.1, s32[2,16]{1,0:T(2,128)} %bitcast.7, ...), custom_call_target="tpu_custom_call" | custom-call | tf_op jit(solution)/shard_map/pallas_call | solution.py:238
  1.1 3.1 %collective-permute-start.5 = (bf16[16,6144]{1,0:T(8,128)(2,1)S(1)}, bf16[16,6144]{1,0:T(8,128)(2,1)S(1)}, u32[]{:S(2)}, u32[]{:S(2)}) collective-permute-start(bf16[16,6144]{1,0:T(8,128)(2,1)S(1)} %get-tuple-element.50), channel_id=1, source_target_pairs={{0,4},{4,0},{8,12},{12,8},{1,5},{5,1},{9,13},{13,9},{2,6},{6,2},{1... | collective-permute-start | bytes 589832 | tf_op jit(solution)/shard_map/ppermute | solution.py:380
  4.2 2.5 %collective-permute-start.1 = (bf16[16,3072]{1,0:T(8,128)(2,1)}, bf16[16,3072]{1,0:T(8,128)(2,1)S(1)}, u32[]{:S(2)}, u32[]{:S(2)}) collective-permute-start(bf16[16,3072]{1,0:T(8,128)(2,1)} %tokens_ref.1), channel_id=1, source_target_pairs={{0,12},{4,8},{8,4},{12,0},{1,13},{5,9},{9,5},{13,1},{2,14},{6,10},... | collective-permute-start | bytes 294920 | tf_op jit(solution)/shard_map/ppermute | solution.py:380
  6.6 0.1 collective-permute-start
  6.8 1.5 %collective-permute-start.2 = (bf16[16,6144]{1,0:T(8,128)(2,1)S(1)}, bf16[16,6144]{1,0:T(8,128)(2,1)S(1)}, u32[]{:S(2)}, u32[]{:S(2)}) collective-permute-start(bf16[16,6144]{1,0:T(8,128)(2,1)S(1)} %get-tuple-element.43.refs_0_), channel_id=1, source_target_pairs={{0,2},{1,3},{2,0},{3,1},{4,6},{5,7},{6,4},{7,5},{8,10},{9,11},{10,... | collective-permute-start | bytes 589832 | tf_op jit(solution)/shard_map/ppermute | solution.py:380
  8.3 4.6 %shard_map.66.refs_2_.refs_6_.weight_ref = bf16[3072,2048]{1,0:T(8,128)(2,1)S(1)} custom-call(bf16[3072,2048]{1,0:T(8,128)(2,1)} %bitcast.5), custom_call_target="tpu_custom_call" | custom-call | tf_op jit(solution)/shard_map/pallas_call | solution.py:273
  12.9 0.6 %collective-permute-start.6 = (bf16[16,6144]{1,0:T(8,128)(2,1)S(1)}, bf16[16,6144]{1,0:T(8,128)(2,1)S(1)}, u32[]{:S(2)}, u32[]{:S(2)}) collective-permute-start(bf16[16,6144]{1,0:T(8,128)(2,1)S(1)} %collective-permute-done.5.refs_2_.refs_3_), channel_id=1, source_target_pairs={{0,2},{1,3},{2,0},{3,1},{4,6},{5,7},{6,4},{7,5},{8,10},{9,11},{10,... | collective-permute-start | bytes 589832 | tf_op jit(solution)/shard_map/ppermute | solution.py:380
  13.5 1.0 %collective-permute-done.1.refs_1_ = bf16[16,3072]{1,0:T(8,128)(2,1)S(1)} collective-permute-done((bf16[16,3072]{1,0:T(8,128)(2,1)}, bf16[16,3072]{1,0:T(8,128)(2,1)S(1)}, u32[]{:S(2)}, u32[]{:S(2)}) %collective-permute-start.1) | collective-permute-done | bytes 98336 | tf_op jit(solution)/shard_map/ppermute | solution.py:380
  14.5 1.6 %collective-permute-done.refs_0_ = bf16[16,3072]{1,0:T(8,128)(2,1)S(1)} collective-permute-done((bf16[16,3072]{1,0:T(8,128)(2,1)}, bf16[16,3072]{1,0:T(8,128)(2,1)S(1)}, u32[]{:S(2)}, u32[]{:S(2)}) %collective-permute-start) | collective-permute-done | bytes 98336 | tf_op jit(solution)/shard_map/ppermute | solution.py:380
  16.1 0.5 collective-permute-start.7
  16.6 2.0 %collective-permute-start.8 = (bf16[16,3072]{1,0:T(8,128)(2,1)S(1)}, bf16[16,3072]{1,0:T(8,128)(2,1)S(1)}, u32[]{:S(2)}, u32[]{:S(2)}) collective-permute-start(bf16[16,3072]{1,0:T(8,128)(2,1)S(1)} %get-tuple-element.52), channel_id=1, source_target_pairs={{0,12},{4,8},{8,4},{12,0},{1,13},{5,9},{9,5},{13,1},{2,14},{6,10},... | collective-permute-start | bytes 294920 | tf_op jit(solution)/shard_map/ppermute | solution.py:380
  18.6 1.5 %collective-permute-start.3 = (bf16[16,3072]{1,0:T(8,128)(2,1)S(1)}, bf16[16,3072]{1,0:T(8,128)(2,1)S(1)}, u32[]{:S(2)}, u32[]{:S(2)}) collective-permute-start(bf16[16,3072]{1,0:T(8,128)(2,1)S(1)} %get-tuple-element.48.refs_1_), channel_id=1, source_target_pairs={{0,2},{1,3},{2,0},{3,1},{4,6},{5,7},{6,4},{7,5},{8,10},{9,11},{10,... | collective-permute-start | bytes 294920 | tf_op jit(solution)/shard_map/ppermute | solution.py:380
  20.1 0.5 collective-permute-start.4
  20.6 3.6 %collective-permute-done.7.refs_0_ = bf16[16,3072]{1,0:T(8,128)(2,1)S(1)} collective-permute-done((bf16[16,3072]{1,0:T(8,128)(2,1)S(1)}, bf16[16,3072]{1,0:T(8,128)(2,1)S(1)}, u32[]{:S(2)}, u32[]{:S(2)}) %collective-permute-start.7) | collective-permute-done | bytes 98336 | tf_op jit(solution)/shard_map/ppermute | solution.py:380
  24.3 0.5 collective-permute-done.4.refs_6_
  24.7 0.0 collective-permute-done.6.refs_7_.refs_2_
  24.7 0.1 shard_map.69.refs_0_
  24.8 0.1 collective-permute-start.10
  24.9 0.6 collective-permute-start.11
  25.5 1.1 %collective-permute-start.9 = (bf16[32,3072]{1,0:T(8,128)(2,1)S(1)}, bf16[32,3072]{1,0:T(8,128)(2,1)S(1)}, u32[]{:S(2)}, u32[]{:S(2)}) collective-permute-start(bf16[32,3072]{1,0:T(8,128)(2,1)S(1)} %shard_map.67.refs_1_), channel_id=1, source_target_pairs={{0,2},{1,3},{2,0},{3,1},{4,6},{5,7},{6,4},{7,5},{8,10},{9,11},{10,... | collective-permute-start | bytes 589832 | tf_op jit(solution)/shard_map/ppermute | solution.py:380
  26.5 0.6 %collective-permute-done.10.refs_1_ = bf16[128,3072]{1,0:T(8,128)(2,1)S(1)} collective-permute-done((bf16[128,3072]{1,0:T(8,128)(2,1)S(1)}, bf16[128,3072]{1,0:T(8,128)(2,1)S(1)}, u32[]{:S(2)}, u32[]{:S(2)}) %collective-permute-start.10) | collective-permute-done | bytes 786464 | tf_op jit(solution)/shard_map/ppermute | solution.py:380
  27.1 4.6 %shard_map.70 = (f32[256,2048]{1,0:T(8,128)S(1)}, bf16[2048,3072]{1,0:T(8,128)(2,1)S(1)}) custom-call(bf16[128,3072]{1,0:T(8,128)(2,1)S(1)} %shard_map.69.refs_0_, bf16[128,3072]{1,0:T(8,128)(2,1)S(1)} %collective-permute-done.10.refs_1_, bf16[3072,2048]{1,0:T(8,128)(2,1)S(1)} %shard_map.66.refs_2_.refs_6_.weight_ref, bf16[2048,3072]{1,0:T(8,128)(2,1)} %bitcast.6), custom_call_target="tpu_custom_call" | custom-call | tf_op jit(solution)/shard_map/pallas_call | solution.py:301
  31.7 0.6 %collective-permute-done.9.refs_1_ = bf16[32,3072]{1,0:T(8,128)(2,1)S(1)} collective-permute-done((bf16[32,3072]{1,0:T(8,128)(2,1)S(1)}, bf16[32,3072]{1,0:T(8,128)(2,1)S(1)}, u32[]{:S(2)}, u32[]{:S(2)}) %collective-permute-start.9) | collective-permute-done | bytes 196640 | tf_op jit(solution)/shard_map/ppermute | solution.py:380
  32.3 0.0 collective-permute-done.11.refs_2_
  32.4 0.1 collective-permute-start.12
  32.5 1.7 %collective-permute-done.12.refs_3_ = bf16[64,3072]{1,0:T(8,128)(2,1)S(1)} collective-permute-done((bf16[64,3072]{1,0:T(8,128)(2,1)S(1)}, bf16[64,3072]{1,0:T(8,128)(2,1)S(1)}, u32[]{:S(2)}, u32[]{:S(2)}) %collective-permute-start.12) | collective-permute-done | bytes 393248 | tf_op jit(solution)/shard_map/ppermute | solution.py:380
  34.2 5.6 %shard_map.72 = (bf16[256,2048]{1,0:T(8,128)(2,1)S(1)}, bf16[128,1920]{1,0:T(8,128)(2,1)S(1)}, bf16[128,1920]{1,0:T(8,128)(2,1)S(1)}) custom-call(bf16[64,3072]{1,0:T(8,128)(2,1)S(1)} %shard_map.68.refs_0_, bf16[64,3072]{1,0:T(8,128)(2,1)S(1)} %shard_map.71.refs_1_, bf16[64,3072]{1,0:T(8,128)(2,1)S(1)} %collective-permute-done.11.refs_2_, ...), custom_call_target="tpu_custom_call" | custom-call | tf_op jit(solution)/shard_map/pallas_call | solution.py:336
  39.8 0.2 collective-permute-start.13
  40.0 1.5 %shard_map.75 = (bf16[128,1152]{1,0:T(8,128)(2,1)S(1)}, bf16[128,1152]{1,0:T(8,128)(2,1)S(1)}) custom-call(bf16[256,2048]{1,0:T(8,128)(2,1)S(1)} %get-tuple-element.72.scaled_ref, bf16[3072,2048]{1,0:T(8,128)(2,1)S(1)} %shard_map.66.refs_2_.refs_6_.weight_ref), custom_call_target="tpu_custom_call" | custom-call | tf_op jit(solution)/shard_map/pallas_call | solution.py:368
  41.5 0.4 collective-permute-start.18
  42.0 0.1 shard_map.73
  42.1 1.1 %collective-permute-start.14 = (bf16[64,1920]{1,0:T(8,128)(2,1)S(1)}, bf16[64,1920]{1,0:T(8,128)(2,1)S(1)}, u32[]{:S(2)}, u32[]{:S(2)}) collective-permute-start(bf16[64,1920]{1,0:T(8,128)(2,1)S(1)} %get-tuple-element.67), channel_id=1, source_target_pairs={{0,2},{1,3},{2,0},{3,1},{4,6},{5,7},{6,4},{7,5},{8,10},{9,11},{10,... | collective-permute-start | bytes 737288 | tf_op jit(solution)/shard_map/ppermute | solution.py:380
  43.2 0.0 collective-permute-done.18.refs_1_
  43.2 0.1 shard_map.76
  43.3 2.7 %collective-permute-start.19 = (bf16[32,1152]{1,0:T(8,128)(2,1)S(1)}, bf16[32,1152]{1,0:T(8,128)(2,1)S(1)}, u32[]{:S(2)}, u32[]{:S(2)}) collective-permute-start(bf16[32,1152]{1,0:T(8,128)(2,1)S(1)} %get-tuple-element.76), channel_id=1, source_target_pairs={{0,8},{4,12},{8,0},{12,4},{1,9},{5,13},{9,1},{13,5},{2,10},{6,14},... | collective-permute-start | bytes 221192 | tf_op jit(solution)/shard_map/ppermute | solution.py:380
  46.0 1.3 %collective-permute-start.20 = (bf16[32,1152]{1,0:T(8,128)(2,1)S(1)}, bf16[32,1152]{1,0:T(8,128)(2,1)S(1)}, u32[]{:S(2)}, u32[]{:S(2)}) collective-permute-start(bf16[32,1152]{1,0:T(8,128)(2,1)S(1)} %get-tuple-element.77), channel_id=1, source_target_pairs={{0,12},{4,8},{8,4},{12,0},{1,13},{5,9},{9,5},{13,1},{2,14},{6,10},... | collective-permute-start | bytes 221192 | tf_op jit(solution)/shard_map/ppermute | solution.py:380
  47.3 2.8 %collective-permute-done.14.refs_1_ = bf16[64,1920]{1,0:T(8,128)(2,1)S(1)} collective-permute-done((bf16[64,1920]{1,0:T(8,128)(2,1)S(1)}, bf16[64,1920]{1,0:T(8,128)(2,1)S(1)}, u32[]{:S(2)}, u32[]{:S(2)}) %collective-permute-start.14) | collective-permute-done | bytes 245792 | tf_op jit(solution)/shard_map/ppermute | solution.py:380
  50.2 0.1 shard_map.74
  50.2 2.2 %collective-permute-start.15 = (bf16[16,1920]{1,0:T(8,128)(2,1)S(1)}, bf16[16,1920]{1,0:T(8,128)(2,1)S(1)}, u32[]{:S(2)}, u32[]{:S(2)}) collective-permute-start(bf16[16,1920]{1,0:T(8,128)(2,1)S(1)} %get-tuple-element.69), channel_id=1, source_target_pairs={{0,8},{4,12},{8,0},{12,4},{1,9},{5,13},{9,1},{13,5},{2,10},{6,14},... | collective-permute-start | bytes 184328 | tf_op jit(solution)/shard_map/ppermute | solution.py:380
  52.5 1.3 %collective-permute-start.16 = (bf16[16,1920]{1,0:T(8,128)(2,1)S(1)}, bf16[16,1920]{1,0:T(8,128)(2,1)S(1)}, u32[]{:S(2)}, u32[]{:S(2)}) collective-permute-start(bf16[16,1920]{1,0:T(8,128)(2,1)S(1)} %get-tuple-element.70), channel_id=1, source_target_pairs={{0,12},{4,8},{8,4},{12,0},{1,13},{5,9},{9,5},{13,1},{2,14},{6,10},... | collective-permute-start | bytes 184328 | tf_op jit(solution)/shard_map/ppermute | solution.py:380
  53.8 0.0 collective-permute-done.19.refs_1_
  53.8 0.0 collective-permute-start.17
  53.8 0.0 collective-permute-done.20.refs_2_
  53.9 1.6 %collective-permute-start.22 = (bf16[16,1152]{1,0:T(8,128)(2,1)S(1)}, bf16[16,1152]{1,0:T(8,128)(2,1)S(1)}, u32[]{:S(2)}, u32[]{:S(2)}) collective-permute-start(bf16[16,1152]{1,0:T(8,128)(2,1)S(1)} %get-tuple-element.80), channel_id=1, source_target_pairs={{0,2},{1,3},{2,0},{3,1},{4,6},{5,7},{6,4},{7,5},{8,10},{9,11},{10,... | collective-permute-start | bytes 110600 | tf_op jit(solution)/shard_map/ppermute | solution.py:380
  55.4 2.5 %collective-permute-done.22.refs_5_ = bf16[16,1152]{1,0:T(8,128)(2,1)S(1)} collective-permute-done((bf16[16,1152]{1,0:T(8,128)(2,1)S(1)}, bf16[16,1152]{1,0:T(8,128)(2,1)S(1)}, u32[]{:S(2)}, u32[]{:S(2)}) %collective-permute-start.22) | collective-permute-done | bytes 36896 | tf_op jit(solution)/shard_map/ppermute | solution.py:380
  57.9 0.7 %collective-permute-done.16.refs_2_ = bf16[16,1920]{1,0:T(8,128)(2,1)S(1)} collective-permute-done((bf16[16,1920]{1,0:T(8,128)(2,1)S(1)}, bf16[16,1920]{1,0:T(8,128)(2,1)S(1)}, u32[]{:S(2)}, u32[]{:S(2)}) %collective-permute-start.16) | collective-permute-done | bytes 61472 | tf_op jit(solution)/shard_map/ppermute | solution.py:380
  58.7 0.1 collective-permute-done.17.refs_3_
  58.7 0.7 %shard_map.78 = bf16[16,3072]{1,0:T(8,128)(2,1)} custom-call(bf16[16,1920]{1,0:T(8,128)(2,1)S(1)} %get-tuple-element.68.refs_0_, bf16[16,1920]{1,0:T(8,128)(2,1)S(1)} %collective-permute-done.15.refs_1_, bf16[16,1920]{1,0:T(8,128)(2,1)S(1)} %collective-permute-done.16.refs_2_, bf16[16,1920]{1,0:T(8,128)(2,1)S(1)} %collective-permute-done.17.refs_3_, ...), custom_call_target="tpu_custom_call" | custom-call | tf_op jit(solution)/shard_map/pallas_call | solution.py:111
  (13 shorter events, 0.1 us)
Async XLA Ops:
  1.1 11.8 %collective-permute-start.5 = (bf16[16,6144]{1,0:T(8,128)(2,1)S(1)}, bf16[16,6144]{1,0:T(8,128)(2,1)S(1)}, u32[]{:S(2)}, u32[]{:S(2)}) collective-permute-start(bf16[16,6144]{1,0:T(8,128)(2,1)S(1)} %get-tuple-element.50), channel_id=1, source_target_pairs={{0,4},{4,0},{8,12},{12,8},{1,5},{5,1},{9,13},{13,9},{2,6},{6,2},{1... | collective-permute-start | bytes 589832 | tf_op jit(solution)/shard_map/ppermute | solution.py:380
  4.2 10.4 %collective-permute-start.1 = (bf16[16,3072]{1,0:T(8,128)(2,1)}, bf16[16,3072]{1,0:T(8,128)(2,1)S(1)}, u32[]{:S(2)}, u32[]{:S(2)}) collective-permute-start(bf16[16,3072]{1,0:T(8,128)(2,1)} %tokens_ref.1), channel_id=1, source_target_pairs={{0,12},{4,8},{8,4},{12,0},{1,13},{5,9},{9,5},{13,1},{2,14},{6,10},... | collective-permute-start | bytes 294920 | tf_op jit(solution)/shard_map/ppermute | solution.py:380
  6.6 9.4 %collective-permute-start = (bf16[16,3072]{1,0:T(8,128)(2,1)}, bf16[16,3072]{1,0:T(8,128)(2,1)S(1)}, u32[]{:S(2)}, u32[]{:S(2)}) collective-permute-start(bf16[16,3072]{1,0:T(8,128)(2,1)} %tokens_ref.1), channel_id=1, source_target_pairs={{0,8},{4,12},{8,0},{12,4},{1,9},{5,13},{9,1},{13,5},{2,10},{6,14},... | collective-permute-start | bytes 294920 | tf_op jit(solution)/shard_map/ppermute | solution.py:380
  6.8 9.3 %collective-permute-start.2 = (bf16[16,6144]{1,0:T(8,128)(2,1)S(1)}, bf16[16,6144]{1,0:T(8,128)(2,1)S(1)}, u32[]{:S(2)}, u32[]{:S(2)}) collective-permute-start(bf16[16,6144]{1,0:T(8,128)(2,1)S(1)} %get-tuple-element.43.refs_0_), channel_id=1, source_target_pairs={{0,2},{1,3},{2,0},{3,1},{4,6},{5,7},{6,4},{7,5},{8,10},{9,11},{10,... | collective-permute-start | bytes 589832 | tf_op jit(solution)/shard_map/ppermute | solution.py:380
  12.9 11.8 %collective-permute-start.6 = (bf16[16,6144]{1,0:T(8,128)(2,1)S(1)}, bf16[16,6144]{1,0:T(8,128)(2,1)S(1)}, u32[]{:S(2)}, u32[]{:S(2)}) collective-permute-start(bf16[16,6144]{1,0:T(8,128)(2,1)S(1)} %collective-permute-done.5.refs_2_.refs_3_), channel_id=1, source_target_pairs={{0,2},{1,3},{2,0},{3,1},{4,6},{5,7},{6,4},{7,5},{8,10},{9,11},{10,... | collective-permute-start | bytes 589832 | tf_op jit(solution)/shard_map/ppermute | solution.py:380
  16.1 8.1 %collective-permute-start.7 = (bf16[16,3072]{1,0:T(8,128)(2,1)S(1)}, bf16[16,3072]{1,0:T(8,128)(2,1)S(1)}, u32[]{:S(2)}, u32[]{:S(2)}) collective-permute-start(bf16[16,3072]{1,0:T(8,128)(2,1)S(1)} %get-tuple-element.51), channel_id=1, source_target_pairs={{0,8},{4,12},{8,0},{12,4},{1,9},{5,13},{9,1},{13,5},{2,10},{6,14},... | collective-permute-start | bytes 294920 | tf_op jit(solution)/shard_map/ppermute | solution.py:380
  16.6 7.6 %collective-permute-start.8 = (bf16[16,3072]{1,0:T(8,128)(2,1)S(1)}, bf16[16,3072]{1,0:T(8,128)(2,1)S(1)}, u32[]{:S(2)}, u32[]{:S(2)}) collective-permute-start(bf16[16,3072]{1,0:T(8,128)(2,1)S(1)} %get-tuple-element.52), channel_id=1, source_target_pairs={{0,12},{4,8},{8,4},{12,0},{1,13},{5,9},{9,5},{13,1},{2,14},{6,10},... | collective-permute-start | bytes 294920 | tf_op jit(solution)/shard_map/ppermute | solution.py:380
  18.6 5.6 %collective-permute-start.3 = (bf16[16,3072]{1,0:T(8,128)(2,1)S(1)}, bf16[16,3072]{1,0:T(8,128)(2,1)S(1)}, u32[]{:S(2)}, u32[]{:S(2)}) collective-permute-start(bf16[16,3072]{1,0:T(8,128)(2,1)S(1)} %get-tuple-element.48.refs_1_), channel_id=1, source_target_pairs={{0,2},{1,3},{2,0},{3,1},{4,6},{5,7},{6,4},{7,5},{8,10},{9,11},{10,... | collective-permute-start | bytes 294920 | tf_op jit(solution)/shard_map/ppermute | solution.py:380
  20.1 4.6 %collective-permute-start.4 = (bf16[16,3072]{1,0:T(8,128)(2,1)S(1)}, bf16[16,3072]{1,0:T(8,128)(2,1)S(1)}, u32[]{:S(2)}, u32[]{:S(2)}) collective-permute-start(bf16[16,3072]{1,0:T(8,128)(2,1)S(1)} %get-tuple-element.49.refs_2_), channel_id=1, source_target_pairs={{0,2},{1,3},{2,0},{3,1},{4,6},{5,7},{6,4},{7,5},{8,10},{9,11},{10,... | collective-permute-start | bytes 294920 | tf_op jit(solution)/shard_map/ppermute | solution.py:380
  24.8 2.4 %collective-permute-start.10 = (bf16[128,3072]{1,0:T(8,128)(2,1)S(1)}, bf16[128,3072]{1,0:T(8,128)(2,1)S(1)}, u32[]{:S(2)}, u32[]{:S(2)}) collective-permute-start(bf16[128,3072]{1,0:T(8,128)(2,1)S(1)} %shard_map.69.refs_0_), channel_id=1, source_target_pairs={{0,1},{1,0},{2,3},{3,2},{4,5},{5,4},{6,7},{7,6},{8,9},{9,8},{10,11... | collective-permute-start | bytes 2359304 | tf_op jit(solution)/shard_map/ppermute | solution.py:380
  24.9 7.4 %collective-permute-start.11 = (bf16[64,3072]{1,0:T(8,128)(2,1)S(1)}, bf16[64,3072]{1,0:T(8,128)(2,1)S(1)}, u32[]{:S(2)}, u32[]{:S(2)}) collective-permute-start(bf16[64,3072]{1,0:T(8,128)(2,1)S(1)} %shard_map.68.refs_0_), channel_id=1, source_target_pairs={{0,1},{1,0},{2,3},{3,2},{4,5},{5,4},{6,7},{7,6},{8,9},{9,8},{10,11... | collective-permute-start | bytes 1179656 | tf_op jit(solution)/shard_map/ppermute | solution.py:380
  25.5 6.9 %collective-permute-start.9 = (bf16[32,3072]{1,0:T(8,128)(2,1)S(1)}, bf16[32,3072]{1,0:T(8,128)(2,1)S(1)}, u32[]{:S(2)}, u32[]{:S(2)}) collective-permute-start(bf16[32,3072]{1,0:T(8,128)(2,1)S(1)} %shard_map.67.refs_1_), channel_id=1, source_target_pairs={{0,2},{1,3},{2,0},{3,1},{4,6},{5,7},{6,4},{7,5},{8,10},{9,11},{10,... | collective-permute-start | bytes 589832 | tf_op jit(solution)/shard_map/ppermute | solution.py:380
  32.4 1.8 %collective-permute-start.12 = (bf16[64,3072]{1,0:T(8,128)(2,1)S(1)}, bf16[64,3072]{1,0:T(8,128)(2,1)S(1)}, u32[]{:S(2)}, u32[]{:S(2)}) collective-permute-start(bf16[64,3072]{1,0:T(8,128)(2,1)S(1)} %shard_map.71.refs_1_), channel_id=1, source_target_pairs={{0,1},{1,0},{2,3},{3,2},{4,5},{5,4},{6,7},{7,6},{8,9},{9,8},{10,11... | collective-permute-start | bytes 1179656 | tf_op jit(solution)/shard_map/ppermute | solution.py:380
  39.8 2.2 %collective-permute-start.13 = (bf16[128,1920]{1,0:T(8,128)(2,1)S(1)}, bf16[128,1920]{1,0:T(8,128)(2,1)S(1)}, u32[]{:S(2)}, u32[]{:S(2)}) collective-permute-start(bf16[128,1920]{1,0:T(8,128)(2,1)S(1)} %get-tuple-element.65), channel_id=1, source_target_pairs={{0,1},{1,0},{2,3},{3,2},{4,5},{5,4},{6,7},{7,6},{8,9},{9,8},{10,11... | collective-permute-start | bytes 1474568 | tf_op jit(solution)/shard_map/ppermute | solution.py:380
  41.5 1.7 %collective-permute-start.18 = (bf16[128,1152]{1,0:T(8,128)(2,1)S(1)}, bf16[128,1152]{1,0:T(8,128)(2,1)S(1)}, u32[]{:S(2)}, u32[]{:S(2)}) collective-permute-start(bf16[128,1152]{1,0:T(8,128)(2,1)S(1)} %get-tuple-element.74), channel_id=1, source_target_pairs={{0,1},{1,0},{2,3},{3,2},{4,5},{5,4},{6,7},{7,6},{8,9},{9,8},{10,11... | collective-permute-start | bytes 884744 | tf_op jit(solution)/shard_map/ppermute | solution.py:380
  42.1 8.1 %collective-permute-start.14 = (bf16[64,1920]{1,0:T(8,128)(2,1)S(1)}, bf16[64,1920]{1,0:T(8,128)(2,1)S(1)}, u32[]{:S(2)}, u32[]{:S(2)}) collective-permute-start(bf16[64,1920]{1,0:T(8,128)(2,1)S(1)} %get-tuple-element.67), channel_id=1, source_target_pairs={{0,2},{1,3},{2,0},{3,1},{4,6},{5,7},{6,4},{7,5},{8,10},{9,11},{10,... | collective-permute-start | bytes 737288 | tf_op jit(solution)/shard_map/ppermute | solution.py:380
  43.3 10.5 %collective-permute-start.19 = (bf16[32,1152]{1,0:T(8,128)(2,1)S(1)}, bf16[32,1152]{1,0:T(8,128)(2,1)S(1)}, u32[]{:S(2)}, u32[]{:S(2)}) collective-permute-start(bf16[32,1152]{1,0:T(8,128)(2,1)S(1)} %get-tuple-element.76), channel_id=1, source_target_pairs={{0,8},{4,12},{8,0},{12,4},{1,9},{5,13},{9,1},{13,5},{2,10},{6,14},... | collective-permute-start | bytes 221192 | tf_op jit(solution)/shard_map/ppermute | solution.py:380
  46.0 7.8 %collective-permute-start.20 = (bf16[32,1152]{1,0:T(8,128)(2,1)S(1)}, bf16[32,1152]{1,0:T(8,128)(2,1)S(1)}, u32[]{:S(2)}, u32[]{:S(2)}) collective-permute-start(bf16[32,1152]{1,0:T(8,128)(2,1)S(1)} %get-tuple-element.77), channel_id=1, source_target_pairs={{0,12},{4,8},{8,4},{12,0},{1,13},{5,9},{9,5},{13,1},{2,14},{6,10},... | collective-permute-start | bytes 221192 | tf_op jit(solution)/shard_map/ppermute | solution.py:380
  47.3 6.5 %collective-permute-start.21 = (bf16[32,1152]{1,0:T(8,128)(2,1)S(1)}, bf16[32,1152]{1,0:T(8,128)(2,1)S(1)}, u32[]{:S(2)}, u32[]{:S(2)}) collective-permute-start(bf16[32,1152]{1,0:T(8,128)(2,1)S(1)} %get-tuple-element.78), channel_id=1, source_target_pairs={{0,4},{4,0},{8,12},{12,8},{1,5},{5,1},{9,13},{13,9},{2,6},{6,2},{1... | collective-permute-start | bytes 221192 | tf_op jit(solution)/shard_map/ppermute | solution.py:380
  50.2 7.7 %collective-permute-start.15 = (bf16[16,1920]{1,0:T(8,128)(2,1)S(1)}, bf16[16,1920]{1,0:T(8,128)(2,1)S(1)}, u32[]{:S(2)}, u32[]{:S(2)}) collective-permute-start(bf16[16,1920]{1,0:T(8,128)(2,1)S(1)} %get-tuple-element.69), channel_id=1, source_target_pairs={{0,8},{4,12},{8,0},{12,4},{1,9},{5,13},{9,1},{13,5},{2,10},{6,14},... | collective-permute-start | bytes 184328 | tf_op jit(solution)/shard_map/ppermute | solution.py:380
  52.5 6.2 %collective-permute-start.16 = (bf16[16,1920]{1,0:T(8,128)(2,1)S(1)}, bf16[16,1920]{1,0:T(8,128)(2,1)S(1)}, u32[]{:S(2)}, u32[]{:S(2)}) collective-permute-start(bf16[16,1920]{1,0:T(8,128)(2,1)S(1)} %get-tuple-element.70), channel_id=1, source_target_pairs={{0,12},{4,8},{8,4},{12,0},{1,13},{5,9},{9,5},{13,1},{2,14},{6,10},... | collective-permute-start | bytes 184328 | tf_op jit(solution)/shard_map/ppermute | solution.py:380
  53.8 4.9 %collective-permute-start.17 = (bf16[16,1920]{1,0:T(8,128)(2,1)S(1)}, bf16[16,1920]{1,0:T(8,128)(2,1)S(1)}, u32[]{:S(2)}, u32[]{:S(2)}) collective-permute-start(bf16[16,1920]{1,0:T(8,128)(2,1)S(1)} %get-tuple-element.71), channel_id=1, source_target_pairs={{0,4},{4,0},{8,12},{12,8},{1,5},{5,1},{9,13},{13,9},{2,6},{6,2},{1... | collective-permute-start | bytes 184328 | tf_op jit(solution)/shard_map/ppermute | solution.py:380
  53.9 4.0 %collective-permute-start.22 = (bf16[16,1152]{1,0:T(8,128)(2,1)S(1)}, bf16[16,1152]{1,0:T(8,128)(2,1)S(1)}, u32[]{:S(2)}, u32[]{:S(2)}) collective-permute-start(bf16[16,1152]{1,0:T(8,128)(2,1)S(1)} %get-tuple-element.80), channel_id=1, source_target_pairs={{0,2},{1,3},{2,0},{3,1},{4,6},{5,7},{6,4},{7,5},{8,10},{9,11},{10,... | collective-permute-start | bytes 110600 | tf_op jit(solution)/shard_map/ppermute | solution.py:380

commit v8 on v7

--- a/solution.py
+++ b/solution.py
@@ -96,10 +96,6 @@
     return pl.BlockSpec(memory_space=pltpu.VMEM)
 
 
-def after(array, *earlier):
-    return lax.optimization_barrier((array, *earlier))[0]
-
-
 def assemble(pieces, rows_ref):
     start = 0
     for piece in pieces:
@@ -218,8 +214,9 @@
         )
         upright = lambda row: jnp.sum(jnp.where(here, row, 0.0), axis=1, keepdims=True)
         choices = range(ids.shape[0])
-        named = [upright(ids[k : k + 1, :].astype(jnp.float32)).astype(jnp.int32) for k in choices]
-        chosen = [upright(probs[k : k + 1, :].astype(jnp.float32)) for k in choices]
+        all_ids, all_probs = ids[...].astype(jnp.float32), probs[...].astype(jnp.float32)
+        named = [upright(all_ids[k : k + 1]).astype(jnp.int32) for k in choices]
+        chosen = [upright(all_probs[k : k + 1]) for k in choices]
         rows_grad = held[...].astype(jnp.float32)
         places = (
             own_ref.at[:, pl.ds(features, features)],

time: 59.6 us -> 59.6 us (level)
  no operation moved by 1% of the time
where the time goes in v8:
time: 59.6 us; the launch traced here: 59.4 us
  starting transfers between devices  25 us (42%)
  Pallas kernels  18.5 us (31%)
  waiting for transfers between devices  15.7 us (26%)
    ppermute x23, starting transfers between devices, beside(): return lax.ppermute(array, axis, [(i, i ^ step) for i in range(size)])  25 us
    ppermute x23, waiting for transfers between devices, beside(): return lax.ppermute(array, axis, [(i, i ^ step) for i in range(size)])  15.7 us
    pallas_call x1, Pallas kernels, scaled_rows(): pl.pallas_call(kernel, out_shape=[jax.ShapeDtypeStruct((rows, width), jnp...  5.61 us
    pallas_call x1, Pallas kernels, prefetched(): pl.pallas_call(kernel, out_shape=pltpu.VMEM((rows, weight.shape[1]), weig...  4.62 us
    pallas_call x1, Pallas kernels, slope_rows(): pl.pallas_call(kernel, out_shape=[jax.ShapeDtypeStruct((rows, width), jnp...  4.58 us
    pallas_call x1, Pallas kernels, partial_rows(): pl.pallas_call(kernel, out_shape=[half, half], in_specs=[whole_block()] *...  1.55 us
  transfers between devices with their start and end apart: 23, of which 11 were waited for; matrix products, arithmetic and copies ran while one was open for 0% of the time, Pallas kernels for 19%

profile of v8, /device:TPU:0, one launch (start us, length us, event | category | flops | bytes accessed | tf_op | source)
XLA Modules:
  0.0 59.4 jit_solution(11552839409491670751)
XLA Ops:
  0.0 1.1 %shard_map.64 = (bf16[16,6144]{1,0:T(8,128)(2,1)S(1)}, bf16[16,6144]{1,0:T(8,128)(2,1)S(1)}, bf16[16,3072]{1,0:T(8,128)(2,1)S(1)}, bf16[16,3072]{1,0:T(8,128)(2,1)S(1)}) custom-call(s32[1]{0:T(128)} %bitcast.expert_ref, bf16[16,3072]{1,0:T(8,128)(2,1)} %tokens_ref.1, bf16[16,3072]{1,0:T(8,128)(2,1)} %grads_ref.1, s32[2,16]{1,0:T(2,128)} %bitcast.7, ...), custom_call_target="tpu_custom_call" | custom-call | tf_op jit(solution)/shard_map/pallas_call | solution.py:235
  1.1 3.1 %collective-permute-start.5 = (bf16[16,6144]{1,0:T(8,128)(2,1)S(1)}, bf16[16,6144]{1,0:T(8,128)(2,1)S(1)}, u32[]{:S(2)}, u32[]{:S(2)}) collective-permute-start(bf16[16,6144]{1,0:T(8,128)(2,1)S(1)} %get-tuple-element.50), channel_id=1, source_target_pairs={{0,4},{4,0},{8,12},{12,8},{1,5},{5,1},{9,13},{13,9},{2,6},{6,2},{1... | collective-permute-start | bytes 589832 | tf_op jit(solution)/shard_map/ppermute | solution.py:377
  4.2 2.5 %collective-permute-start.1 = (bf16[16,3072]{1,0:T(8,128)(2,1)}, bf16[16,3072]{1,0:T(8,128)(2,1)S(1)}, u32[]{:S(2)}, u32[]{:S(2)}) collective-permute-start(bf16[16,3072]{1,0:T(8,128)(2,1)} %tokens_ref.1), channel_id=1, source_target_pairs={{0,12},{4,8},{8,4},{12,0},{1,13},{5,9},{9,5},{13,1},{2,14},{6,10},... | collective-permute-start | bytes 294920 | tf_op jit(solution)/shard_map/ppermute | solution.py:377
  6.6 0.1 collective-permute-start
  6.8 1.5 %collective-permute-start.2 = (bf16[16,6144]{1,0:T(8,128)(2,1)S(1)}, bf16[16,6144]{1,0:T(8,128)(2,1)S(1)}, u32[]{:S(2)}, u32[]{:S(2)}) collective-permute-start(bf16[16,6144]{1,0:T(8,128)(2,1)S(1)} %get-tuple-element.43.refs_0_), channel_id=1, source_target_pairs={{0,2},{1,3},{2,0},{3,1},{4,6},{5,7},{6,4},{7,5},{8,10},{9,11},{10,... | collective-permute-start | bytes 589832 | tf_op jit(solution)/shard_map/ppermute | solution.py:377
  8.3 4.6 %shard_map.66.refs_2_.refs_6_.weight_ref = bf16[3072,2048]{1,0:T(8,128)(2,1)S(1)} custom-call(bf16[3072,2048]{1,0:T(8,128)(2,1)} %bitcast.5), custom_call_target="tpu_custom_call" | custom-call | tf_op jit(solution)/shard_map/pallas_call | solution.py:270
  12.9 0.6 %collective-permute-start.6 = (bf16[16,6144]{1,0:T(8,128)(2,1)S(1)}, bf16[16,6144]{1,0:T(8,128)(2,1)S(1)}, u32[]{:S(2)}, u32[]{:S(2)}) collective-permute-start(bf16[16,6144]{1,0:T(8,128)(2,1)S(1)} %collective-permute-done.5.refs_2_.refs_3_), channel_id=1, source_target_pairs={{0,2},{1,3},{2,0},{3,1},{4,6},{5,7},{6,4},{7,5},{8,10},{9,11},{10,... | collective-permute-start | bytes 589832 | tf_op jit(solution)/shard_map/ppermute | solution.py:377
  13.5 1.0 %collective-permute-done.1.refs_1_ = bf16[16,3072]{1,0:T(8,128)(2,1)S(1)} collective-permute-done((bf16[16,3072]{1,0:T(8,128)(2,1)}, bf16[16,3072]{1,0:T(8,128)(2,1)S(1)}, u32[]{:S(2)}, u32[]{:S(2)}) %collective-permute-start.1) | collective-permute-done | bytes 98336 | tf_op jit(solution)/shard_map/ppermute | solution.py:377
  14.5 1.6 %collective-permute-done.refs_0_ = bf16[16,3072]{1,0:T(8,128)(2,1)S(1)} collective-permute-done((bf16[16,3072]{1,0:T(8,128)(2,1)}, bf16[16,3072]{1,0:T(8,128)(2,1)S(1)}, u32[]{:S(2)}, u32[]{:S(2)}) %collective-permute-start) | collective-permute-done | bytes 98336 | tf_op jit(solution)/shard_map/ppermute | solution.py:377
  16.1 0.5 collective-permute-start.7
  16.6 2.0 %collective-permute-start.8 = (bf16[16,3072]{1,0:T(8,128)(2,1)S(1)}, bf16[16,3072]{1,0:T(8,128)(2,1)S(1)}, u32[]{:S(2)}, u32[]{:S(2)}) collective-permute-start(bf16[16,3072]{1,0:T(8,128)(2,1)S(1)} %get-tuple-element.52), channel_id=1, source_target_pairs={{0,12},{4,8},{8,4},{12,0},{1,13},{5,9},{9,5},{13,1},{2,14},{6,10},... | collective-permute-start | bytes 294920 | tf_op jit(solution)/shard_map/ppermute | solution.py:377
  18.6 1.5 %collective-permute-start.3 = (bf16[16,3072]{1,0:T(8,128)(2,1)S(1)}, bf16[16,3072]{1,0:T(8,128)(2,1)S(1)}, u32[]{:S(2)}, u32[]{:S(2)}) collective-permute-start(bf16[16,3072]{1,0:T(8,128)(2,1)S(1)} %get-tuple-element.48.refs_1_), channel_id=1, source_target_pairs={{0,2},{1,3},{2,0},{3,1},{4,6},{5,7},{6,4},{7,5},{8,10},{9,11},{10,... | collective-permute-start | bytes 294920 | tf_op jit(solution)/shard_map/ppermute | solution.py:377
  20.1 0.5 collective-permute-start.4
  20.6 3.6 %collective-permute-done.7.refs_0_ = bf16[16,3072]{1,0:T(8,128)(2,1)S(1)} collective-permute-done((bf16[16,3072]{1,0:T(8,128)(2,1)S(1)}, bf16[16,3072]{1,0:T(8,128)(2,1)S(1)}, u32[]{:S(2)}, u32[]{:S(2)}) %collective-permute-start.7) | collective-permute-done | bytes 98336 | tf_op jit(solution)/shard_map/ppermute | solution.py:377
  24.3 0.5 collective-permute-done.4.refs_6_
  24.7 0.0 collective-permute-done.6.refs_7_.refs_2_
  24.7 0.1 shard_map.69.refs_0_
  24.8 0.1 collective-permute-start.10
  24.9 0.6 collective-permute-start.11
  25.5 1.1 %collective-permute-start.9 = (bf16[32,3072]{1,0:T(8,128)(2,1)S(1)}, bf16[32,3072]{1,0:T(8,128)(2,1)S(1)}, u32[]{:S(2)}, u32[]{:S(2)}) collective-permute-start(bf16[32,3072]{1,0:T(8,128)(2,1)S(1)} %shard_map.67.refs_1_), channel_id=1, source_target_pairs={{0,2},{1,3},{2,0},{3,1},{4,6},{5,7},{6,4},{7,5},{8,10},{9,11},{10,... | collective-permute-start | bytes 589832 | tf_op jit(solution)/shard_map/ppermute | solution.py:377
  26.5 0.6 %collective-permute-done.10.refs_1_ = bf16[128,3072]{1,0:T(8,128)(2,1)S(1)} collective-permute-done((bf16[128,3072]{1,0:T(8,128)(2,1)S(1)}, bf16[128,3072]{1,0:T(8,128)(2,1)S(1)}, u32[]{:S(2)}, u32[]{:S(2)}) %collective-permute-start.10) | collective-permute-done | bytes 786464 | tf_op jit(solution)/shard_map/ppermute | solution.py:377
  27.1 4.6 %shard_map.70 = (f32[256,2048]{1,0:T(8,128)S(1)}, bf16[2048,3072]{1,0:T(8,128)(2,1)S(1)}) custom-call(bf16[128,3072]{1,0:T(8,128)(2,1)S(1)} %shard_map.69.refs_0_, bf16[128,3072]{1,0:T(8,128)(2,1)S(1)} %collective-permute-done.10.refs_1_, bf16[3072,2048]{1,0:T(8,128)(2,1)S(1)} %shard_map.66.refs_2_.refs_6_.weight_ref, bf16[2048,3072]{1,0:T(8,128)(2,1)} %bitcast.6), custom_call_target="tpu_custom_call" | custom-call | tf_op jit(solution)/shard_map/pallas_call | solution.py:298
  31.7 0.6 %collective-permute-done.9.refs_1_ = bf16[32,3072]{1,0:T(8,128)(2,1)S(1)} collective-permute-done((bf16[32,3072]{1,0:T(8,128)(2,1)S(1)}, bf16[32,3072]{1,0:T(8,128)(2,1)S(1)}, u32[]{:S(2)}, u32[]{:S(2)}) %collective-permute-start.9) | collective-permute-done | bytes 196640 | tf_op jit(solution)/shard_map/ppermute | solution.py:377
  32.3 0.0 collective-permute-done.11.refs_2_
  32.4 0.1 collective-permute-start.12
  32.5 1.7 %collective-permute-done.12.refs_3_ = bf16[64,3072]{1,0:T(8,128)(2,1)S(1)} collective-permute-done((bf16[64,3072]{1,0:T(8,128)(2,1)S(1)}, bf16[64,3072]{1,0:T(8,128)(2,1)S(1)}, u32[]{:S(2)}, u32[]{:S(2)}) %collective-permute-start.12) | collective-permute-done | bytes 393248 | tf_op jit(solution)/shard_map/ppermute | solution.py:377
  34.2 5.6 %shard_map.72 = (bf16[256,2048]{1,0:T(8,128)(2,1)S(1)}, bf16[128,1920]{1,0:T(8,128)(2,1)S(1)}, bf16[128,1920]{1,0:T(8,128)(2,1)S(1)}) custom-call(bf16[64,3072]{1,0:T(8,128)(2,1)S(1)} %shard_map.68.refs_0_, bf16[64,3072]{1,0:T(8,128)(2,1)S(1)} %shard_map.71.refs_1_, bf16[64,3072]{1,0:T(8,128)(2,1)S(1)} %collective-permute-done.11.refs_2_, ...), custom_call_target="tpu_custom_call" | custom-call | tf_op jit(solution)/shard_map/pallas_call | solution.py:333
  39.8 0.2 collective-permute-start.13
  40.0 1.5 %shard_map.75 = (bf16[128,1152]{1,0:T(8,128)(2,1)S(1)}, bf16[128,1152]{1,0:T(8,128)(2,1)S(1)}) custom-call(bf16[256,2048]{1,0:T(8,128)(2,1)S(1)} %get-tuple-element.72.scaled_ref, bf16[3072,2048]{1,0:T(8,128)(2,1)S(1)} %shard_map.66.refs_2_.refs_6_.weight_ref), custom_call_target="tpu_custom_call" | custom-call | tf_op jit(solution)/shard_map/pallas_call | solution.py:365
  41.5 0.4 collective-permute-start.18
  42.0 0.1 shard_map.73
  42.1 1.1 %collective-permute-start.14 = (bf16[64,1920]{1,0:T(8,128)(2,1)S(1)}, bf16[64,1920]{1,0:T(8,128)(2,1)S(1)}, u32[]{:S(2)}, u32[]{:S(2)}) collective-permute-start(bf16[64,1920]{1,0:T(8,128)(2,1)S(1)} %get-tuple-element.67), channel_id=1, source_target_pairs={{0,2},{1,3},{2,0},{3,1},{4,6},{5,7},{6,4},{7,5},{8,10},{9,11},{10,... | collective-permute-start | bytes 737288 | tf_op jit(solution)/shard_map/ppermute | solution.py:377
  43.2 0.0 collective-permute-done.18.refs_1_
  43.2 0.1 shard_map.76
  43.3 2.7 %collective-permute-start.19 = (bf16[32,1152]{1,0:T(8,128)(2,1)S(1)}, bf16[32,1152]{1,0:T(8,128)(2,1)S(1)}, u32[]{:S(2)}, u32[]{:S(2)}) collective-permute-start(bf16[32,1152]{1,0:T(8,128)(2,1)S(1)} %get-tuple-element.76), channel_id=1, source_target_pairs={{0,8},{4,12},{8,0},{12,4},{1,9},{5,13},{9,1},{13,5},{2,10},{6,14},... | collective-permute-start | bytes 221192 | tf_op jit(solution)/shard_map/ppermute | solution.py:377
  46.0 1.3 %collective-permute-start.20 = (bf16[32,1152]{1,0:T(8,128)(2,1)S(1)}, bf16[32,1152]{1,0:T(8,128)(2,1)S(1)}, u32[]{:S(2)}, u32[]{:S(2)}) collective-permute-start(bf16[32,1152]{1,0:T(8,128)(2,1)S(1)} %get-tuple-element.77), channel_id=1, source_target_pairs={{0,12},{4,8},{8,4},{12,0},{1,13},{5,9},{9,5},{13,1},{2,14},{6,10},... | collective-permute-start | bytes 221192 | tf_op jit(solution)/shard_map/ppermute | solution.py:377
  47.3 2.8 %collective-permute-done.14.refs_1_ = bf16[64,1920]{1,0:T(8,128)(2,1)S(1)} collective-permute-done((bf16[64,1920]{1,0:T(8,128)(2,1)S(1)}, bf16[64,1920]{1,0:T(8,128)(2,1)S(1)}, u32[]{:S(2)}, u32[]{:S(2)}) %collective-permute-start.14) | collective-permute-done | bytes 245792 | tf_op jit(solution)/shard_map/ppermute | solution.py:377
  50.2 0.1 shard_map.74
  50.2 2.2 %collective-permute-start.15 = (bf16[16,1920]{1,0:T(8,128)(2,1)S(1)}, bf16[16,1920]{1,0:T(8,128)(2,1)S(1)}, u32[]{:S(2)}, u32[]{:S(2)}) collective-permute-start(bf16[16,1920]{1,0:T(8,128)(2,1)S(1)} %get-tuple-element.69), channel_id=1, source_target_pairs={{0,8},{4,12},{8,0},{12,4},{1,9},{5,13},{9,1},{13,5},{2,10},{6,14},... | collective-permute-start | bytes 184328 | tf_op jit(solution)/shard_map/ppermute | solution.py:377
  52.5 1.3 %collective-permute-start.16 = (bf16[16,1920]{1,0:T(8,128)(2,1)S(1)}, bf16[16,1920]{1,0:T(8,128)(2,1)S(1)}, u32[]{:S(2)}, u32[]{:S(2)}) collective-permute-start(bf16[16,1920]{1,0:T(8,128)(2,1)S(1)} %get-tuple-element.70), channel_id=1, source_target_pairs={{0,12},{4,8},{8,4},{12,0},{1,13},{5,9},{9,5},{13,1},{2,14},{6,10},... | collective-permute-start | bytes 184328 | tf_op jit(solution)/shard_map/ppermute | solution.py:377
  53.8 0.0 collective-permute-done.19.refs_1_
  53.8 0.0 collective-permute-start.17
  53.8 0.0 collective-permute-done.20.refs_2_
  53.9 1.6 %collective-permute-start.22 = (bf16[16,1152]{1,0:T(8,128)(2,1)S(1)}, bf16[16,1152]{1,0:T(8,128)(2,1)S(1)}, u32[]{:S(2)}, u32[]{:S(2)}) collective-permute-start(bf16[16,1152]{1,0:T(8,128)(2,1)S(1)} %get-tuple-element.80), channel_id=1, source_target_pairs={{0,2},{1,3},{2,0},{3,1},{4,6},{5,7},{6,4},{7,5},{8,10},{9,11},{10,... | collective-permute-start | bytes 110600 | tf_op jit(solution)/shard_map/ppermute | solution.py:377
  55.4 2.5 %collective-permute-done.22.refs_5_ = bf16[16,1152]{1,0:T(8,128)(2,1)S(1)} collective-permute-done((bf16[16,1152]{1,0:T(8,128)(2,1)S(1)}, bf16[16,1152]{1,0:T(8,128)(2,1)S(1)}, u32[]{:S(2)}, u32[]{:S(2)}) %collective-permute-start.22) | collective-permute-done | bytes 36896 | tf_op jit(solution)/shard_map/ppermute | solution.py:377
  57.9 0.7 %collective-permute-done.16.refs_2_ = bf16[16,1920]{1,0:T(8,128)(2,1)S(1)} collective-permute-done((bf16[16,1920]{1,0:T(8,128)(2,1)S(1)}, bf16[16,1920]{1,0:T(8,128)(2,1)S(1)}, u32[]{:S(2)}, u32[]{:S(2)}) %collective-permute-start.16) | collective-permute-done | bytes 61472 | tf_op jit(solution)/shard_map/ppermute | solution.py:377
  58.7 0.1 collective-permute-done.17.refs_3_
  58.7 0.7 %shard_map.78 = bf16[16,3072]{1,0:T(8,128)(2,1)} custom-call(bf16[16,1920]{1,0:T(8,128)(2,1)S(1)} %get-tuple-element.68.refs_0_, bf16[16,1920]{1,0:T(8,128)(2,1)S(1)} %collective-permute-done.15.refs_1_, bf16[16,1920]{1,0:T(8,128)(2,1)S(1)} %collective-permute-done.16.refs_2_, bf16[16,1920]{1,0:T(8,128)(2,1)S(1)} %collective-permute-done.17.refs_3_, ...), custom_call_target="tpu_custom_call" | custom-call | tf_op jit(solution)/shard_map/pallas_call | solution.py:107
  (13 shorter events, 0.1 us)
Async XLA Ops:
  1.1 11.8 %collective-permute-start.5 = (bf16[16,6144]{1,0:T(8,128)(2,1)S(1)}, bf16[16,6144]{1,0:T(8,128)(2,1)S(1)}, u32[]{:S(2)}, u32[]{:S(2)}) collective-permute-start(bf16[16,6144]{1,0:T(8,128)(2,1)S(1)} %get-tuple-element.50), channel_id=1, source_target_pairs={{0,4},{4,0},{8,12},{12,8},{1,5},{5,1},{9,13},{13,9},{2,6},{6,2},{1... | collective-permute-start | bytes 589832 | tf_op jit(solution)/shard_map/ppermute | solution.py:377
  4.2 10.4 %collective-permute-start.1 = (bf16[16,3072]{1,0:T(8,128)(2,1)}, bf16[16,3072]{1,0:T(8,128)(2,1)S(1)}, u32[]{:S(2)}, u32[]{:S(2)}) collective-permute-start(bf16[16,3072]{1,0:T(8,128)(2,1)} %tokens_ref.1), channel_id=1, source_target_pairs={{0,12},{4,8},{8,4},{12,0},{1,13},{5,9},{9,5},{13,1},{2,14},{6,10},... | collective-permute-start | bytes 294920 | tf_op jit(solution)/shard_map/ppermute | solution.py:377
  6.6 9.4 %collective-permute-start = (bf16[16,3072]{1,0:T(8,128)(2,1)}, bf16[16,3072]{1,0:T(8,128)(2,1)S(1)}, u32[]{:S(2)}, u32[]{:S(2)}) collective-permute-start(bf16[16,3072]{1,0:T(8,128)(2,1)} %tokens_ref.1), channel_id=1, source_target_pairs={{0,8},{4,12},{8,0},{12,4},{1,9},{5,13},{9,1},{13,5},{2,10},{6,14},... | collective-permute-start | bytes 294920 | tf_op jit(solution)/shard_map/ppermute | solution.py:377
  6.8 9.3 %collective-permute-start.2 = (bf16[16,6144]{1,0:T(8,128)(2,1)S(1)}, bf16[16,6144]{1,0:T(8,128)(2,1)S(1)}, u32[]{:S(2)}, u32[]{:S(2)}) collective-permute-start(bf16[16,6144]{1,0:T(8,128)(2,1)S(1)} %get-tuple-element.43.refs_0_), channel_id=1, source_target_pairs={{0,2},{1,3},{2,0},{3,1},{4,6},{5,7},{6,4},{7,5},{8,10},{9,11},{10,... | collective-permute-start | bytes 589832 | tf_op jit(solution)/shard_map/ppermute | solution.py:377
  12.9 11.8 %collective-permute-start.6 = (bf16[16,6144]{1,0:T(8,128)(2,1)S(1)}, bf16[16,6144]{1,0:T(8,128)(2,1)S(1)}, u32[]{:S(2)}, u32[]{:S(2)}) collective-permute-start(bf16[16,6144]{1,0:T(8,128)(2,1)S(1)} %collective-permute-done.5.refs_2_.refs_3_), channel_id=1, source_target_pairs={{0,2},{1,3},{2,0},{3,1},{4,6},{5,7},{6,4},{7,5},{8,10},{9,11},{10,... | collective-permute-start | bytes 589832 | tf_op jit(solution)/shard_map/ppermute | solution.py:377
  16.1 8.1 %collective-permute-start.7 = (bf16[16,3072]{1,0:T(8,128)(2,1)S(1)}, bf16[16,3072]{1,0:T(8,128)(2,1)S(1)}, u32[]{:S(2)}, u32[]{:S(2)}) collective-permute-start(bf16[16,3072]{1,0:T(8,128)(2,1)S(1)} %get-tuple-element.51), channel_id=1, source_target_pairs={{0,8},{4,12},{8,0},{12,4},{1,9},{5,13},{9,1},{13,5},{2,10},{6,14},... | collective-permute-start | bytes 294920 | tf_op jit(solution)/shard_map/ppermute | solution.py:377
  16.6 7.6 %collective-permute-start.8 = (bf16[16,3072]{1,0:T(8,128)(2,1)S(1)}, bf16[16,3072]{1,0:T(8,128)(2,1)S(1)}, u32[]{:S(2)}, u32[]{:S(2)}) collective-permute-start(bf16[16,3072]{1,0:T(8,128)(2,1)S(1)} %get-tuple-element.52), channel_id=1, source_target_pairs={{0,12},{4,8},{8,4},{12,0},{1,13},{5,9},{9,5},{13,1},{2,14},{6,10},... | collective-permute-start | bytes 294920 | tf_op jit(solution)/shard_map/ppermute | solution.py:377
  18.6 5.6 %collective-permute-start.3 = (bf16[16,3072]{1,0:T(8,128)(2,1)S(1)}, bf16[16,3072]{1,0:T(8,128)(2,1)S(1)}, u32[]{:S(2)}, u32[]{:S(2)}) collective-permute-start(bf16[16,3072]{1,0:T(8,128)(2,1)S(1)} %get-tuple-element.48.refs_1_), channel_id=1, source_target_pairs={{0,2},{1,3},{2,0},{3,1},{4,6},{5,7},{6,4},{7,5},{8,10},{9,11},{10,... | collective-permute-start | bytes 294920 | tf_op jit(solution)/shard_map/ppermute | solution.py:377
  20.1 4.6 %collective-permute-start.4 = (bf16[16,3072]{1,0:T(8,128)(2,1)S(1)}, bf16[16,3072]{1,0:T(8,128)(2,1)S(1)}, u32[]{:S(2)}, u32[]{:S(2)}) collective-permute-start(bf16[16,3072]{1,0:T(8,128)(2,1)S(1)} %get-tuple-element.49.refs_2_), channel_id=1, source_target_pairs={{0,2},{1,3},{2,0},{3,1},{4,6},{5,7},{6,4},{7,5},{8,10},{9,11},{10,... | collective-permute-start | bytes 294920 | tf_op jit(solution)/shard_map/ppermute | solution.py:377
  24.8 2.4 %collective-permute-start.10 = (bf16[128,3072]{1,0:T(8,128)(2,1)S(1)}, bf16[128,3072]{1,0:T(8,128)(2,1)S(1)}, u32[]{:S(2)}, u32[]{:S(2)}) collective-permute-start(bf16[128,3072]{1,0:T(8,128)(2,1)S(1)} %shard_map.69.refs_0_), channel_id=1, source_target_pairs={{0,1},{1,0},{2,3},{3,2},{4,5},{5,4},{6,7},{7,6},{8,9},{9,8},{10,11... | collective-permute-start | bytes 2359304 | tf_op jit(solution)/shard_map/ppermute | solution.py:377
  24.9 7.4 %collective-permute-start.11 = (bf16[64,3072]{1,0:T(8,128)(2,1)S(1)}, bf16[64,3072]{1,0:T(8,128)(2,1)S(1)}, u32[]{:S(2)}, u32[]{:S(2)}) collective-permute-start(bf16[64,3072]{1,0:T(8,128)(2,1)S(1)} %shard_map.68.refs_0_), channel_id=1, source_target_pairs={{0,1},{1,0},{2,3},{3,2},{4,5},{5,4},{6,7},{7,6},{8,9},{9,8},{10,11... | collective-permute-start | bytes 1179656 | tf_op jit(solution)/shard_map/ppermute | solution.py:377
  25.5 6.9 %collective-permute-start.9 = (bf16[32,3072]{1,0:T(8,128)(2,1)S(1)}, bf16[32,3072]{1,0:T(8,128)(2,1)S(1)}, u32[]{:S(2)}, u32[]{:S(2)}) collective-permute-start(bf16[32,3072]{1,0:T(8,128)(2,1)S(1)} %shard_map.67.refs_1_), channel_id=1, source_target_pairs={{0,2},{1,3},{2,0},{3,1},{4,6},{5,7},{6,4},{7,5},{8,10},{9,11},{10,... | collective-permute-start | bytes 589832 | tf_op jit(solution)/shard_map/ppermute | solution.py:377
  32.4 1.8 %collective-permute-start.12 = (bf16[64,3072]{1,0:T(8,128)(2,1)S(1)}, bf16[64,3072]{1,0:T(8,128)(2,1)S(1)}, u32[]{:S(2)}, u32[]{:S(2)}) collective-permute-start(bf16[64,3072]{1,0:T(8,128)(2,1)S(1)} %shard_map.71.refs_1_), channel_id=1, source_target_pairs={{0,1},{1,0},{2,3},{3,2},{4,5},{5,4},{6,7},{7,6},{8,9},{9,8},{10,11... | collective-permute-start | bytes 1179656 | tf_op jit(solution)/shard_map/ppermute | solution.py:377
  39.8 2.2 %collective-permute-start.13 = (bf16[128,1920]{1,0:T(8,128)(2,1)S(1)}, bf16[128,1920]{1,0:T(8,128)(2,1)S(1)}, u32[]{:S(2)}, u32[]{:S(2)}) collective-permute-start(bf16[128,1920]{1,0:T(8,128)(2,1)S(1)} %get-tuple-element.65), channel_id=1, source_target_pairs={{0,1},{1,0},{2,3},{3,2},{4,5},{5,4},{6,7},{7,6},{8,9},{9,8},{10,11... | collective-permute-start | bytes 1474568 | tf_op jit(solution)/shard_map/ppermute | solution.py:377
  41.5 1.7 %collective-permute-start.18 = (bf16[128,1152]{1,0:T(8,128)(2,1)S(1)}, bf16[128,1152]{1,0:T(8,128)(2,1)S(1)}, u32[]{:S(2)}, u32[]{:S(2)}) collective-permute-start(bf16[128,1152]{1,0:T(8,128)(2,1)S(1)} %get-tuple-element.74), channel_id=1, source_target_pairs={{0,1},{1,0},{2,3},{3,2},{4,5},{5,4},{6,7},{7,6},{8,9},{9,8},{10,11... | collective-permute-start | bytes 884744 | tf_op jit(solution)/shard_map/ppermute | solution.py:377
  42.1 8.1 %collective-permute-start.14 = (bf16[64,1920]{1,0:T(8,128)(2,1)S(1)}, bf16[64,1920]{1,0:T(8,128)(2,1)S(1)}, u32[]{:S(2)}, u32[]{:S(2)}) collective-permute-start(bf16[64,1920]{1,0:T(8,128)(2,1)S(1)} %get-tuple-element.67), channel_id=1, source_target_pairs={{0,2},{1,3},{2,0},{3,1},{4,6},{5,7},{6,4},{7,5},{8,10},{9,11},{10,... | collective-permute-start | bytes 737288 | tf_op jit(solution)/shard_map/ppermute | solution.py:377
  43.3 10.5 %collective-permute-start.19 = (bf16[32,1152]{1,0:T(8,128)(2,1)S(1)}, bf16[32,1152]{1,0:T(8,128)(2,1)S(1)}, u32[]{:S(2)}, u32[]{:S(2)}) collective-permute-start(bf16[32,1152]{1,0:T(8,128)(2,1)S(1)} %get-tuple-element.76), channel_id=1, source_target_pairs={{0,8},{4,12},{8,0},{12,4},{1,9},{5,13},{9,1},{13,5},{2,10},{6,14},... | collective-permute-start | bytes 221192 | tf_op jit(solution)/shard_map/ppermute | solution.py:377
  46.0 7.8 %collective-permute-start.20 = (bf16[32,1152]{1,0:T(8,128)(2,1)S(1)}, bf16[32,1152]{1,0:T(8,128)(2,1)S(1)}, u32[]{:S(2)}, u32[]{:S(2)}) collective-permute-start(bf16[32,1152]{1,0:T(8,128)(2,1)S(1)} %get-tuple-element.77), channel_id=1, source_target_pairs={{0,12},{4,8},{8,4},{12,0},{1,13},{5,9},{9,5},{13,1},{2,14},{6,10},... | collective-permute-start | bytes 221192 | tf_op jit(solution)/shard_map/ppermute | solution.py:377
  47.3 6.5 %collective-permute-start.21 = (bf16[32,1152]{1,0:T(8,128)(2,1)S(1)}, bf16[32,1152]{1,0:T(8,128)(2,1)S(1)}, u32[]{:S(2)}, u32[]{:S(2)}) collective-permute-start(bf16[32,1152]{1,0:T(8,128)(2,1)S(1)} %get-tuple-element.78), channel_id=1, source_target_pairs={{0,4},{4,0},{8,12},{12,8},{1,5},{5,1},{9,13},{13,9},{2,6},{6,2},{1... | collective-permute-start | bytes 221192 | tf_op jit(solution)/shard_map/ppermute | solution.py:377
  50.2 7.7 %collective-permute-start.15 = (bf16[16,1920]{1,0:T(8,128)(2,1)S(1)}, bf16[16,1920]{1,0:T(8,128)(2,1)S(1)}, u32[]{:S(2)}, u32[]{:S(2)}) collective-permute-start(bf16[16,1920]{1,0:T(8,128)(2,1)S(1)} %get-tuple-element.69), channel_id=1, source_target_pairs={{0,8},{4,12},{8,0},{12,4},{1,9},{5,13},{9,1},{13,5},{2,10},{6,14},... | collective-permute-start | bytes 184328 | tf_op jit(solution)/shard_map/ppermute | solution.py:377
  52.5 6.2 %collective-permute-start.16 = (bf16[16,1920]{1,0:T(8,128)(2,1)S(1)}, bf16[16,1920]{1,0:T(8,128)(2,1)S(1)}, u32[]{:S(2)}, u32[]{:S(2)}) collective-permute-start(bf16[16,1920]{1,0:T(8,128)(2,1)S(1)} %get-tuple-element.70), channel_id=1, source_target_pairs={{0,12},{4,8},{8,4},{12,0},{1,13},{5,9},{9,5},{13,1},{2,14},{6,10},... | collective-permute-start | bytes 184328 | tf_op jit(solution)/shard_map/ppermute | solution.py:377
  53.8 4.9 %collective-permute-start.17 = (bf16[16,1920]{1,0:T(8,128)(2,1)S(1)}, bf16[16,1920]{1,0:T(8,128)(2,1)S(1)}, u32[]{:S(2)}, u32[]{:S(2)}) collective-permute-start(bf16[16,1920]{1,0:T(8,128)(2,1)S(1)} %get-tuple-element.71), channel_id=1, source_target_pairs={{0,4},{4,0},{8,12},{12,8},{1,5},{5,1},{9,13},{13,9},{2,6},{6,2},{1... | collective-permute-start | bytes 184328 | tf_op jit(solution)/shard_map/ppermute | solution.py:377
  53.9 4.0 %collective-permute-start.22 = (bf16[16,1152]{1,0:T(8,128)(2,1)S(1)}, bf16[16,1152]{1,0:T(8,128)(2,1)S(1)}, u32[]{:S(2)}, u32[]{:S(2)}) collective-permute-start(bf16[16,1152]{1,0:T(8,128)(2,1)S(1)} %get-tuple-element.80), channel_id=1, source_target_pairs={{0,2},{1,3},{2,0},{3,1},{4,6},{5,7},{6,4},{7,5},{8,10},{9,11},{10,... | collective-permute-start | bytes 110600 | tf_op jit(solution)/shard_map/ppermute | solution.py:377

commit v9 on v8

--- a/solution.py
+++ b/solution.py
@@ -312,7 +312,7 @@
     )(*pieces, in_vmem(weight), in_hbm(later))
 
 
-def scaled_rows(pieces, weight, slope, back, count, tile=1024):
+def scaled_rows(pieces, weight, slope, back, count, tile=2048):
     rows, width = slope.shape
     features = weight.shape[1]
 
@@ -433,7 +433,7 @@
         across, far_grads_across, near_across, width=features, offsets=[features, 0, features]
     )
     grad_pieces = [grad_column, grad_across, grad_column_other, beside(grad_across, "tensor", 1)]
-    count = features * 5 // 8
+    count = features * 2 // 3
     scaled, *halves = scaled_rows(
         grad_pieces, held_out, slope, held_in, count
     )

time: 59.6 us -> 59.8 us (level)
  transfers between devices with their start and end apart: 23 -> 23, of which waited for: 11 -> 12; matrix products, arithmetic and copies ran while one was open for 0% -> 0% of each run, Pallas kernels for 19% -> 18%
where the time goes in v9:
time: 59.8 us; the launch traced here: 59.6 us
  starting transfers between devices  25 us (42%)
  Pallas kernels  18.3 us (31%)
  waiting for transfers between devices  16.2 us (27%)
    ppermute x23, starting transfers between devices, beside(): return lax.ppermute(array, axis, [(i, i ^ step) for i in range(size)])  25 us
    ppermute x23, waiting for transfers between devices, beside(): return lax.ppermute(array, axis, [(i, i ^ step) for i in range(size)])  16.2 us
    pallas_call x1, Pallas kernels, scaled_rows(): pl.pallas_call(kernel, out_shape=[jax.ShapeDtypeStruct((rows, width), jnp...  5.61 us
    pallas_call x1, Pallas kernels, prefetched(): pl.pallas_call(kernel, out_shape=pltpu.VMEM((rows, weight.shape[1]), weig...  4.62 us
    pallas_call x1, Pallas kernels, slope_rows(): pl.pallas_call(kernel, out_shape=[jax.ShapeDtypeStruct((rows, width), jnp...  4.58 us
    pallas_call x1, Pallas kernels, partial_rows(): pl.pallas_call(kernel, out_shape=[half, half], in_specs=[whole_block()] *...  1.28 us
  transfers between devices with their start and end apart: 23, of which 12 were waited for; matrix products, arithmetic and copies ran while one was open for 0% of the time, Pallas kernels for 18%

profile of v9, /device:TPU:0, one launch (start us, length us, event | category | flops | bytes accessed | tf_op | source)
XLA Modules:
  0.0 59.6 jit_solution(16278647473221003919)
XLA Ops:
  0.0 1.1 %shard_map.64 = (bf16[16,6144]{1,0:T(8,128)(2,1)S(1)}, bf16[16,6144]{1,0:T(8,128)(2,1)S(1)}, bf16[16,3072]{1,0:T(8,128)(2,1)S(1)}, bf16[16,3072]{1,0:T(8,128)(2,1)S(1)}) custom-call(s32[1]{0:T(128)} %bitcast.expert_ref, bf16[16,3072]{1,0:T(8,128)(2,1)} %tokens_ref.1, bf16[16,3072]{1,0:T(8,128)(2,1)} %grads_ref.1, s32[2,16]{1,0:T(2,128)} %bitcast.7, ...), custom_call_target="tpu_custom_call" | custom-call | tf_op jit(solution)/shard_map/pallas_call | solution.py:235
  1.1 3.1 %collective-permute-start.5 = (bf16[16,6144]{1,0:T(8,128)(2,1)S(1)}, bf16[16,6144]{1,0:T(8,128)(2,1)S(1)}, u32[]{:S(2)}, u32[]{:S(2)}) collective-permute-start(bf16[16,6144]{1,0:T(8,128)(2,1)S(1)} %get-tuple-element.50), channel_id=1, source_target_pairs={{0,4},{4,0},{8,12},{12,8},{1,5},{5,1},{9,13},{13,9},{2,6},{6,2},{1... | collective-permute-start | bytes 589832 | tf_op jit(solution)/shard_map/ppermute | solution.py:377
  4.2 2.5 %collective-permute-start.1 = (bf16[16,3072]{1,0:T(8,128)(2,1)}, bf16[16,3072]{1,0:T(8,128)(2,1)S(1)}, u32[]{:S(2)}, u32[]{:S(2)}) collective-permute-start(bf16[16,3072]{1,0:T(8,128)(2,1)} %tokens_ref.1), channel_id=1, source_target_pairs={{0,12},{4,8},{8,4},{12,0},{1,13},{5,9},{9,5},{13,1},{2,14},{6,10},... | collective-permute-start | bytes 294920 | tf_op jit(solution)/shard_map/ppermute | solution.py:377
  6.6 0.1 collective-permute-start
  6.8 1.5 %collective-permute-start.2 = (bf16[16,6144]{1,0:T(8,128)(2,1)S(1)}, bf16[16,6144]{1,0:T(8,128)(2,1)S(1)}, u32[]{:S(2)}, u32[]{:S(2)}) collective-permute-start(bf16[16,6144]{1,0:T(8,128)(2,1)S(1)} %get-tuple-element.43.refs_0_), channel_id=1, source_target_pairs={{0,2},{1,3},{2,0},{3,1},{4,6},{5,7},{6,4},{7,5},{8,10},{9,11},{10,... | collective-permute-start | bytes 589832 | tf_op jit(solution)/shard_map/ppermute | solution.py:377
  8.3 4.6 %shard_map.66.refs_2_.refs_6_.weight_ref = bf16[3072,2048]{1,0:T(8,128)(2,1)S(1)} custom-call(bf16[3072,2048]{1,0:T(8,128)(2,1)} %bitcast.5), custom_call_target="tpu_custom_call" | custom-call | tf_op jit(solution)/shard_map/pallas_call | solution.py:270
  12.9 0.6 %collective-permute-start.6 = (bf16[16,6144]{1,0:T(8,128)(2,1)S(1)}, bf16[16,6144]{1,0:T(8,128)(2,1)S(1)}, u32[]{:S(2)}, u32[]{:S(2)}) collective-permute-start(bf16[16,6144]{1,0:T(8,128)(2,1)S(1)} %collective-permute-done.5.refs_2_.refs_3_), channel_id=1, source_target_pairs={{0,2},{1,3},{2,0},{3,1},{4,6},{5,7},{6,4},{7,5},{8,10},{9,11},{10,... | collective-permute-start | bytes 589832 | tf_op jit(solution)/shard_map/ppermute | solution.py:377
  13.5 1.0 %collective-permute-done.1.refs_1_ = bf16[16,3072]{1,0:T(8,128)(2,1)S(1)} collective-permute-done((bf16[16,3072]{1,0:T(8,128)(2,1)}, bf16[16,3072]{1,0:T(8,128)(2,1)S(1)}, u32[]{:S(2)}, u32[]{:S(2)}) %collective-permute-start.1) | collective-permute-done | bytes 98336 | tf_op jit(solution)/shard_map/ppermute | solution.py:377
  14.5 1.6 %collective-permute-done.refs_0_ = bf16[16,3072]{1,0:T(8,128)(2,1)S(1)} collective-permute-done((bf16[16,3072]{1,0:T(8,128)(2,1)}, bf16[16,3072]{1,0:T(8,128)(2,1)S(1)}, u32[]{:S(2)}, u32[]{:S(2)}) %collective-permute-start) | collective-permute-done | bytes 98336 | tf_op jit(solution)/shard_map/ppermute | solution.py:377
  16.1 0.5 collective-permute-start.7
  16.6 2.0 %collective-permute-start.8 = (bf16[16,3072]{1,0:T(8,128)(2,1)S(1)}, bf16[16,3072]{1,0:T(8,128)(2,1)S(1)}, u32[]{:S(2)}, u32[]{:S(2)}) collective-permute-start(bf16[16,3072]{1,0:T(8,128)(2,1)S(1)} %get-tuple-element.52), channel_id=1, source_target_pairs={{0,12},{4,8},{8,4},{12,0},{1,13},{5,9},{9,5},{13,1},{2,14},{6,10},... | collective-permute-start | bytes 294920 | tf_op jit(solution)/shard_map/ppermute | solution.py:377
  18.6 1.5 %collective-permute-start.3 = (bf16[16,3072]{1,0:T(8,128)(2,1)S(1)}, bf16[16,3072]{1,0:T(8,128)(2,1)S(1)}, u32[]{:S(2)}, u32[]{:S(2)}) collective-permute-start(bf16[16,3072]{1,0:T(8,128)(2,1)S(1)} %get-tuple-element.48.refs_1_), channel_id=1, source_target_pairs={{0,2},{1,3},{2,0},{3,1},{4,6},{5,7},{6,4},{7,5},{8,10},{9,11},{10,... | collective-permute-start | bytes 294920 | tf_op jit(solution)/shard_map/ppermute | solution.py:377
  20.1 0.5 collective-permute-start.4
  20.6 3.6 %collective-permute-done.7.refs_0_ = bf16[16,3072]{1,0:T(8,128)(2,1)S(1)} collective-permute-done((bf16[16,3072]{1,0:T(8,128)(2,1)S(1)}, bf16[16,3072]{1,0:T(8,128)(2,1)S(1)}, u32[]{:S(2)}, u32[]{:S(2)}) %collective-permute-start.7) | collective-permute-done | bytes 98336 | tf_op jit(solution)/shard_map/ppermute | solution.py:377
  24.3 0.5 collective-permute-done.4.refs_6_
  24.7 0.1 shard_map.69.refs_0_
  24.8 0.1 collective-permute-start.10
  24.9 0.6 collective-permute-start.11
  25.5 1.1 %collective-permute-start.9 = (bf16[32,3072]{1,0:T(8,128)(2,1)S(1)}, bf16[32,3072]{1,0:T(8,128)(2,1)S(1)}, u32[]{:S(2)}, u32[]{:S(2)}) collective-permute-start(bf16[32,3072]{1,0:T(8,128)(2,1)S(1)} %shard_map.67.refs_1_), channel_id=1, source_target_pairs={{0,2},{1,3},{2,0},{3,1},{4,6},{5,7},{6,4},{7,5},{8,10},{9,11},{10,... | collective-permute-start | bytes 589832 | tf_op jit(solution)/shard_map/ppermute | solution.py:377
  26.5 0.6 %collective-permute-done.10.refs_1_ = bf16[128,3072]{1,0:T(8,128)(2,1)S(1)} collective-permute-done((bf16[128,3072]{1,0:T(8,128)(2,1)S(1)}, bf16[128,3072]{1,0:T(8,128)(2,1)S(1)}, u32[]{:S(2)}, u32[]{:S(2)}) %collective-permute-start.10) | collective-permute-done | bytes 786464 | tf_op jit(solution)/shard_map/ppermute | solution.py:377
  27.1 4.6 %shard_map.70 = (f32[256,2048]{1,0:T(8,128)S(1)}, bf16[2048,3072]{1,0:T(8,128)(2,1)S(1)}) custom-call(bf16[128,3072]{1,0:T(8,128)(2,1)S(1)} %shard_map.69.refs_0_, bf16[128,3072]{1,0:T(8,128)(2,1)S(1)} %collective-permute-done.10.refs_1_, bf16[3072,2048]{1,0:T(8,128)(2,1)S(1)} %shard_map.66.refs_2_.refs_6_.weight_ref, bf16[2048,3072]{1,0:T(8,128)(2,1)} %bitcast.6), custom_call_target="tpu_custom_call" | custom-call | tf_op jit(solution)/shard_map/pallas_call | solution.py:298
  31.7 0.6 %collective-permute-done.9.refs_1_ = bf16[32,3072]{1,0:T(8,128)(2,1)S(1)} collective-permute-done((bf16[32,3072]{1,0:T(8,128)(2,1)S(1)}, bf16[32,3072]{1,0:T(8,128)(2,1)S(1)}, u32[]{:S(2)}, u32[]{:S(2)}) %collective-permute-start.9) | collective-permute-done | bytes 196640 | tf_op jit(solution)/shard_map/ppermute | solution.py:377
  32.3 0.0 collective-permute-done.11.refs_2_
  32.4 0.1 collective-permute-start.12
  32.5 1.7 %collective-permute-done.12.refs_3_ = bf16[64,3072]{1,0:T(8,128)(2,1)S(1)} collective-permute-done((bf16[64,3072]{1,0:T(8,128)(2,1)S(1)}, bf16[64,3072]{1,0:T(8,128)(2,1)S(1)}, u32[]{:S(2)}, u32[]{:S(2)}) %collective-permute-start.12) | collective-permute-done | bytes 393248 | tf_op jit(solution)/shard_map/ppermute | solution.py:377
  34.2 5.6 %shard_map.72 = (bf16[256,2048]{1,0:T(8,128)(2,1)S(1)}, bf16[128,2048]{1,0:T(8,128)(2,1)S(1)}, bf16[128,2048]{1,0:T(8,128)(2,1)S(1)}) custom-call(bf16[64,3072]{1,0:T(8,128)(2,1)S(1)} %shard_map.68.refs_0_, bf16[64,3072]{1,0:T(8,128)(2,1)S(1)} %shard_map.71.refs_1_, bf16[64,3072]{1,0:T(8,128)(2,1)S(1)} %collective-permute-done.11.refs_2_, ...), custom_call_target="tpu_custom_call" | custom-call | tf_op jit(solution)/shard_map/pallas_call | solution.py:333
  39.8 0.2 collective-permute-start.13
  40.0 1.3 %shard_map.75 = (bf16[128,1024]{1,0:T(8,128)(2,1)S(1)}, bf16[128,1024]{1,0:T(8,128)(2,1)S(1)}) custom-call(bf16[256,2048]{1,0:T(8,128)(2,1)S(1)} %get-tuple-element.72.scaled_ref, bf16[3072,2048]{1,0:T(8,128)(2,1)S(1)} %shard_map.66.refs_2_.refs_6_.weight_ref), custom_call_target="tpu_custom_call" | custom-call | tf_op jit(solution)/shard_map/pallas_call | solution.py:365
  41.3 0.4 collective-permute-start.18
  41.7 0.1 collective-permute-done.13.refs_1_
  41.8 0.1 shard_map.73
  41.9 1.1 %collective-permute-start.14 = (bf16[64,2048]{1,0:T(8,128)(2,1)S(1)}, bf16[64,2048]{1,0:T(8,128)(2,1)S(1)}, u32[]{:S(2)}, u32[]{:S(2)}) collective-permute-start(bf16[64,2048]{1,0:T(8,128)(2,1)S(1)} %get-tuple-element.67), channel_id=1, source_target_pairs={{0,2},{1,3},{2,0},{3,1},{4,6},{5,7},{6,4},{7,5},{8,10},{9,11},{10,... | collective-permute-start | bytes 786440 | tf_op jit(solution)/shard_map/ppermute | solution.py:377
  43.0 0.0 collective-permute-done.18.refs_1_
  43.0 0.1 shard_map.76
  43.1 2.7 %collective-permute-start.19 = (bf16[32,1024]{1,0:T(8,128)(2,1)S(1)}, bf16[32,1024]{1,0:T(8,128)(2,1)S(1)}, u32[]{:S(2)}, u32[]{:S(2)}) collective-permute-start(bf16[32,1024]{1,0:T(8,128)(2,1)S(1)} %get-tuple-element.76), channel_id=1, source_target_pairs={{0,8},{4,12},{8,0},{12,4},{1,9},{5,13},{9,1},{13,5},{2,10},{6,14},... | collective-permute-start | bytes 196616 | tf_op jit(solution)/shard_map/ppermute | solution.py:377
  45.8 1.3 %collective-permute-start.20 = (bf16[32,1024]{1,0:T(8,128)(2,1)S(1)}, bf16[32,1024]{1,0:T(8,128)(2,1)S(1)}, u32[]{:S(2)}, u32[]{:S(2)}) collective-permute-start(bf16[32,1024]{1,0:T(8,128)(2,1)S(1)} %get-tuple-element.77), channel_id=1, source_target_pairs={{0,12},{4,8},{8,4},{12,0},{1,13},{5,9},{9,5},{13,1},{2,14},{6,10},... | collective-permute-start | bytes 196616 | tf_op jit(solution)/shard_map/ppermute | solution.py:377
  47.1 0.0 collective-permute-start.21
  47.1 3.2 %collective-permute-done.14.refs_1_ = bf16[64,2048]{1,0:T(8,128)(2,1)S(1)} collective-permute-done((bf16[64,2048]{1,0:T(8,128)(2,1)S(1)}, bf16[64,2048]{1,0:T(8,128)(2,1)S(1)}, u32[]{:S(2)}, u32[]{:S(2)}) %collective-permute-start.14) | collective-permute-done | bytes 262176 | tf_op jit(solution)/shard_map/ppermute | solution.py:377
  50.3 0.1 shard_map.74
  50.4 2.2 %collective-permute-start.15 = (bf16[16,2048]{1,0:T(8,128)(2,1)S(1)}, bf16[16,2048]{1,0:T(8,128)(2,1)S(1)}, u32[]{:S(2)}, u32[]{:S(2)}) collective-permute-start(bf16[16,2048]{1,0:T(8,128)(2,1)S(1)} %get-tuple-element.69), channel_id=1, source_target_pairs={{0,8},{4,12},{8,0},{12,4},{1,9},{5,13},{9,1},{13,5},{2,10},{6,14},... | collective-permute-start | bytes 196616 | tf_op jit(solution)/shard_map/ppermute | solution.py:377
  52.6 1.3 %collective-permute-start.16 = (bf16[16,2048]{1,0:T(8,128)(2,1)S(1)}, bf16[16,2048]{1,0:T(8,128)(2,1)S(1)}, u32[]{:S(2)}, u32[]{:S(2)}) collective-permute-start(bf16[16,2048]{1,0:T(8,128)(2,1)S(1)} %get-tuple-element.70), channel_id=1, source_target_pairs={{0,12},{4,8},{8,4},{12,0},{1,13},{5,9},{9,5},{13,1},{2,14},{6,10},... | collective-permute-start | bytes 196616 | tf_op jit(solution)/shard_map/ppermute | solution.py:377
  54.0 0.0 collective-permute-done.19.refs_1_
  54.0 0.0 collective-permute-start.17
  54.0 1.6 %collective-permute-start.22 = (bf16[16,1024]{1,0:T(8,128)(2,1)S(1)}, bf16[16,1024]{1,0:T(8,128)(2,1)S(1)}, u32[]{:S(2)}, u32[]{:S(2)}) collective-permute-start(bf16[16,1024]{1,0:T(8,128)(2,1)S(1)} %get-tuple-element.80), channel_id=1, source_target_pairs={{0,2},{1,3},{2,0},{3,1},{4,6},{5,7},{6,4},{7,5},{8,10},{9,11},{10,... | collective-permute-start | bytes 98312 | tf_op jit(solution)/shard_map/ppermute | solution.py:377
  55.6 2.4 %collective-permute-done.22.refs_5_ = bf16[16,1024]{1,0:T(8,128)(2,1)S(1)} collective-permute-done((bf16[16,1024]{1,0:T(8,128)(2,1)S(1)}, bf16[16,1024]{1,0:T(8,128)(2,1)S(1)}, u32[]{:S(2)}, u32[]{:S(2)}) %collective-permute-start.22) | collective-permute-done | bytes 32800 | tf_op jit(solution)/shard_map/ppermute | solution.py:377
  58.0 0.8 %collective-permute-done.16.refs_2_ = bf16[16,2048]{1,0:T(8,128)(2,1)S(1)} collective-permute-done((bf16[16,2048]{1,0:T(8,128)(2,1)S(1)}, bf16[16,2048]{1,0:T(8,128)(2,1)S(1)}, u32[]{:S(2)}, u32[]{:S(2)}) %collective-permute-start.16) | collective-permute-done | bytes 65568 | tf_op jit(solution)/shard_map/ppermute | solution.py:377
  58.8 0.1 collective-permute-done.17.refs_3_
  58.9 0.7 %shard_map.78 = bf16[16,3072]{1,0:T(8,128)(2,1)} custom-call(bf16[16,2048]{1,0:T(8,128)(2,1)S(1)} %get-tuple-element.68.refs_0_, bf16[16,2048]{1,0:T(8,128)(2,1)S(1)} %collective-permute-done.15.refs_1_, bf16[16,2048]{1,0:T(8,128)(2,1)S(1)} %collective-permute-done.16.refs_2_, bf16[16,2048]{1,0:T(8,128)(2,1)S(1)} %collective-permute-done.17.refs_3_, ...), custom_call_target="tpu_custom_call" | custom-call | tf_op jit(solution)/shard_map/pallas_call | solution.py:107
  (13 shorter events, 0.1 us)
Async XLA Ops:
  1.1 11.8 %collective-permute-start.5 = (bf16[16,6144]{1,0:T(8,128)(2,1)S(1)}, bf16[16,6144]{1,0:T(8,128)(2,1)S(1)}, u32[]{:S(2)}, u32[]{:S(2)}) collective-permute-start(bf16[16,6144]{1,0:T(8,128)(2,1)S(1)} %get-tuple-element.50), channel_id=1, source_target_pairs={{0,4},{4,0},{8,12},{12,8},{1,5},{5,1},{9,13},{13,9},{2,6},{6,2},{1... | collective-permute-start | bytes 589832 | tf_op jit(solution)/shard_map/ppermute | solution.py:377
  4.2 10.4 %collective-permute-start.1 = (bf16[16,3072]{1,0:T(8,128)(2,1)}, bf16[16,3072]{1,0:T(8,128)(2,1)S(1)}, u32[]{:S(2)}, u32[]{:S(2)}) collective-permute-start(bf16[16,3072]{1,0:T(8,128)(2,1)} %tokens_ref.1), channel_id=1, source_target_pairs={{0,12},{4,8},{8,4},{12,0},{1,13},{5,9},{9,5},{13,1},{2,14},{6,10},... | collective-permute-start | bytes 294920 | tf_op jit(solution)/shard_map/ppermute | solution.py:377
  6.6 9.4 %collective-permute-start = (bf16[16,3072]{1,0:T(8,128)(2,1)}, bf16[16,3072]{1,0:T(8,128)(2,1)S(1)}, u32[]{:S(2)}, u32[]{:S(2)}) collective-permute-start(bf16[16,3072]{1,0:T(8,128)(2,1)} %tokens_ref.1), channel_id=1, source_target_pairs={{0,8},{4,12},{8,0},{12,4},{1,9},{5,13},{9,1},{13,5},{2,10},{6,14},... | collective-permute-start | bytes 294920 | tf_op jit(solution)/shard_map/ppermute | solution.py:377
  6.8 9.3 %collective-permute-start.2 = (bf16[16,6144]{1,0:T(8,128)(2,1)S(1)}, bf16[16,6144]{1,0:T(8,128)(2,1)S(1)}, u32[]{:S(2)}, u32[]{:S(2)}) collective-permute-start(bf16[16,6144]{1,0:T(8,128)(2,1)S(1)} %get-tuple-element.43.refs_0_), channel_id=1, source_target_pairs={{0,2},{1,3},{2,0},{3,1},{4,6},{5,7},{6,4},{7,5},{8,10},{9,11},{10,... | collective-permute-start | bytes 589832 | tf_op jit(solution)/shard_map/ppermute | solution.py:377
  12.9 11.8 %collective-permute-start.6 = (bf16[16,6144]{1,0:T(8,128)(2,1)S(1)}, bf16[16,6144]{1,0:T(8,128)(2,1)S(1)}, u32[]{:S(2)}, u32[]{:S(2)}) collective-permute-start(bf16[16,6144]{1,0:T(8,128)(2,1)S(1)} %collective-permute-done.5.refs_2_.refs_3_), channel_id=1, source_target_pairs={{0,2},{1,3},{2,0},{3,1},{4,6},{5,7},{6,4},{7,5},{8,10},{9,11},{10,... | collective-permute-start | bytes 589832 | tf_op jit(solution)/shard_map/ppermute | solution.py:377
  16.1 8.1 %collective-permute-start.7 = (bf16[16,3072]{1,0:T(8,128)(2,1)S(1)}, bf16[16,3072]{1,0:T(8,128)(2,1)S(1)}, u32[]{:S(2)}, u32[]{:S(2)}) collective-permute-start(bf16[16,3072]{1,0:T(8,128)(2,1)S(1)} %get-tuple-element.51), channel_id=1, source_target_pairs={{0,8},{4,12},{8,0},{12,4},{1,9},{5,13},{9,1},{13,5},{2,10},{6,14},... | collective-permute-start | bytes 294920 | tf_op jit(solution)/shard_map/ppermute | solution.py:377
  16.6 7.6 %collective-permute-start.8 = (bf16[16,3072]{1,0:T(8,128)(2,1)S(1)}, bf16[16,3072]{1,0:T(8,128)(2,1)S(1)}, u32[]{:S(2)}, u32[]{:S(2)}) collective-permute-start(bf16[16,3072]{1,0:T(8,128)(2,1)S(1)} %get-tuple-element.52), channel_id=1, source_target_pairs={{0,12},{4,8},{8,4},{12,0},{1,13},{5,9},{9,5},{13,1},{2,14},{6,10},... | collective-permute-start | bytes 294920 | tf_op jit(solution)/shard_map/ppermute | solution.py:377
  18.6 5.6 %collective-permute-start.3 = (bf16[16,3072]{1,0:T(8,128)(2,1)S(1)}, bf16[16,3072]{1,0:T(8,128)(2,1)S(1)}, u32[]{:S(2)}, u32[]{:S(2)}) collective-permute-start(bf16[16,3072]{1,0:T(8,128)(2,1)S(1)} %get-tuple-element.48.refs_1_), channel_id=1, source_target_pairs={{0,2},{1,3},{2,0},{3,1},{4,6},{5,7},{6,4},{7,5},{8,10},{9,11},{10,... | collective-permute-start | bytes 294920 | tf_op jit(solution)/shard_map/ppermute | solution.py:377
  20.1 4.6 %collective-permute-start.4 = (bf16[16,3072]{1,0:T(8,128)(2,1)S(1)}, bf16[16,3072]{1,0:T(8,128)(2,1)S(1)}, u32[]{:S(2)}, u32[]{:S(2)}) collective-permute-start(bf16[16,3072]{1,0:T(8,128)(2,1)S(1)} %get-tuple-element.49.refs_2_), channel_id=1, source_target_pairs={{0,2},{1,3},{2,0},{3,1},{4,6},{5,7},{6,4},{7,5},{8,10},{9,11},{10,... | collective-permute-start | bytes 294920 | tf_op jit(solution)/shard_map/ppermute | solution.py:377
  24.8 2.4 %collective-permute-start.10 = (bf16[128,3072]{1,0:T(8,128)(2,1)S(1)}, bf16[128,3072]{1,0:T(8,128)(2,1)S(1)}, u32[]{:S(2)}, u32[]{:S(2)}) collective-permute-start(bf16[128,3072]{1,0:T(8,128)(2,1)S(1)} %shard_map.69.refs_0_), channel_id=1, source_target_pairs={{0,1},{1,0},{2,3},{3,2},{4,5},{5,4},{6,7},{7,6},{8,9},{9,8},{10,11... | collective-permute-start | bytes 2359304 | tf_op jit(solution)/shard_map/ppermute | solution.py:377
  24.9 7.4 %collective-permute-start.11 = (bf16[64,3072]{1,0:T(8,128)(2,1)S(1)}, bf16[64,3072]{1,0:T(8,128)(2,1)S(1)}, u32[]{:S(2)}, u32[]{:S(2)}) collective-permute-start(bf16[64,3072]{1,0:T(8,128)(2,1)S(1)} %shard_map.68.refs_0_), channel_id=1, source_target_pairs={{0,1},{1,0},{2,3},{3,2},{4,5},{5,4},{6,7},{7,6},{8,9},{9,8},{10,11... | collective-permute-start | bytes 1179656 | tf_op jit(solution)/shard_map/ppermute | solution.py:377
  25.5 6.9 %collective-permute-start.9 = (bf16[32,3072]{1,0:T(8,128)(2,1)S(1)}, bf16[32,3072]{1,0:T(8,128)(2,1)S(1)}, u32[]{:S(2)}, u32[]{:S(2)}) collective-permute-start(bf16[32,3072]{1,0:T(8,128)(2,1)S(1)} %shard_map.67.refs_1_), channel_id=1, source_target_pairs={{0,2},{1,3},{2,0},{3,1},{4,6},{5,7},{6,4},{7,5},{8,10},{9,11},{10,... | collective-permute-start | bytes 589832 | tf_op jit(solution)/shard_map/ppermute | solution.py:377
  32.4 1.8 %collective-permute-start.12 = (bf16[64,3072]{1,0:T(8,128)(2,1)S(1)}, bf16[64,3072]{1,0:T(8,128)(2,1)S(1)}, u32[]{:S(2)}, u32[]{:S(2)}) collective-permute-start(bf16[64,3072]{1,0:T(8,128)(2,1)S(1)} %shard_map.71.refs_1_), channel_id=1, source_target_pairs={{0,1},{1,0},{2,3},{3,2},{4,5},{5,4},{6,7},{7,6},{8,9},{9,8},{10,11... | collective-permute-start | bytes 1179656 | tf_op jit(solution)/shard_map/ppermute | solution.py:377
  39.8 2.0 %collective-permute-start.13 = (bf16[128,2048]{1,0:T(8,128)(2,1)S(1)}, bf16[128,2048]{1,0:T(8,128)(2,1)S(1)}, u32[]{:S(2)}, u32[]{:S(2)}) collective-permute-start(bf16[128,2048]{1,0:T(8,128)(2,1)S(1)} %get-tuple-element.65), channel_id=1, source_target_pairs={{0,1},{1,0},{2,3},{3,2},{4,5},{5,4},{6,7},{7,6},{8,9},{9,8},{10,11... | collective-permute-start | bytes 1572872 | tf_op jit(solution)/shard_map/ppermute | solution.py:377
  41.3 1.7 %collective-permute-start.18 = (bf16[128,1024]{1,0:T(8,128)(2,1)S(1)}, bf16[128,1024]{1,0:T(8,128)(2,1)S(1)}, u32[]{:S(2)}, u32[]{:S(2)}) collective-permute-start(bf16[128,1024]{1,0:T(8,128)(2,1)S(1)} %get-tuple-element.74), channel_id=1, source_target_pairs={{0,1},{1,0},{2,3},{3,2},{4,5},{5,4},{6,7},{7,6},{8,9},{9,8},{10,11... | collective-permute-start | bytes 786440 | tf_op jit(solution)/shard_map/ppermute | solution.py:377
  41.9 8.4 %collective-permute-start.14 = (bf16[64,2048]{1,0:T(8,128)(2,1)S(1)}, bf16[64,2048]{1,0:T(8,128)(2,1)S(1)}, u32[]{:S(2)}, u32[]{:S(2)}) collective-permute-start(bf16[64,2048]{1,0:T(8,128)(2,1)S(1)} %get-tuple-element.67), channel_id=1, source_target_pairs={{0,2},{1,3},{2,0},{3,1},{4,6},{5,7},{6,4},{7,5},{8,10},{9,11},{10,... | collective-permute-start | bytes 786440 | tf_op jit(solution)/shard_map/ppermute | solution.py:377
  43.1 10.9 %collective-permute-start.19 = (bf16[32,1024]{1,0:T(8,128)(2,1)S(1)}, bf16[32,1024]{1,0:T(8,128)(2,1)S(1)}, u32[]{:S(2)}, u32[]{:S(2)}) collective-permute-start(bf16[32,1024]{1,0:T(8,128)(2,1)S(1)} %get-tuple-element.76), channel_id=1, source_target_pairs={{0,8},{4,12},{8,0},{12,4},{1,9},{5,13},{9,1},{13,5},{2,10},{6,14},... | collective-permute-start | bytes 196616 | tf_op jit(solution)/shard_map/ppermute | solution.py:377
  45.8 8.2 %collective-permute-start.20 = (bf16[32,1024]{1,0:T(8,128)(2,1)S(1)}, bf16[32,1024]{1,0:T(8,128)(2,1)S(1)}, u32[]{:S(2)}, u32[]{:S(2)}) collective-permute-start(bf16[32,1024]{1,0:T(8,128)(2,1)S(1)} %get-tuple-element.77), channel_id=1, source_target_pairs={{0,12},{4,8},{8,4},{12,0},{1,13},{5,9},{9,5},{13,1},{2,14},{6,10},... | collective-permute-start | bytes 196616 | tf_op jit(solution)/shard_map/ppermute | solution.py:377
  47.1 6.9 %collective-permute-start.21 = (bf16[32,1024]{1,0:T(8,128)(2,1)S(1)}, bf16[32,1024]{1,0:T(8,128)(2,1)S(1)}, u32[]{:S(2)}, u32[]{:S(2)}) collective-permute-start(bf16[32,1024]{1,0:T(8,128)(2,1)S(1)} %get-tuple-element.78), channel_id=1, source_target_pairs={{0,4},{4,0},{8,12},{12,8},{1,5},{5,1},{9,13},{13,9},{2,6},{6,2},{1... | collective-permute-start | bytes 196616 | tf_op jit(solution)/shard_map/ppermute | solution.py:377
  50.4 7.6 %collective-permute-start.15 = (bf16[16,2048]{1,0:T(8,128)(2,1)S(1)}, bf16[16,2048]{1,0:T(8,128)(2,1)S(1)}, u32[]{:S(2)}, u32[]{:S(2)}) collective-permute-start(bf16[16,2048]{1,0:T(8,128)(2,1)S(1)} %get-tuple-element.69), channel_id=1, source_target_pairs={{0,8},{4,12},{8,0},{12,4},{1,9},{5,13},{9,1},{13,5},{2,10},{6,14},... | collective-permute-start | bytes 196616 | tf_op jit(solution)/shard_map/ppermute | solution.py:377
  52.6 6.2 %collective-permute-start.16 = (bf16[16,2048]{1,0:T(8,128)(2,1)S(1)}, bf16[16,2048]{1,0:T(8,128)(2,1)S(1)}, u32[]{:S(2)}, u32[]{:S(2)}) collective-permute-start(bf16[16,2048]{1,0:T(8,128)(2,1)S(1)} %get-tuple-element.70), channel_id=1, source_target_pairs={{0,12},{4,8},{8,4},{12,0},{1,13},{5,9},{9,5},{13,1},{2,14},{6,10},... | collective-permute-start | bytes 196616 | tf_op jit(solution)/shard_map/ppermute | solution.py:377
  54.0 5.0 %collective-permute-start.17 = (bf16[16,2048]{1,0:T(8,128)(2,1)S(1)}, bf16[16,2048]{1,0:T(8,128)(2,1)S(1)}, u32[]{:S(2)}, u32[]{:S(2)}) collective-permute-start(bf16[16,2048]{1,0:T(8,128)(2,1)S(1)} %get-tuple-element.71), channel_id=1, source_target_pairs={{0,4},{4,0},{8,12},{12,8},{1,5},{5,1},{9,13},{13,9},{2,6},{6,2},{1... | collective-permute-start | bytes 196616 | tf_op jit(solution)/shard_map/ppermute | solution.py:377
  54.0 4.0 %collective-permute-start.22 = (bf16[16,1024]{1,0:T(8,128)(2,1)S(1)}, bf16[16,1024]{1,0:T(8,128)(2,1)S(1)}, u32[]{:S(2)}, u32[]{:S(2)}) collective-permute-start(bf16[16,1024]{1,0:T(8,128)(2,1)S(1)} %get-tuple-element.80), channel_id=1, source_target_pairs={{0,2},{1,3},{2,0},{3,1},{4,6},{5,7},{6,4},{7,5},{8,10},{9,11},{10,... | collective-permute-start | bytes 98312 | tf_op jit(solution)/shard_map/ppermute | solution.py:377
